TPU v7x, 32 devices: a whole 2x2x4 slice. The times are simulated.
32 devices in a mesh: energy: 16 (over z, x, core), slab: 2 (over y).
Axes of the slice: x: 2, y: 2, z: 4, core: 2. Of those that a mesh axis runs over, the one named last changes fastest.
Arguments:
- energies: float32 [16], P('energy'), may hold values from 0.6 to 1.2
- hamiltonian: float32 [2, 256, 256], P('slab')
- coupling: float32 [2, 64, 64], P('slab'), may hold values from -1.04 to 1.04
- green_prev: float32 [16, 2, 2, 256, 256], P('energy', 'slab'), may hold values from -0.5 to 0.5
- profile: float32 [256, 256], replicated, may hold values from 0.2 to 1
- phonon_weights: float32 [8], replicated, may hold values from 0.02 to 0.1
- source: int32 [16, 2], P('energy'), may hold values from 0 to 15, as said below
- weight_index: int32 [16, 2], P('energy'), may hold values from 0 to 7
- left_face: int32 [2, 64], P('slab'), may hold values from 0 to 255, as said below
- right_face: int32 [2, 64], P('slab'), may hold values from 0 to 255, as said below
Outputs:
- green: float32 [16, 2, 2, 256, 256], P('energy', 'slab')
Inputs may be any that keep to these rules, and one draw needn't show every extreme that they name: source[j, 0] = min(j + d, 15) and source[j, 1] = max(j - d', 0) with d, d' in 1 .. 5; in each column some energy has its partner exactly 5 points away. `left_face`: each row holds 64 distinct orbitals. right_face[s] holds the same 64 orbitals as left_face[s], in an order of its own.
All inputs are finite; a program needn't handle non-finite values.
Results may differ from a plain program's by a relative error of at most 0.00011.
Values sent between devices are 32-bit elements; how exact they have to be, the bound alone decides.
No kernel may reach another device: no remote copies, remote signals or barrier semaphores. Data moves between devices by JAX's collectives and lax.ppermute only.
A program may use at most 64 MiB of HBM per device.

v0:
```python
import jax
import jax.numpy as jnp
from jax import lax
from jax.sharding import PartitionSpec as P

SPAN = 5
NEWTON = 5


BROAD = 0.02
highest = lax.Precision.HIGHEST


def passed_along(value, axis, steps):
    count = lax.axis_size(axis)
    initial, last = (max(0, -steps), min(count, count - steps))
    return lax.ppermute(value, axis, [(source, source + steps) for source in range(initial, last)])


def product(left, right):
    return jnp.matmul(left, right, precision=highest)


def complex_product(a_real, a_imag, b_real, b_imag):
    return (
        product(a_real, b_real) - product(a_imag, b_imag),
        product(a_real, b_imag) + product(a_imag, b_real),
    )


def invert(a_real, a_imag):
    width = a_real.shape[-1]
    unit = jnp.eye(width, dtype=a_real.dtype)
    modulus = jnp.sqrt(a_real * a_real + a_imag * a_imag)
    col_norm = jnp.max(jnp.sum(modulus, axis=-2), axis=-1)
    row_norm = jnp.max(jnp.sum(modulus, axis=-1), axis=-1)
    scale = (1.0 / (col_norm * row_norm))[..., None, None]
    x_real = scale * jnp.swapaxes(a_real, -1, -2)
    x_imag = -scale * jnp.swapaxes(a_imag, -1, -2)
    for turn in range(NEWTON):
        p_real, p_imag = complex_product(a_real, a_imag, x_real, x_imag)
        x_real, x_imag = complex_product(x_real, x_imag, 2.0 * unit - p_real, -p_imag)
    return (x_real, x_imag)


def corner(block, hot):
    return product(product(hot, block), hot.T)


def place(block, hot):
    return product(product(hot.T, block), hot)


def forward_step(incoming, a_real, a_imag, coup, left_hot, right_hot, first):
    faces = coup.shape[0]
    in_real = incoming[..., :faces]
    in_imag = incoming[..., faces:]
    lead = -0.5 * product(coup.T, coup)
    inner_real = product(product(coup.T, in_real), coup)
    inner_imag = product(product(coup.T, in_imag), coup)
    b_real = jnp.where(first, 0.0, inner_real)
    b_imag = jnp.where(first, lead, inner_imag)
    g_real, g_imag = invert(a_real - place(b_real, left_hot), a_imag - place(b_imag, left_hot))
    outgoing = jnp.concatenate([corner(g_real, right_hot), corner(g_imag, right_hot)], axis=-1)
    return (g_real, g_imag, outgoing)


def backward_step(incoming, g_real, g_imag, coup, left_hot, right_hot):
    faces = coup.shape[0]
    m_real = incoming[..., :faces]
    m_imag = incoming[..., faces:]
    col_real = product(g_real, right_hot.T)
    col_imag = product(g_imag, right_hot.T)
    row_real = product(right_hot, g_real)
    row_imag = product(right_hot, g_imag)
    t_real, t_imag = complex_product(col_real, col_imag, m_real, m_imag)
    c_real, c_imag = complex_product(t_real, t_imag, row_real, row_imag)
    big_real = g_real + c_real
    big_imag = g_imag + c_imag
    out_real = product(product(coup, corner(big_real, left_hot)), coup.T)
    out_imag = product(product(coup, corner(big_imag, left_hot)), coup.T)
    return (big_real, big_imag, jnp.concatenate([out_real, out_imag], axis=-1))


def on_device(
    energies,
    hamiltonian,
    coupling,
    green_prev,
    profile,
    phonon_weights,
    source,
    weight_index,
    left_face,
    right_face,
):
    count_dev = energies.shape[0]
    width = hamiltonian.shape[1]
    faces = coupling.shape[1]
    base = lax.axis_index("energy") * count_dev
    reach = (SPAN + count_dev - 1) // count_dev
    table_size = phonon_weights.shape[0]
    chosen = jnp.sum(
        phonon_weights[None, None, :]
        * (weight_index[:, :, None] == jnp.arange(table_size, dtype=jnp.int32)[None, None, :]),
        axis=2,
    )

    def add_piece(total, piece, start):
        rows = piece.shape[0]
        position = start + jnp.arange(rows, dtype=jnp.int32)
        coef = jnp.sum(chosen[:, :, None] * (source[:, :, None] == position[None, None, :]), axis=1)
        return total + product(coef, piece.reshape(rows, -1))

    summed = add_piece(jnp.zeros((count_dev, 2 * width * width), jnp.float32), green_prev, base)
    for offset in range(1, reach + 1):
        rows = count_dev
        upper = passed_along(green_prev, "energy", -offset)
        lower = passed_along(green_prev, "energy", offset)
        summed = add_piece(summed, upper, base + offset * count_dev)
        summed = add_piece(summed, lower, base - offset * count_dev + count_dev - rows)
    sigma = summed.reshape(count_dev, 2, width, width) * profile
    unit = jnp.eye(width, dtype=jnp.float32)
    a_real = energies[:, None, None] * unit - hamiltonian[0] - sigma[:, 0]
    a_imag = BROAD * unit - sigma[:, 1]
    coup = coupling[0]
    orbitals = jnp.arange(width, dtype=jnp.int32)
    left_hot = (left_face[0][:, None] == orbitals[None, :]).astype(jnp.float32)
    right_hot = (right_face[0][:, None] == orbitals[None, :]).astype(jnp.float32)
    slab_index = lax.axis_index("slab")
    slab_count = lax.axis_size("slab")
    first = slab_index == 0
    blocks = jnp.zeros((count_dev, width, width), jnp.float32)
    face_zero = jnp.zeros((faces, 2 * faces), jnp.float32)
    turns = slab_count + count_dev - 1

    def forward_turn(section, carry):
        g_real, g_imag, sent = carry
        incoming = passed_along(sent, "slab", 1)
        which = section - slab_index

        def forward_work(operand):
            pick = jnp.clip(which, 0, count_dev - 1)
            one_real = lax.dynamic_index_in_dim(a_real, pick, 0, keepdims=False)
            one_imag = lax.dynamic_index_in_dim(a_imag, pick, 0, keepdims=False)
            new_real, new_imag, outgoing = forward_step(
                operand, one_real, one_imag, coup, left_hot, right_hot, first
            )
            return (
                lax.dynamic_update_index_in_dim(g_real, new_real, pick, 0),
                lax.dynamic_update_index_in_dim(g_imag, new_imag, pick, 0),
                outgoing,
            )

        def forward_keep(operand):
            return (g_real, g_imag, sent)

        return lax.cond((which >= 0) & (which < count_dev), forward_work, forward_keep, incoming)

    g_real, g_imag, sent = lax.fori_loop(0, turns, forward_turn, (blocks, blocks, face_zero))

    def backward_turn(section, carry):
        big_real, big_imag, sent = carry
        incoming = passed_along(sent, "slab", -1)
        which = section - (slab_count - 1 - slab_index)

        def backward_work(operand):
            pick = jnp.clip(which, 0, count_dev - 1)
            one_real = lax.dynamic_index_in_dim(g_real, pick, 0, keepdims=False)
            one_imag = lax.dynamic_index_in_dim(g_imag, pick, 0, keepdims=False)
            new_real, new_imag, outgoing = backward_step(
                operand, one_real, one_imag, coup, left_hot, right_hot
            )
            return (
                lax.dynamic_update_index_in_dim(big_real, new_real, pick, 0),
                lax.dynamic_update_index_in_dim(big_imag, new_imag, pick, 0),
                outgoing,
            )

        def backward_keep(operand):
            return (big_real, big_imag, sent)

        return lax.cond((which >= 0) & (which < count_dev), backward_work, backward_keep, incoming)

    big_real, big_imag, sent = lax.fori_loop(0, turns, backward_turn, (blocks, blocks, face_zero))
    return jnp.stack([big_real, big_imag], axis=1)[:, None]


def solution(mesh):
    in_specs = (
        P("energy"),
        P("slab", None, None),
        P("slab", None, None),
        P("energy", "slab", None, None, None),
        P(),
        P(),
        P("energy", None),
        P("energy", None),
        P("slab", None),
        P("slab", None),
    )
    out_specs = P("energy", "slab", None, None, None)
    return jax.shard_map(
        on_device, mesh=mesh, in_specs=in_specs, out_specs=out_specs, check_vma=False
    )
```

profile of v0, /device:TPU:16, one launch (start us, length us, event | category | flops | bytes accessed | tf_op | source)
XLA Modules:
  0.0 179.0 jit_solution(4497816313121547179)
XLA Ops:
  0.0 2.6 %collective-permute-start.10 = (f32[1,1,2,256,256]{4,3,2,1,0:T(8,128)}, f32[1,1,2,256,256]{4,3,2,1,0:T(8,128)S(1)}, u32[]{:S(2)}, u32[]{:S(2)}) collective-permute-start(f32[1,1,2,256,256]{4,3,2,1,0:T(8,128)} %param.21), channel_id=1, source_target_pairs={{10,0},{12,2},{14,4},{16,6},{18,8},{20,10},{22,12},{24,14},{26,16}... | collective-permute-start | bytes 1572872 | tf_op jit(solution)/shard_map/ppermute | solution.py:17
  2.6 3.0 %collective-permute-start.11 = (f32[1,1,2,256,256]{4,3,2,1,0:T(8,128)}, f32[1,1,2,256,256]{4,3,2,1,0:T(8,128)S(1)}, u32[]{:S(2)}, u32[]{:S(2)}) collective-permute-start(f32[1,1,2,256,256]{4,3,2,1,0:T(8,128)} %param.21), channel_id=1, source_target_pairs={{0,10},{2,12},{4,14},{6,16},{8,18},{10,20},{12,22},{14,24},{16,26}... | collective-permute-start | bytes 1572872 | tf_op jit(solution)/shard_map/ppermute | solution.py:17
  5.6 4.5 %collective-permute-start.2 = (f32[1,1,2,256,256]{4,3,2,1,0:T(8,128)}, f32[1,1,2,256,256]{4,3,2,1,0:T(8,128)S(1)}, u32[]{:S(2)}, u32[]{:S(2)}) collective-permute-start(f32[1,1,2,256,256]{4,3,2,1,0:T(8,128)} %param.21), channel_id=1, source_target_pairs={{2,0},{4,2},{6,4},{8,6},{10,8},{12,10},{14,12},{16,14},{18,16},{20... | collective-permute-start | bytes 1572872 | tf_op jit(solution)/shard_map/ppermute | solution.py:17
  10.1 1.9 %collective-permute-start.3 = (f32[1,1,2,256,256]{4,3,2,1,0:T(8,128)}, f32[1,1,2,256,256]{4,3,2,1,0:T(8,128)S(1)}, u32[]{:S(2)}, u32[]{:S(2)}) collective-permute-start(f32[1,1,2,256,256]{4,3,2,1,0:T(8,128)} %param.21), channel_id=1, source_target_pairs={{0,2},{2,4},{4,6},{6,8},{8,10},{10,12},{12,14},{14,16},{16,18},{18... | collective-permute-start | bytes 1572872 | tf_op jit(solution)/shard_map/ppermute | solution.py:17
  12.1 2.3 %collective-permute-start.4 = (f32[1,1,2,256,256]{4,3,2,1,0:T(8,128)}, f32[1,1,2,256,256]{4,3,2,1,0:T(8,128)S(1)}, u32[]{:S(2)}, u32[]{:S(2)}) collective-permute-start(f32[1,1,2,256,256]{4,3,2,1,0:T(8,128)} %param.21), channel_id=1, source_target_pairs={{4,0},{6,2},{8,4},{10,6},{12,8},{14,10},{16,12},{18,14},{20,16},{2... | collective-permute-start | bytes 1572872 | tf_op jit(solution)/shard_map/ppermute | solution.py:17
  14.4 6.4 %collective-permute-done.10 = f32[1,1,2,256,256]{4,3,2,1,0:T(8,128)S(1)} collective-permute-done((f32[1,1,2,256,256]{4,3,2,1,0:T(8,128)}, f32[1,1,2,256,256]{4,3,2,1,0:T(8,128)S(1)}, u32[]{:S(2)}, u32[]{:S(2)}) %collective-permute-start.10) | collective-permute-done | bytes 524320 | tf_op jit(solution)/shard_map/ppermute | solution.py:17
  20.8 1.9 %collective-permute-start.5 = (f32[1,1,2,256,256]{4,3,2,1,0:T(8,128)}, f32[1,1,2,256,256]{4,3,2,1,0:T(8,128)S(1)}, u32[]{:S(2)}, u32[]{:S(2)}) collective-permute-start(f32[1,1,2,256,256]{4,3,2,1,0:T(8,128)} %param.21), channel_id=1, source_target_pairs={{0,4},{2,6},{4,8},{6,10},{8,12},{10,14},{12,16},{14,18},{16,20},{1... | collective-permute-start | bytes 1572872 | tf_op jit(solution)/shard_map/ppermute | solution.py:17
  22.7 1.9 %collective-permute-start.6 = (f32[1,1,2,256,256]{4,3,2,1,0:T(8,128)}, f32[1,1,2,256,256]{4,3,2,1,0:T(8,128)}, u32[]{:S(2)}, u32[]{:S(2)}) collective-permute-start(f32[1,1,2,256,256]{4,3,2,1,0:T(8,128)} %param.21), channel_id=1, source_target_pairs={{6,0},{8,2},{10,4},{12,6},{14,8},{16,10},{18,12},{20,14},{22,16},{... | collective-permute-start | bytes 1572872 | tf_op jit(solution)/shard_map/ppermute | solution.py:17
  24.7 7.4 %collective-permute-done.2 = f32[1,1,2,256,256]{4,3,2,1,0:T(8,128)S(1)} collective-permute-done((f32[1,1,2,256,256]{4,3,2,1,0:T(8,128)}, f32[1,1,2,256,256]{4,3,2,1,0:T(8,128)S(1)}, u32[]{:S(2)}, u32[]{:S(2)}) %collective-permute-start.2) | collective-permute-done | bytes 524320 | tf_op jit(solution)/shard_map/ppermute | solution.py:17
  32.1 1.9 %collective-permute-start.7 = (f32[1,1,2,256,256]{4,3,2,1,0:T(8,128)}, f32[1,1,2,256,256]{4,3,2,1,0:T(8,128)}, u32[]{:S(2)}, u32[]{:S(2)}) collective-permute-start(f32[1,1,2,256,256]{4,3,2,1,0:T(8,128)} %param.21), channel_id=1, source_target_pairs={{0,6},{2,8},{4,10},{6,12},{8,14},{10,16},{12,18},{14,20},{16,22},{... | collective-permute-start | bytes 1572872 | tf_op jit(solution)/shard_map/ppermute | solution.py:17
  35.1 4.5 %collective-permute-start.8 = (f32[1,1,2,256,256]{4,3,2,1,0:T(8,128)}, f32[1,1,2,256,256]{4,3,2,1,0:T(8,128)}, u32[]{:S(2)}, u32[]{:S(2)}) collective-permute-start(f32[1,1,2,256,256]{4,3,2,1,0:T(8,128)} %param.21), channel_id=1, source_target_pairs={{8,0},{10,2},{12,4},{14,6},{16,8},{18,10},{20,12},{22,14},{24,16},... | collective-permute-start | bytes 1572872 | tf_op jit(solution)/shard_map/ppermute | solution.py:17
  39.6 23.4 %collective-permute-done.4 = f32[1,1,2,256,256]{4,3,2,1,0:T(8,128)S(1)} collective-permute-done((f32[1,1,2,256,256]{4,3,2,1,0:T(8,128)}, f32[1,1,2,256,256]{4,3,2,1,0:T(8,128)S(1)}, u32[]{:S(2)}, u32[]{:S(2)}) %collective-permute-start.4) | collective-permute-done | bytes 524320 | tf_op jit(solution)/shard_map/ppermute | solution.py:17
  63.0 1.9 %collective-permute-start.9 = (f32[1,1,2,256,256]{4,3,2,1,0:T(8,128)}, f32[1,1,2,256,256]{4,3,2,1,0:T(8,128)}, u32[]{:S(2)}, u32[]{:S(2)}) collective-permute-start(f32[1,1,2,256,256]{4,3,2,1,0:T(8,128)} %param.21), channel_id=1, source_target_pairs={{0,8},{2,10},{4,12},{6,14},{8,16},{10,18},{12,20},{14,22},{16,24},... | collective-permute-start | bytes 1572872 | tf_op jit(solution)/shard_map/ppermute | solution.py:17
  67.6 6.8 %collective-permute-done.9 = f32[1,1,2,256,256]{4,3,2,1,0:T(8,128)} collective-permute-done((f32[1,1,2,256,256]{4,3,2,1,0:T(8,128)}, f32[1,1,2,256,256]{4,3,2,1,0:T(8,128)}, u32[]{:S(2)}, u32[]{:S(2)}) %collective-permute-start.9) | collective-permute-done | bytes 524320 | tf_op jit(solution)/shard_map/ppermute | solution.py:17
  74.4 9.1 %bitcast_multiply_fusion = f32[1,2,256,256]{3,2,1,0:T(8,128)S(1)} fusion(f32[1,1,2,256,256]{4,3,2,1,0:T(8,128)S(1)} %collective-permute-done.11, f32[1,1,2,256,256]{4,3,2,1,0:T(8,128)S(1)} %collective-permute-done.10, f32[1,1,2,256,256]{4,3,2,1,0:T(8,128)} %collective-permute-done.9, f32[1,1,2,256,256]{4,3,2,1,0:T(8,128)} %collective-permute-done.8, ...), kind=kLoop, calls=%fused_computation.98 | loop fusion | flops 2883584 | bytes 6553644 | tf_op jit(solution)/shard_map/mul | solution.py:122
  85.1 33.8 %while.38 = (s32[]{:T(128)}, f32[1,256,256]{2,1,0:T(8,128)}, f32[1,256,256]{2,1,0:T(8,128)S(1)}, f32[64,128]{1,0:T(8,128)S(1)}, s32[]{:T(128)}, /*index=5*/f32[1...) while((s32[]{:T(128)}, f32[1,256,256]{2,1,0:T(8,128)}, ...), condition=%wide.region_19.20_spmd.clone, body=%wide.region_12.19_spmd.clone.sunk | while | flops 8324141056 | bytes 41833408 | solution.py:160
  85.1 3.4 %collective-permute-start = (f32[64,128]{1,0:T(8,128)S(1)}, f32[64,128]{1,0:T(8,128)S(1)}, u32[]{:S(2)}, u32[]{:S(2)}) collective-permute-start(f32[64,128]{1,0:T(8,128)S(1)} %get-tuple-element.831), channel_id=1, source_target_pairs={{0,1},{2,3},{4,5},{6,7},{8,9},{10,11},{12,13},{14,15},{16,17},{18,... | collective-permute-start | bytes 98312 | tf_op jit(solution)/shard_map/while/body/eval_jaxpr/ppermute | solution.py:17
  90.1 25.9 %conditional.6 = ((f32[1,256,256]{2,1,0:T(8,128)}, f32[1,256,256]{2,1,0:T(8,128)S(1)}, f32[64,128]{1,0:T(8,128)S(1)})) conditional(s32[]{:T(128)} %convert_element_type.66, (f32[1,256,256]{2,1,0:T(8,128)}, f32[1,256,256]{2,1,0:T(8,128)S(1)}, f32[64,128]{1,0:T(8,128)S(1)}) %tuple.108, (f32[1,256,256]{2,1,0:T(8,128)S(1)}, pred[]{:T(512)}, ...), branch_computations={%region_13.0_spmd, %region_14.18_spmd} | conditional | flops 8324075520 | bytes 41570472 | solution.py:158
  119.6 57.6 %while.39 = (s32[]{:T(128)}, f32[1,256,256]{2,1,0:T(8,128)}, f32[1,256,256]{2,1,0:T(8,128)S(1)}, f32[64,128]{1,0:T(8,128)S(1)}, s32[]{:T(128)}, /*index=5*/f32[1...) while((s32[]{:T(128)}, f32[1,256,256]{2,1,0:T(8,128)}, ...), condition=%wide.region_23.24_spmd.clone, body=%wide.region_20.23_spmd.clone.sunk | while | flops 591765504 | bytes 8684387 | solution.py:185
  121.1 30.0 %collective-permute-done.1 = f32[64,128]{1,0:T(8,128)S(1)} collective-permute-done((f32[64,128]{1,0:T(8,128)S(1)}, f32[64,128]{1,0:T(8,128)S(1)}, u32[]{:S(2)}, u32[]{:S(2)}) %collective-permute-start.1) | collective-permute-done | bytes 32800 | tf_op jit(solution)/shard_map/while/body/eval_jaxpr/ppermute | solution.py:17
  152.4 13.2 %collective-permute-done.1 = f32[64,128]{1,0:T(8,128)S(1)} collective-permute-done((f32[64,128]{1,0:T(8,128)S(1)}, f32[64,128]{1,0:T(8,128)S(1)}, u32[]{:S(2)}, u32[]{:S(2)}) %collective-permute-start.1) | collective-permute-done | bytes 32800 | tf_op jit(solution)/shard_map/while/body/eval_jaxpr/ppermute | solution.py:17
  165.6 11.7 %conditional.7 = ((f32[1,256,256]{2,1,0:T(8,128)}, f32[1,256,256]{2,1,0:T(8,128)S(1)}, f32[64,128]{1,0:T(8,128)S(1)})) conditional(s32[]{:T(128)} %convert_element_type.68, (f32[1,256,256]{2,1,0:T(8,128)}, f32[1,256,256]{2,1,0:T(8,128)S(1)}, f32[64,128]{1,0:T(8,128)S(1)}) %tuple.112, (f32[1,256,256]{2,1,0:T(8,128)}, f32[64,256]{1,0:T(8,128)S(1)}, ...), branch_computations={%region_21.21_spmd, %region_22.22_spmd} | conditional | flops 591699968 | bytes 8421464 | solution.py:183
  172.7 2.1 %fusion.45 = f32[256,256]{1,0:T(8,128)} fusion(f32[256,256]{1,0:T(8,128)S(1)} %fusion.100, f32[256,64]{0,1:T(8,128)S(1)} %convolution_add_fusion.11, f32[64,256]{1,0:T(8,128)S(1)} %fusion.46, f32[1,256,256]{2,1,0:T(8,128)} %get-tuple-element.507), kind=kOutput, calls=%fused_computation.71 | convolution fusion | flops 50462720 | bytes 917504 | tf_op jit(solution)/shard_map/while/body/eval_jaxpr/cond/branch_1_fun/dot_general | solution.py:21
  177.2 1.8 maximum_bitcast_fusion
  (124 shorter events, 46.1 us)
Async XLA Ops:
  0.0 20.8 %collective-permute-start.10 = (f32[1,1,2,256,256]{4,3,2,1,0:T(8,128)}, f32[1,1,2,256,256]{4,3,2,1,0:T(8,128)S(1)}, u32[]{:S(2)}, u32[]{:S(2)}) collective-permute-start(f32[1,1,2,256,256]{4,3,2,1,0:T(8,128)} %param.21), channel_id=1, source_target_pairs={{10,0},{12,2},{14,4},{16,6},{18,8},{20,10},{22,12},{24,14},{26,16}... | collective-permute-start | bytes 1572872 | tf_op jit(solution)/shard_map/ppermute | solution.py:17
  2.6 20.1 %collective-permute-start.11 = (f32[1,1,2,256,256]{4,3,2,1,0:T(8,128)}, f32[1,1,2,256,256]{4,3,2,1,0:T(8,128)S(1)}, u32[]{:S(2)}, u32[]{:S(2)}) collective-permute-start(f32[1,1,2,256,256]{4,3,2,1,0:T(8,128)} %param.21), channel_id=1, source_target_pairs={{0,10},{2,12},{4,14},{6,16},{8,18},{10,20},{12,22},{14,24},{16,26}... | collective-permute-start | bytes 1572872 | tf_op jit(solution)/shard_map/ppermute | solution.py:17
  5.6 26.5 %collective-permute-start.2 = (f32[1,1,2,256,256]{4,3,2,1,0:T(8,128)}, f32[1,1,2,256,256]{4,3,2,1,0:T(8,128)S(1)}, u32[]{:S(2)}, u32[]{:S(2)}) collective-permute-start(f32[1,1,2,256,256]{4,3,2,1,0:T(8,128)} %param.21), channel_id=1, source_target_pairs={{2,0},{4,2},{6,4},{8,6},{10,8},{12,10},{14,12},{16,14},{18,16},{20... | collective-permute-start | bytes 1572872 | tf_op jit(solution)/shard_map/ppermute | solution.py:17
  10.1 24.9 %collective-permute-start.3 = (f32[1,1,2,256,256]{4,3,2,1,0:T(8,128)}, f32[1,1,2,256,256]{4,3,2,1,0:T(8,128)S(1)}, u32[]{:S(2)}, u32[]{:S(2)}) collective-permute-start(f32[1,1,2,256,256]{4,3,2,1,0:T(8,128)} %param.21), channel_id=1, source_target_pairs={{0,2},{2,4},{4,6},{6,8},{8,10},{10,12},{12,14},{14,16},{16,18},{18... | collective-permute-start | bytes 1572872 | tf_op jit(solution)/shard_map/ppermute | solution.py:17
  12.1 51.0 %collective-permute-start.4 = (f32[1,1,2,256,256]{4,3,2,1,0:T(8,128)}, f32[1,1,2,256,256]{4,3,2,1,0:T(8,128)S(1)}, u32[]{:S(2)}, u32[]{:S(2)}) collective-permute-start(f32[1,1,2,256,256]{4,3,2,1,0:T(8,128)} %param.21), channel_id=1, source_target_pairs={{4,0},{6,2},{8,4},{10,6},{12,8},{14,10},{16,12},{18,14},{20,16},{2... | collective-permute-start | bytes 1572872 | tf_op jit(solution)/shard_map/ppermute | solution.py:17
  20.8 46.8 %collective-permute-start.5 = (f32[1,1,2,256,256]{4,3,2,1,0:T(8,128)}, f32[1,1,2,256,256]{4,3,2,1,0:T(8,128)S(1)}, u32[]{:S(2)}, u32[]{:S(2)}) collective-permute-start(f32[1,1,2,256,256]{4,3,2,1,0:T(8,128)} %param.21), channel_id=1, source_target_pairs={{0,4},{2,6},{4,8},{6,10},{8,12},{10,14},{12,16},{14,18},{16,20},{1... | collective-permute-start | bytes 1572872 | tf_op jit(solution)/shard_map/ppermute | solution.py:17
  22.7 44.9 %collective-permute-start.6 = (f32[1,1,2,256,256]{4,3,2,1,0:T(8,128)}, f32[1,1,2,256,256]{4,3,2,1,0:T(8,128)}, u32[]{:S(2)}, u32[]{:S(2)}) collective-permute-start(f32[1,1,2,256,256]{4,3,2,1,0:T(8,128)} %param.21), channel_id=1, source_target_pairs={{6,0},{8,2},{10,4},{12,6},{14,8},{16,10},{18,12},{20,14},{22,16},{... | collective-permute-start | bytes 1572872 | tf_op jit(solution)/shard_map/ppermute | solution.py:17
  32.1 35.5 %collective-permute-start.7 = (f32[1,1,2,256,256]{4,3,2,1,0:T(8,128)}, f32[1,1,2,256,256]{4,3,2,1,0:T(8,128)}, u32[]{:S(2)}, u32[]{:S(2)}) collective-permute-start(f32[1,1,2,256,256]{4,3,2,1,0:T(8,128)} %param.21), channel_id=1, source_target_pairs={{0,6},{2,8},{4,10},{6,12},{8,14},{10,16},{12,18},{14,20},{16,22},{... | collective-permute-start | bytes 1572872 | tf_op jit(solution)/shard_map/ppermute | solution.py:17
  35.1 32.6 %collective-permute-start.8 = (f32[1,1,2,256,256]{4,3,2,1,0:T(8,128)}, f32[1,1,2,256,256]{4,3,2,1,0:T(8,128)}, u32[]{:S(2)}, u32[]{:S(2)}) collective-permute-start(f32[1,1,2,256,256]{4,3,2,1,0:T(8,128)} %param.21), channel_id=1, source_target_pairs={{8,0},{10,2},{12,4},{14,6},{16,8},{18,10},{20,12},{22,14},{24,16},... | collective-permute-start | bytes 1572872 | tf_op jit(solution)/shard_map/ppermute | solution.py:17
  63.0 11.4 %collective-permute-start.9 = (f32[1,1,2,256,256]{4,3,2,1,0:T(8,128)}, f32[1,1,2,256,256]{4,3,2,1,0:T(8,128)}, u32[]{:S(2)}, u32[]{:S(2)}) collective-permute-start(f32[1,1,2,256,256]{4,3,2,1,0:T(8,128)} %param.21), channel_id=1, source_target_pairs={{0,8},{2,10},{4,12},{6,14},{8,16},{10,18},{12,20},{14,22},{16,24},... | collective-permute-start | bytes 1572872 | tf_op jit(solution)/shard_map/ppermute | solution.py:17
  65.6 0.7 copy-start.9
  65.6 0.7 copy-start.10
  66.3 0.7 copy-start.8
  74.4 9.1 %copy-start.5 = (f32[1,256,256]{2,1,0:T(8,128)S(1)}, f32[1,256,256]{2,1,0:T(8,128)}, u32[]{:S(2)}) copy-start(f32[1,256,256]{2,1,0:T(8,128)} %param.19) | copy-start | bytes 786436
  84.4 0.8 copy-start.2
  84.4 0.8 copy-start.6
  85.1 5.0 %collective-permute-start = (f32[64,128]{1,0:T(8,128)S(1)}, f32[64,128]{1,0:T(8,128)S(1)}, u32[]{:S(2)}, u32[]{:S(2)}) collective-permute-start(f32[64,128]{1,0:T(8,128)S(1)} %get-tuple-element.831), channel_id=1, source_target_pairs={{0,1},{2,3},{4,5},{6,7},{8,9},{10,11},{12,13},{14,15},{16,17},{18,... | collective-permute-start | bytes 98312 | tf_op jit(solution)/shard_map/while/body/eval_jaxpr/ppermute | solution.py:17
  111.1 1.0 copy-start
  115.1 1.0 copy-start.1
  116.0 2.9 %collective-permute-start = (f32[64,128]{1,0:T(8,128)S(1)}, f32[64,128]{1,0:T(8,128)S(1)}, u32[]{:S(2)}, u32[]{:S(2)}) collective-permute-start(f32[64,128]{1,0:T(8,128)S(1)} %get-tuple-element.831), channel_id=1, source_target_pairs={{0,1},{2,3},{4,5},{6,7},{8,9},{10,11},{12,13},{14,15},{16,17},{18,... | collective-permute-start | bytes 98312 | tf_op jit(solution)/shard_map/while/body/eval_jaxpr/ppermute | solution.py:17
  119.7 31.4 %collective-permute-start.1 = (f32[64,128]{1,0:T(8,128)S(1)}, f32[64,128]{1,0:T(8,128)S(1)}, u32[]{:S(2)}, u32[]{:S(2)}) collective-permute-start(f32[64,128]{1,0:T(8,128)S(1)} %get-tuple-element.869), channel_id=1, source_target_pairs={{1,0},{3,2},{5,4},{7,6},{9,8},{11,10},{13,12},{15,14},{17,16},{19,... | collective-permute-start | bytes 98312 | tf_op jit(solution)/shard_map/while/body/eval_jaxpr/ppermute | solution.py:17
  151.0 14.5 %collective-permute-start.1 = (f32[64,128]{1,0:T(8,128)S(1)}, f32[64,128]{1,0:T(8,128)S(1)}, u32[]{:S(2)}, u32[]{:S(2)}) collective-permute-start(f32[64,128]{1,0:T(8,128)S(1)} %get-tuple-element.869), channel_id=1, source_target_pairs={{1,0},{3,2},{5,4},{7,6},{9,8},{11,10},{13,12},{15,14},{17,16},{19,... | collective-permute-start | bytes 98312 | tf_op jit(solution)/shard_map/while/body/eval_jaxpr/ppermute | solution.py:17
  170.8 1.0 copy-start.3
  176.3 1.0 copy-start.4
  (1 other events, 0.7 us)
where the time goes:
time: 180 us; the launch traced here: 179 us
  waiting for transfers between devices  91.2 us (51%)
  starting transfers between devices  33.8 us (19%)
  matrix products  33.8 us (19%)
  other arithmetic  13.6 us (8%)
  local copies, waits for them, and re-layouts  3.84 us (2%)
  loops' own time  1.99 us (1%)
    ppermute x14, waiting for transfers between devices, passed_along(): lax.ppermute(value, axis, [(source, source + steps) for source in range(i...  91.2 us
    ppermute x14, starting transfers between devices, passed_along(): lax.ppermute(value, axis, [(source, source + steps) for source in range(i...  33.8 us
    dot_general x73, matrix products, product(): return jnp.matmul(left, right, precision=highest)  33.8 us
    mul x1, other arithmetic, on_device(): sigma = summed.reshape(count_dev, 2, width, width) * profile  9.12 us
  transfers between devices with their start and end apart: 14, of which 9 were waited for; matrix products, arithmetic and copies ran while one was open for 1% of the time, Pallas kernels for 0%

commit v1 on v0

v1 whole, which is shorter than its diff:
```python
import jax
import jax.numpy as jnp
from jax import lax
from jax.experimental import pallas as pl
from jax.experimental.pallas import tpu as pltpu
from jax.sharding import PartitionSpec as P

SPAN = 5
BROAD = 0.02
DOUBLINGS = 4

f32 = jnp.float32
bf16 = jnp.bfloat16
NN = (((1,), (0,)), ((), ()))
NT = (((1,), (1,)), ((), ()))
TN = (((0,), (0,)), ((), ()))


def split(x):
    high = x.astype(bf16)
    return high, (x - high.astype(f32)).astype(bf16)


def mm(a, b, dims=NN):
    return lax.dot_general(a, b, dims, preferred_element_type=f32)


def left3(*terms):
    out = []
    for x in terms:
        high, low = split(x)
        out += [high, high, low]
    return jnp.concatenate(out, axis=1)


def right3(*terms, axis=0):
    out = []
    for x in terms:
        high, low = split(x)
        out += [high, low, high]
    return jnp.concatenate(out, axis=axis)


def pair(x, axis):
    return jnp.concatenate(split(x), axis=axis)


def twice(x, axis):
    return jnp.concatenate([x, x], axis=axis)


def both(x_re, x_im):
    return jnp.concatenate([x_re, x_im], axis=0)


def skew(e):
    return 0.5 * (e - e.T)


def herm_left(e, q):
    return left3(e, -2.0 * q)


def any_left(y_re, y_im):
    return jnp.concatenate([left3(y_re, -(y_re + y_im)), left3(y_im, y_re - y_im)], axis=0)


def complex_mm(a_re, a_im, b_re, b_im):
    rows = a_re.shape[0]
    out = mm(
        jnp.concatenate([left3(a_re, -a_im), left3(a_im, a_re)], axis=0), right3(b_re, b_im)
    )
    return out[:rows], out[rows:]


def one_hot(width, face):
    return (lax.broadcasted_iota(jnp.int32, (width, face.shape[1]), 0) == face).astype(bf16)


def unit_of(width):
    row = lax.broadcasted_iota(jnp.int32, (width, width), 0)
    return (row == lax.broadcasted_iota(jnp.int32, (width, width), 1)).astype(f32)


def assemble(energy, ham, profile, sig, coup, left, in_re, in_im):
    width, faces = ham.shape[0], coup.shape[0]
    placed = mm(twice(one_hot(width, left), 1), pair(coup, 1), NT)
    t_re = mm(left3(placed), right3(in_re))
    t_im = mm(left3(placed), right3(in_im))
    bound = mm(both(left3(t_re), left3(t_im)), right3(placed, axis=1), NT)
    unit = unit_of(width)
    a_re = energy * unit - ham - profile * sig[0] - bound[:width]
    a_im = BROAD * unit - profile * sig[1] - bound[width:]
    return a_re, a_im


def begin(a_re, a_im):
    total = a_re + a_im
    gram = mm(left3(total, -2.0 * a_re), right3(total, a_im, axis=1), NT)
    modulus = jnp.sqrt(a_re * a_re + a_im * a_im)
    col_norm = jnp.max(jnp.sum(modulus, axis=0))
    row_norm = jnp.max(jnp.sum(modulus, axis=1))
    scale = 1.0 / (col_norm * row_norm)
    e = unit_of(a_re.shape[0]) - scale * gram
    return e, (-scale) * skew(gram), scale


def corner(a_re, a_im, right):
    width, faces = a_re.shape[0], right.shape[1]
    hot = one_hot(width, right)
    e, q, scale = begin(a_re, a_im)
    picked = twice(hot.T, 1)
    y_re = scale * mm(picked, pair(a_re, 1), NT)
    y_im = -scale * mm(picked, pair(a_im, 1), NT)
    powers = []
    for turn in range(DOUBLINGS):
        powers.append((e, q))
        weights = right3(e, q)
        if turn < DOUBLINGS - 1:
            out = mm(jnp.concatenate([herm_left(e, q), any_left(y_re, y_im)], axis=0), weights)
            e = out[:width]
            q = skew(e)
            out = out[width:]
        else:
            out = mm(any_left(y_re, y_im), weights)
        y_re = y_re + out[:faces]
        y_im = y_im + out[faces:]
    out = mm(any_left(y_re, y_im), weights)
    out = mm(any_left(out[:faces], out[faces:]), weights)
    y_re = y_re + out[:faces]
    y_im = y_im + out[faces:]
    face = mm(pair(both(y_re, y_im), 1), twice(hot, 0))
    return face[:faces], face[faces:], powers, scale


def lead_face(faces):
    return jnp.zeros((faces, faces), f32), -0.5 * unit_of(faces)


def first_kernel(energy, ham, profile, sig, coup, left, right, face_out):
    faces = coup.shape[0]
    a_re, a_im = assemble(energy[0], ham[...], profile[...], sig, coup[...], left[...], *lead_face(faces))
    f_re, f_im, _, _ = corner(a_re, a_im, right[...])
    face_out[:, :faces] = f_re
    face_out[:, faces:] = f_im


def message_of(f_re, f_im, m_re, m_im, coup, left, right, width):
    faces = coup.shape[0]
    order = mm(one_hot(width, left), one_hot(width, right), TN).astype(bf16)
    mixed = mm(pair(coup, 1), twice(order, 0))
    if m_re is not None:
        t_re, t_im = complex_mm(f_re, f_im, m_re, m_im)
        c_re, c_im = complex_mm(t_re, t_im, f_re, f_im)
        f_re, f_im = f_re + c_re, f_im + c_im
    t = mm(left3(both(f_re, f_im)), right3(mixed, axis=1), NT)
    wide = jnp.concatenate([t[:faces], t[faces:]], axis=1)
    return mm(left3(mixed), right3(wide))


def next_kernel(
    energy, first, ham, profile, sig, coup, left, right, incoming,
    face_out, message_out, e_out, q_out, a_out, scale_out,
):
    width, faces = ham.shape[0], coup.shape[0]
    lead_re, lead_im = lead_face(faces)
    is_first = first[0] == 1
    in_re = jnp.where(is_first, lead_re, incoming[:, :faces])
    in_im = jnp.where(is_first, lead_im, incoming[:, faces:])
    a_re, a_im = assemble(energy[0], ham[...], profile[...], sig, coup[...], left[...], in_re, in_im)
    f_re, f_im, powers, scale = corner(a_re, a_im, right[...])
    face_out[:, :faces] = f_re
    face_out[:, faces:] = f_im
    message_out[...] = message_of(f_re, f_im, None, None, coup[...], left[...], right[...], width)
    for turn, (e, q) in enumerate(powers):
        e_out[turn] = e
        q_out[turn] = q
    a_out[0] = a_re
    a_out[1] = a_im
    scale_out[0] = scale


def message_kernel(face, message, coup, left, right, width_like, message_out):
    faces = coup.shape[0]
    message_out[...] = message_of(
        face[:, :faces], face[:, faces:], message[:, :faces], message[:, faces:],
        coup[...], left[...], right[...], width_like.shape[0],
    )


def full_kernel(scale, e_in, q_in, a_in, right, g_out, cols_out, rows_out):
    width, faces = a_in.shape[1], right.shape[1]
    unit = unit_of(width)
    s_e, s_q = unit + e_in[0], q_in[0]
    for turn in range(1, DOUBLINGS):
        e, q = e_in[turn], q_in[turn]
        weights = right3(e, q)
        if turn < DOUBLINGS - 1:
            s_e = s_e + mm(herm_left(s_e, s_q), weights)
        else:
            out = mm(jnp.concatenate([herm_left(s_e, s_q), herm_left(e, q)], axis=0), weights)
            s_e = s_e + out[:width]
            e = out[width:]
        s_q = skew(s_e)
    s_e = s_e + mm(herm_left(s_e, s_q), right3(e, skew(e)))
    s_q = skew(s_e)
    b, c = a_in[0].T, a_in[1].T
    g = scale[0] * mm(any_left(b, -c), right3(s_e, s_q))
    g_out[0] = g[:width]
    g_out[1] = g[width:]
    hot = one_hot(width, right[...])
    high, low = split(g)
    cols_out[...] = mm(jnp.concatenate([high, low], axis=1), twice(hot, 0))
    wide_high = jnp.concatenate([high[:width], high[width:]], axis=1)
    wide_low = jnp.concatenate([low[:width], low[width:]], axis=1)
    rows_out[...] = mm(twice(hot.T, 1), jnp.concatenate([wide_high, wide_low], axis=0))


def last_kernel(g, cols, rows, message, green_out):
    width, faces = g.shape[1], message.shape[0]
    t_re, t_im = complex_mm(
        message[:, :faces], message[:, faces:], rows[:, :width], rows[:, width:]
    )
    c_re, c_im = complex_mm(cols[:width], cols[width:], t_re, t_im)
    green_out[0, 0, 0] = g[0] + c_re
    green_out[0, 0, 1] = g[1] + c_im


def call(kernel, outs, scalars, *arrays, scalar_outs=()):
    smem = pl.BlockSpec(memory_space=pltpu.SMEM)
    vmem = pl.BlockSpec(memory_space=pltpu.VMEM)
    return pl.pallas_call(
        kernel,
        out_shape=[jax.ShapeDtypeStruct(shape, f32) for shape in (*outs, *scalar_outs)],
        in_specs=[smem] * len(scalars) + [vmem] * len(arrays),
        out_specs=[vmem] * len(outs) + [smem] * len(scalar_outs),
        compiler_params=pltpu.CompilerParams(vmem_limit_bytes=40 * 2**20),
    )(*scalars, *arrays)


def passed_along(value, axis, steps):
    count = lax.axis_size(axis)
    initial, last = (max(0, -steps), min(count, count - steps))
    return lax.ppermute(value, axis, [(source, source + steps) for source in range(initial, last)])


def exchange(green_prev, phonon_weights, source, weight_index):
    base = lax.axis_index("energy")
    table_size = phonon_weights.shape[0]
    chosen = jnp.sum(
        phonon_weights[None, :] * (weight_index[0][:, None] == jnp.arange(table_size, dtype=jnp.int32)[None, :]),
        axis=1,
    )
    pieces = [(green_prev, base)]
    for offset in range(1, SPAN + 1):
        pieces.append((passed_along(green_prev, "energy", -offset), base + offset))
        pieces.append((passed_along(green_prev, "energy", offset), base - offset))
    total = 0.0
    for piece, position in pieces:
        total = total + jnp.sum(chosen * (source[0] == position)) * piece[0, 0]
    return total


def on_device(
    energies, hamiltonian, coupling, green_prev, profile, phonon_weights, source, weight_index, left_face, right_face,
):
    width, faces = hamiltonian.shape[1], coupling.shape[1]
    slab_count = lax.axis_size("slab")
    first = (lax.axis_index("slab") == 0).astype(jnp.int32)[None]
    sig = exchange(green_prev, phonon_weights, source, weight_index)
    block = (width, width)
    face = (faces, 2 * faces)
    ham, coup = hamiltonian[0], coupling[0]
    (sent,) = call(first_kernel, [face], [energies], ham, profile, sig, coup, left_face, right_face)
    for turn in range(1, slab_count):
        incoming = passed_along(sent, "slab", 1)
        sent, message, e, q, a, scale = call(
            next_kernel,
            [face, face, (DOUBLINGS, *block), (DOUBLINGS, *block), (2, *block)],
            [energies, first],
            ham, profile, sig, coup, left_face, right_face, incoming,
            scalar_outs=[(1,)],
        )
    incoming = passed_along(message, "slab", -1)
    for turn in range(2, slab_count):
        (message,) = call(message_kernel, [face], [], sent, incoming, coup, left_face, right_face, ham)
        incoming = passed_along(message, "slab", -1)
    g, cols, rows = call(
        full_kernel, [(2, *block), (2 * width, faces), (faces, 2 * width)], [scale], e, q, a, right_face
    )
    (green,) = call(last_kernel, [(1, 1, 2, *block)], [], g, cols, rows, incoming)
    return green


def solution(mesh):
    in_specs = (
        P("energy"),
        P("slab", None, None),
        P("slab", None, None),
        P("energy", "slab", None, None, None),
        P(),
        P(),
        P("energy", None),
        P("energy", None),
        P("slab", None),
        P("slab", None),
    )
    out_specs = P("energy", "slab", None, None, None)
    return jax.shard_map(on_device, mesh=mesh, in_specs=in_specs, out_specs=out_specs, check_vma=False)
```

time: 180 us -> 110 us (0.61)
  the two profiles are of different devices: /device:TPU:16 before, /device:TPU:28 now
where the time goes in v1:
time: 110 us
  waiting for transfers between devices  48.1 us (44%)
  starting transfers between devices  32.7 us (30%)
  Pallas kernels  15.6 us (14%)
  other arithmetic  10.4 us (9%)
  local copies, waits for them, and re-layouts  1.78 us (2%)
    ppermute x12, waiting for transfers between devices, passed_along(): lax.ppermute(value, axis, [(source, source + steps) for source in range(i...  48.1 us
    ppermute x12, starting transfers between devices, passed_along(): lax.ppermute(value, axis, [(source, source + steps) for source in range(i...  32.7 us
    pallas_call x4, Pallas kernels, call(): pl.pallas_call(kernel, out_shape=[jax.ShapeDtypeStruct(shape, f32) for sh...  15.6 us
    add x1, other arithmetic, exchange(): total = total + jnp.sum(chosen * (source[0] == position)) * piece[0, 0]  9.53 us
  transfers between devices with their start and end apart: 12, of which 4 were waited for; matrix products, arithmetic and copies ran while one was open for 1% of the time, Pallas kernels for 4%

profile of v1, /device:TPU:28, one launch (start us, length us, event | category | flops | bytes accessed | tf_op | source)
XLA Modules:
  0.0 109.5 jit_solution(44547070225964816)
XLA Ops:
  0.0 2.7 %collective-permute-start = (f32[1,1,2,256,256]{4,3,2,1,0:T(8,128)}, f32[1,1,2,256,256]{4,3,2,1,0:T(8,128)S(1)}, u32[]{:S(2)}, u32[]{:S(2)}) collective-permute-start(f32[1,1,2,256,256]{4,3,2,1,0:T(8,128)} %param.13), channel_id=1, source_target_pairs={{2,0},{4,2},{6,4},{8,6},{10,8},{12,10},{14,12},{16,14},{18,16},{20... | collective-permute-start | bytes 1572872 | tf_op jit(solution)/shard_map/ppermute | solution.py:244
  2.7 1.9 %collective-permute-start.1 = (f32[1,1,2,256,256]{4,3,2,1,0:T(8,128)}, f32[1,1,2,256,256]{4,3,2,1,0:T(8,128)S(1)}, u32[]{:S(2)}, u32[]{:S(2)}) collective-permute-start(f32[1,1,2,256,256]{4,3,2,1,0:T(8,128)} %param.13), channel_id=1, source_target_pairs={{0,2},{2,4},{4,6},{6,8},{8,10},{10,12},{12,14},{14,16},{16,18},{18... | collective-permute-start | bytes 1572872 | tf_op jit(solution)/shard_map/ppermute | solution.py:244
  4.7 3.0 %collective-permute-start.2 = (f32[1,1,2,256,256]{4,3,2,1,0:T(8,128)}, f32[1,1,2,256,256]{4,3,2,1,0:T(8,128)S(1)}, u32[]{:S(2)}, u32[]{:S(2)}) collective-permute-start(f32[1,1,2,256,256]{4,3,2,1,0:T(8,128)} %param.13), channel_id=1, source_target_pairs={{4,0},{6,2},{8,4},{10,6},{12,8},{14,10},{16,12},{18,14},{20,16},{2... | collective-permute-start | bytes 1572872 | tf_op jit(solution)/shard_map/ppermute | solution.py:244
  7.6 2.9 %collective-permute-start.3 = (f32[1,1,2,256,256]{4,3,2,1,0:T(8,128)}, f32[1,1,2,256,256]{4,3,2,1,0:T(8,128)S(1)}, u32[]{:S(2)}, u32[]{:S(2)}) collective-permute-start(f32[1,1,2,256,256]{4,3,2,1,0:T(8,128)} %param.13), channel_id=1, source_target_pairs={{0,4},{2,6},{4,8},{6,10},{8,12},{10,14},{12,16},{14,18},{16,20},{1... | collective-permute-start | bytes 1572872 | tf_op jit(solution)/shard_map/ppermute | solution.py:244
  10.5 2.8 %collective-permute-start.4 = (f32[1,1,2,256,256]{4,3,2,1,0:T(8,128)}, f32[1,1,2,256,256]{4,3,2,1,0:T(8,128)}, u32[]{:S(2)}, u32[]{:S(2)}) collective-permute-start(f32[1,1,2,256,256]{4,3,2,1,0:T(8,128)} %param.13), channel_id=1, source_target_pairs={{6,0},{8,2},{10,4},{12,6},{14,8},{16,10},{18,12},{20,14},{22,16},{... | collective-permute-start | bytes 1572872 | tf_op jit(solution)/shard_map/ppermute | solution.py:244
  13.3 3.6 %collective-permute-start.5 = (f32[1,1,2,256,256]{4,3,2,1,0:T(8,128)}, f32[1,1,2,256,256]{4,3,2,1,0:T(8,128)S(1)}, u32[]{:S(2)}, u32[]{:S(2)}) collective-permute-start(f32[1,1,2,256,256]{4,3,2,1,0:T(8,128)} %param.13), channel_id=1, source_target_pairs={{0,6},{2,8},{4,10},{6,12},{8,14},{10,16},{12,18},{14,20},{16,22},{... | collective-permute-start | bytes 1572872 | tf_op jit(solution)/shard_map/ppermute | solution.py:244
  16.9 2.9 %collective-permute-start.6 = (f32[1,1,2,256,256]{4,3,2,1,0:T(8,128)}, f32[1,1,2,256,256]{4,3,2,1,0:T(8,128)S(1)}, u32[]{:S(2)}, u32[]{:S(2)}) collective-permute-start(f32[1,1,2,256,256]{4,3,2,1,0:T(8,128)} %param.13), channel_id=1, source_target_pairs={{8,0},{10,2},{12,4},{14,6},{16,8},{18,10},{20,12},{22,14},{24,16},... | collective-permute-start | bytes 1572872 | tf_op jit(solution)/shard_map/ppermute | solution.py:244
  19.9 26.0 %collective-permute-done.2 = f32[1,1,2,256,256]{4,3,2,1,0:T(8,128)S(1)} collective-permute-done((f32[1,1,2,256,256]{4,3,2,1,0:T(8,128)}, f32[1,1,2,256,256]{4,3,2,1,0:T(8,128)S(1)}, u32[]{:S(2)}, u32[]{:S(2)}) %collective-permute-start.2) | collective-permute-done | bytes 524320 | tf_op jit(solution)/shard_map/ppermute | solution.py:244
  45.9 1.3 %collective-permute-start.7 = (f32[1,1,2,256,256]{4,3,2,1,0:T(8,128)}, f32[1,1,2,256,256]{4,3,2,1,0:T(8,128)}, u32[]{:S(2)}, u32[]{:S(2)}) collective-permute-start(f32[1,1,2,256,256]{4,3,2,1,0:T(8,128)} %param.13), channel_id=1, source_target_pairs={{0,8},{2,10},{4,12},{6,14},{8,16},{10,18},{12,20},{14,22},{16,24},... | collective-permute-start | bytes 1572872 | tf_op jit(solution)/shard_map/ppermute | solution.py:244
  47.2 7.5 %collective-permute-start.8 = (f32[1,1,2,256,256]{4,3,2,1,0:T(8,128)}, f32[1,1,2,256,256]{4,3,2,1,0:T(8,128)}, u32[]{:S(2)}, u32[]{:S(2)}) collective-permute-start(f32[1,1,2,256,256]{4,3,2,1,0:T(8,128)} %param.13), channel_id=1, source_target_pairs={{10,0},{12,2},{14,4},{16,6},{18,8},{20,10},{22,12},{24,14},{26,16}... | collective-permute-start | bytes 1572872 | tf_op jit(solution)/shard_map/ppermute | solution.py:244
  54.6 1.3 %collective-permute-start.9 = (f32[1,1,2,256,256]{4,3,2,1,0:T(8,128)}, f32[1,1,2,256,256]{4,3,2,1,0:T(8,128)}, u32[]{:S(2)}, u32[]{:S(2)}) collective-permute-start(f32[1,1,2,256,256]{4,3,2,1,0:T(8,128)} %param.13), channel_id=1, source_target_pairs={{0,10},{2,12},{4,14},{6,16},{8,18},{10,20},{12,22},{14,24},{16,26}... | collective-permute-start | bytes 1572872 | tf_op jit(solution)/shard_map/ppermute | solution.py:244
  56.6 0.6 copy-done.8
  57.9 0.7 fusion.1
  58.7 5.5 %collective-permute-done.8 = f32[1,1,2,256,256]{4,3,2,1,0:T(8,128)} collective-permute-done((f32[1,1,2,256,256]{4,3,2,1,0:T(8,128)}, f32[1,1,2,256,256]{4,3,2,1,0:T(8,128)}, u32[]{:S(2)}, u32[]{:S(2)}) %collective-permute-start.8) | collective-permute-done | bytes 524320 | tf_op jit(solution)/shard_map/ppermute | solution.py:244
  64.2 12.0 %collective-permute-done.9 = f32[1,1,2,256,256]{4,3,2,1,0:T(8,128)} collective-permute-done((f32[1,1,2,256,256]{4,3,2,1,0:T(8,128)}, f32[1,1,2,256,256]{4,3,2,1,0:T(8,128)}, u32[]{:S(2)}, u32[]{:S(2)}) %collective-permute-start.9) | collective-permute-done | bytes 524320 | tf_op jit(solution)/shard_map/ppermute | solution.py:244
  76.2 9.5 %add_bitcast_fusion.sig = f32[2,256,256]{2,1,0:T(8,128)S(1)} fusion(f32[1,1,2,256,256]{4,3,2,1,0:T(8,128)} %collective-permute-done.9, f32[1,1,2,256,256]{4,3,2,1,0:T(8,128)} %collective-permute-done.8, f32[1,1,2,256,256]{4,3,2,1,0:T(8,128)} %collective-permute-done.7, f32[1,1,2,256,256]{4,3,2,1,0:T(8,128)} %copy-done.6, f32[1,1,2,256,256]{4,3,2,1,0:T(8,128)} %copy-done.5, ...), kind=kLoop, calls=%fused_computation | loop fusion | flops 2752512 | bytes 6291500 | tf_op jit(solution)/shard_map/add | solution.py:260
  85.8 0.6 copy-done.3
  86.4 4.6 %shard_map.100 = f32[64,128]{1,0:T(8,128)S(1)} custom-call(f32[1]{0:T(128)S(6)} %copy.11.energy, f32[256,256]{1,0:T(8,128)S(1)} %bitcast.50, f32[256,256]{1,0:T(8,128)S(1)} %copy-done.1, f32[2,256,256]{2,1,0:T(8,128)S(1)} %add_bitcast_fusion.sig, f32[64,64]{1,0:T(8,128)S(1)} %bitcast.52, s32[1,64]{1,0:T(1,128)S(1)} %copy-done.4, s32[1,64]{1,0:T(1,128)S(1)} %copy-done.3), custom_call_target="tpu_custom_call" | custom-call | tf_op jit(solution)/shard_map/pallas_call | solution.py:232
  91.0 1.3 %collective-permute-start.10 = (f32[64,128]{1,0:T(8,128)S(1)}, f32[64,128]{1,0:T(8,128)S(1)}, u32[]{:S(2)}, u32[]{:S(2)}) collective-permute-start(f32[64,128]{1,0:T(8,128)S(1)} %shard_map.100), channel_id=1, source_target_pairs={{0,1},{2,3},{4,5},{6,7},{8,9},{10,11},{12,13},{14,15},{16,17},{18,... | collective-permute-start | bytes 98312 | tf_op jit(solution)/shard_map/ppermute | solution.py:244
  92.3 4.5 %collective-permute-done.10.incoming = f32[64,128]{1,0:T(8,128)S(1)} collective-permute-done((f32[64,128]{1,0:T(8,128)S(1)}, f32[64,128]{1,0:T(8,128)S(1)}, u32[]{:S(2)}, u32[]{:S(2)}) %collective-permute-start.10) | collective-permute-done | bytes 32800 | tf_op jit(solution)/shard_map/ppermute | solution.py:244
  96.8 5.4 %shard_map.101 = (f32[64,128]{1,0:T(8,128)}, f32[64,128]{1,0:T(8,128)S(1)}, f32[4,256,256]{2,1,0:T(8,128)S(1)}, f32[4,256,256]{2,1,0:T(8,128)S(1)}, f32[2,256,256]{2,1,0:T(8,128)S(1)}, /*index=5*/f32[1]{0:T(128)}) custom-call(f32[1]{0:T(128)S(6)} %copy.11.energy, s32[1]{0:T(128)} %bitcast.first, f32[256,256]{1,0:T(8,128)S(1)} %bitcast.51, ...), custom_call_target="tpu_custom_call" | custom-call | tf_op jit(solution)/shard_map/pallas_call | solution.py:232
  102.3 1.6 %collective-permute-start.11 = (f32[64,128]{1,0:T(8,128)S(1)}, f32[64,128]{1,0:T(8,128)S(1)}, u32[]{:S(2)}, u32[]{:S(2)}) collective-permute-start(f32[64,128]{1,0:T(8,128)S(1)} %get-tuple-element.20), channel_id=1, source_target_pairs={{1,0},{3,2},{5,4},{7,6},{9,8},{11,10},{13,12},{15,14},{17,16},{19,... | collective-permute-start | bytes 98312 | tf_op jit(solution)/shard_map/ppermute | solution.py:244
  103.9 4.3 %shard_map.102 = (f32[2,256,256]{2,1,0:T(8,128)S(1)}, f32[512,64]{1,0:T(8,128)S(1)}, f32[64,512]{1,0:T(8,128)S(1)}) custom-call(f32[1]{0:T(128)} %get-tuple-element.13.scale, f32[4,256,256]{2,1,0:T(8,128)S(1)} %get-tuple-element.14.e_in, f32[4,256,256]{2,1,0:T(8,128)S(1)} %get-tuple-element.15.q_in, f32[2,256,256]{2,1,0:T(8,128)S(1)} %get-tuple-element.16.a_in, ...), custom_call_target="tpu_custom_call" | custom-call | tf_op jit(solution)/shard_map/pallas_call | solution.py:232
  108.2 1.4 %shard_map.103 = f32[1,1,2,256,256]{4,3,2,1,0:T(8,128)} custom-call(f32[2,256,256]{2,1,0:T(8,128)S(1)} %get-tuple-element.17.g, f32[512,64]{1,0:T(8,128)S(1)} %get-tuple-element.18.cols, f32[64,512]{1,0:T(8,128)S(1)} %get-tuple-element.19.rows, f32[64,128]{1,0:T(8,128)S(1)} %collective-permute-done.11.message), custom_call_target="tpu_custom_call" | custom-call | tf_op jit(solution)/shard_map/pallas_call | solution.py:232
  (27 shorter events, 0.7 us)
Async XLA Ops:
  0.0 13.3 %collective-permute-start = (f32[1,1,2,256,256]{4,3,2,1,0:T(8,128)}, f32[1,1,2,256,256]{4,3,2,1,0:T(8,128)S(1)}, u32[]{:S(2)}, u32[]{:S(2)}) collective-permute-start(f32[1,1,2,256,256]{4,3,2,1,0:T(8,128)} %param.13), channel_id=1, source_target_pairs={{2,0},{4,2},{6,4},{8,6},{10,8},{12,10},{14,12},{16,14},{18,16},{20... | collective-permute-start | bytes 1572872 | tf_op jit(solution)/shard_map/ppermute | solution.py:244
  2.7 14.2 %collective-permute-start.1 = (f32[1,1,2,256,256]{4,3,2,1,0:T(8,128)}, f32[1,1,2,256,256]{4,3,2,1,0:T(8,128)S(1)}, u32[]{:S(2)}, u32[]{:S(2)}) collective-permute-start(f32[1,1,2,256,256]{4,3,2,1,0:T(8,128)} %param.13), channel_id=1, source_target_pairs={{0,2},{2,4},{4,6},{6,8},{8,10},{10,12},{12,14},{14,16},{16,18},{18... | collective-permute-start | bytes 1572872 | tf_op jit(solution)/shard_map/ppermute | solution.py:244
  4.7 41.2 %collective-permute-start.2 = (f32[1,1,2,256,256]{4,3,2,1,0:T(8,128)}, f32[1,1,2,256,256]{4,3,2,1,0:T(8,128)S(1)}, u32[]{:S(2)}, u32[]{:S(2)}) collective-permute-start(f32[1,1,2,256,256]{4,3,2,1,0:T(8,128)} %param.13), channel_id=1, source_target_pairs={{4,0},{6,2},{8,4},{10,6},{12,8},{14,10},{16,12},{18,14},{20,16},{2... | collective-permute-start | bytes 1572872 | tf_op jit(solution)/shard_map/ppermute | solution.py:244
  7.6 39.6 %collective-permute-start.3 = (f32[1,1,2,256,256]{4,3,2,1,0:T(8,128)}, f32[1,1,2,256,256]{4,3,2,1,0:T(8,128)S(1)}, u32[]{:S(2)}, u32[]{:S(2)}) collective-permute-start(f32[1,1,2,256,256]{4,3,2,1,0:T(8,128)} %param.13), channel_id=1, source_target_pairs={{0,4},{2,6},{4,8},{6,10},{8,12},{10,14},{12,16},{14,18},{16,20},{1... | collective-permute-start | bytes 1572872 | tf_op jit(solution)/shard_map/ppermute | solution.py:244
  10.5 44.1 %collective-permute-start.4 = (f32[1,1,2,256,256]{4,3,2,1,0:T(8,128)}, f32[1,1,2,256,256]{4,3,2,1,0:T(8,128)}, u32[]{:S(2)}, u32[]{:S(2)}) collective-permute-start(f32[1,1,2,256,256]{4,3,2,1,0:T(8,128)} %param.13), channel_id=1, source_target_pairs={{6,0},{8,2},{10,4},{12,6},{14,8},{16,10},{18,12},{20,14},{22,16},{... | collective-permute-start | bytes 1572872 | tf_op jit(solution)/shard_map/ppermute | solution.py:244
  13.3 45.3 %collective-permute-start.5 = (f32[1,1,2,256,256]{4,3,2,1,0:T(8,128)}, f32[1,1,2,256,256]{4,3,2,1,0:T(8,128)S(1)}, u32[]{:S(2)}, u32[]{:S(2)}) collective-permute-start(f32[1,1,2,256,256]{4,3,2,1,0:T(8,128)} %param.13), channel_id=1, source_target_pairs={{0,6},{2,8},{4,10},{6,12},{8,14},{10,16},{12,18},{14,20},{16,22},{... | collective-permute-start | bytes 1572872 | tf_op jit(solution)/shard_map/ppermute | solution.py:244
  16.9 41.7 %collective-permute-start.6 = (f32[1,1,2,256,256]{4,3,2,1,0:T(8,128)}, f32[1,1,2,256,256]{4,3,2,1,0:T(8,128)S(1)}, u32[]{:S(2)}, u32[]{:S(2)}) collective-permute-start(f32[1,1,2,256,256]{4,3,2,1,0:T(8,128)} %param.13), channel_id=1, source_target_pairs={{8,0},{10,2},{12,4},{14,6},{16,8},{18,10},{20,12},{22,14},{24,16},... | collective-permute-start | bytes 1572872 | tf_op jit(solution)/shard_map/ppermute | solution.py:244
  45.9 12.8 %collective-permute-start.7 = (f32[1,1,2,256,256]{4,3,2,1,0:T(8,128)}, f32[1,1,2,256,256]{4,3,2,1,0:T(8,128)}, u32[]{:S(2)}, u32[]{:S(2)}) collective-permute-start(f32[1,1,2,256,256]{4,3,2,1,0:T(8,128)} %param.13), channel_id=1, source_target_pairs={{0,8},{2,10},{4,12},{6,14},{8,16},{10,18},{12,20},{14,22},{16,24},... | collective-permute-start | bytes 1572872 | tf_op jit(solution)/shard_map/ppermute | solution.py:244
  47.2 17.0 %collective-permute-start.8 = (f32[1,1,2,256,256]{4,3,2,1,0:T(8,128)}, f32[1,1,2,256,256]{4,3,2,1,0:T(8,128)}, u32[]{:S(2)}, u32[]{:S(2)}) collective-permute-start(f32[1,1,2,256,256]{4,3,2,1,0:T(8,128)} %param.13), channel_id=1, source_target_pairs={{10,0},{12,2},{14,4},{16,6},{18,8},{20,10},{22,12},{24,14},{26,16}... | collective-permute-start | bytes 1572872 | tf_op jit(solution)/shard_map/ppermute | solution.py:244
  54.6 21.6 %collective-permute-start.9 = (f32[1,1,2,256,256]{4,3,2,1,0:T(8,128)}, f32[1,1,2,256,256]{4,3,2,1,0:T(8,128)}, u32[]{:S(2)}, u32[]{:S(2)}) collective-permute-start(f32[1,1,2,256,256]{4,3,2,1,0:T(8,128)} %param.13), channel_id=1, source_target_pairs={{0,10},{2,12},{4,14},{6,16},{8,18},{10,20},{12,22},{14,24},{16,26}... | collective-permute-start | bytes 1572872 | tf_op jit(solution)/shard_map/ppermute | solution.py:244
  56.6 0.7 copy-start.8
  56.6 0.7 copy-start.9
  57.3 0.7 copy-start.7
  58.6 17.6 %copy-start.5 = (f32[1,1,2,256,256]{4,3,2,1,0:T(8,128)}, f32[1,1,2,256,256]{4,3,2,1,0:T(8,128)S(1)}, u32[]{:S(2)}) copy-start(f32[1,1,2,256,256]{4,3,2,1,0:T(8,128)S(1)} %collective-permute-done.5) | copy-start | bytes 1572868
  58.6 17.6 %copy-start.6 = (f32[1,1,2,256,256]{4,3,2,1,0:T(8,128)}, f32[1,1,2,256,256]{4,3,2,1,0:T(8,128)S(1)}, u32[]{:S(2)}) copy-start(f32[1,1,2,256,256]{4,3,2,1,0:T(8,128)S(1)} %collective-permute-done.6) | copy-start | bytes 1572868
  76.2 9.6 %copy-start = (f32[1,256,256]{2,1,0:T(8,128)S(1)}, f32[1,256,256]{2,1,0:T(8,128)}, u32[]{:S(2)}) copy-start(f32[1,256,256]{2,1,0:T(8,128)} %param.11) | copy-start | bytes 786436
  76.2 9.6 %copy-start.1 = (f32[256,256]{1,0:T(8,128)S(1)}, f32[256,256]{1,0:T(8,128)}, u32[]{:S(2)}) copy-start(f32[256,256]{1,0:T(8,128)} %profile.3) | copy-start | bytes 786436
  76.2 9.6 %copy-start.2 = (f32[1,64,64]{2,1,0:T(8,128)S(1)}, f32[1,64,64]{2,1,0:T(8,128)}, u32[]{:S(2)}) copy-start(f32[1,64,64]{2,1,0:T(8,128)} %param.12) | copy-start | bytes 49156
  85.8 0.7 copy-start.3
  85.8 0.7 copy-start.4
  91.0 5.8 %collective-permute-start.10 = (f32[64,128]{1,0:T(8,128)S(1)}, f32[64,128]{1,0:T(8,128)S(1)}, u32[]{:S(2)}, u32[]{:S(2)}) collective-permute-start(f32[64,128]{1,0:T(8,128)S(1)} %shard_map.100), channel_id=1, source_target_pairs={{0,1},{2,3},{4,5},{6,7},{8,9},{10,11},{12,13},{14,15},{16,17},{18,... | collective-permute-start | bytes 98312 | tf_op jit(solution)/shard_map/ppermute | solution.py:244
  102.3 5.9 %collective-permute-start.11 = (f32[64,128]{1,0:T(8,128)S(1)}, f32[64,128]{1,0:T(8,128)S(1)}, u32[]{:S(2)}, u32[]{:S(2)}) collective-permute-start(f32[64,128]{1,0:T(8,128)S(1)} %get-tuple-element.20), channel_id=1, source_target_pairs={{1,0},{3,2},{5,4},{7,6},{9,8},{11,10},{13,12},{15,14},{17,16},{19,... | collective-permute-start | bytes 98312 | tf_op jit(solution)/shard_map/ppermute | solution.py:244

commit v2 on v1

--- a/solution.py
+++ b/solution.py
@@ -82,16 +82,13 @@
     return (row == lax.broadcasted_iota(jnp.int32, (width, width), 1)).astype(f32)
 
 
-def assemble(energy, ham, profile, sig, coup, left, in_re, in_im):
-    width, faces = ham.shape[0], coup.shape[0]
+def bounded(base_re, base_im, coup, left, in_re, in_im):
+    width = base_re.shape[0]
     placed = mm(twice(one_hot(width, left), 1), pair(coup, 1), NT)
     t_re = mm(left3(placed), right3(in_re))
     t_im = mm(left3(placed), right3(in_im))
     bound = mm(both(left3(t_re), left3(t_im)), right3(placed, axis=1), NT)
-    unit = unit_of(width)
-    a_re = energy * unit - ham - profile * sig[0] - bound[:width]
-    a_im = BROAD * unit - profile * sig[1] - bound[width:]
-    return a_re, a_im
+    return base_re - bound[:width], base_im - bound[width:]
 
 
 def begin(a_re, a_im):
@@ -137,9 +134,114 @@
     return jnp.zeros((faces, faces), f32), -0.5 * unit_of(faces)
 
 
-def first_kernel(energy, ham, profile, sig, coup, left, right, face_out):
-    faces = coup.shape[0]
-    a_re, a_im = assemble(energy[0], ham[...], profile[...], sig, coup[...], left[...], *lead_face(faces))
+ROWS = 8
+
+
+def over_x(e):
+    return e ^ 2
+
+
+def twin(e):
+    return e ^ 1
+
+
+def group_1(e):
+    return e + 4 if e % 2 == 0 else e - 4
+
+
+def group_2(e):
+    return e - 4 if e % 2 == 0 else e + 4
+
+
+def sent(value, pairs):
+    return lax.ppermute(value, "energy", pairs)
+
+
+def pairs_of(target, count):
+    return [(e, target(e)) for e in range(count) if 0 <= target(e) < count]
+
+
+def pack_kernel(source, weight_index, table, green, re_out, im_out):
+    width = green.shape[3]
+    re_out[:width] = green[0, 0, 0]
+    im_out[:width] = green[0, 0, 1]
+    row = lax.broadcasted_iota(jnp.int32, (ROWS, width), 0)
+    rows = jnp.zeros((ROWS, width), f32)
+    for term in range(2):
+        rows = jnp.where(row == term, source[0, term].astype(f32), rows)
+        rows = jnp.where(row == 2 + term, table[weight_index[0, term]], rows)
+    re_out[width:] = rows
+    im_out[width:] = rows
+
+
+def coef_of(source, weight_index, table, index):
+    weight = jnp.float32(0.0)
+    for term in range(2):
+        weight += jnp.where(source[0, term] == index, table[weight_index[0, term]], 0.0)
+    return weight
+
+
+def coef(rows, index):
+    at = index.astype(f32)
+    return jnp.where(rows[0:1] == at, rows[2:3], 0.0) + jnp.where(rows[1:2] == at, rows[3:4], 0.0)
+
+
+def held(e):
+    step = jnp.where(e % 2 == 0, 4, -4)
+    other = e + 1 - 2 * (e % 2)
+    return other, e - step, e + step, other + step, other - step
+
+
+def outward_kernel(mine, pair, one, two, pair_one, pair_two, x, pair_x, near, over_x_out, out_1, out_2):
+    width = mine.shape[3]
+    e = lax.axis_index("energy")
+    other, at_one, at_two, at_pair_one, at_pair_two = held(e)
+    rows = x[width:]
+    total = coef(rows, e) * mine[0, 0, 0] + coef(rows, other) * pair[0, 0, 0]
+    total += coef(rows, at_one) * one[:width] + coef(rows, at_two) * two[:width]
+    total += coef(rows, at_pair_one) * pair_one[:width] + coef(rows, at_pair_two) * pair_two[:width]
+    over_x_out[...] = total
+    across = e + 2 - 4 * ((e // 2) % 2)
+    pair_across = other + 2 - 4 * ((other // 2) % 2)
+    for target, rows, out in ((at_two, two[width:], out_1), (at_one, one[width:], out_2)):
+        upward = target > e
+        near_index = jnp.where(upward, e - 1, e + 1)
+        counts = e % 4 == jnp.where(upward, 0, 3)
+        total = coef(rows, e) * mine[0, 0, 1] + coef(rows, other) * pair[0, 0, 1]
+        total += coef(rows, across) * x[:width] + coef(rows, pair_across) * pair_x[:width]
+        out[...] = total + jnp.where(counts, coef(rows, near_index), 0.0) * near[:width]
+
+
+def own_kernel(source, weight_index, table, mine, pair, one, two, pair_one, pair_two, x, pair_x, own_out):
+    width = mine.shape[3]
+    e = lax.axis_index("energy")
+    other, at_one, at_two, at_pair_one, at_pair_two = held(e)
+    across = e + 2 - 4 * ((e // 2) % 2)
+    pair_across = other + 2 - 4 * ((other // 2) % 2)
+
+    def weight(index):
+        return coef_of(source, weight_index, table, index)
+
+    total = weight(e) * mine[0, 0, 0] + weight(other) * pair[0, 0, 0]
+    total += weight(at_one) * one[:width] + weight(at_two) * two[:width]
+    own_out[0] = total + weight(at_pair_one) * pair_one[:width] + weight(at_pair_two) * pair_two[:width]
+    total = weight(e) * mine[0, 0, 1] + weight(other) * pair[0, 0, 1]
+    own_out[1] = total + weight(across) * x[:width] + weight(pair_across) * pair_x[:width]
+
+
+def first_kernel(energy, source, weight_index, table, ham, profile, own, over_x, far, over_1, over_2, coup, left, right, face_out, base_out):
+    width, faces = ham.shape[1], coup.shape[1]
+    e = lax.axis_index("energy")
+    far_index = jnp.where(e % 4 == 3, e + SPAN, e - SPAN)
+    weight = coef_of(source, weight_index, table, far_index)
+    sig_re = own[0] + over_x[...] + weight * far[:width]
+    sig_im = own[1] + over_1[...] + over_2[...]
+    unit = unit_of(width)
+    base_re = energy[0] * unit - ham[0] - profile[...] * sig_re
+    base_im = BROAD * unit - profile[...] * sig_im
+    base_out[0] = base_re
+    base_out[1] = base_im
+    a_re, a_im = bounded(base_re, base_im, coup[0], left[...], *lead_face(faces))
     f_re, f_im, _, _ = corner(a_re, a_im, right[...])
     face_out[:, :faces] = f_re
     face_out[:, faces:] = f_im
@@ -159,19 +261,19 @@
 
 
 def next_kernel(
-    energy, first, ham, profile, sig, coup, left, right, incoming,
+    base, coup, left, right, incoming,
     face_out, message_out, e_out, q_out, a_out, scale_out,
 ):
-    width, faces = ham.shape[0], coup.shape[0]
+    width, faces = base.shape[1], coup.shape[1]
     lead_re, lead_im = lead_face(faces)
-    is_first = first[0] == 1
+    is_first = lax.axis_index("slab") == 0
     in_re = jnp.where(is_first, lead_re, incoming[:, :faces])
     in_im = jnp.where(is_first, lead_im, incoming[:, faces:])
-    a_re, a_im = assemble(energy[0], ham[...], profile[...], sig, coup[...], left[...], in_re, in_im)
+    a_re, a_im = bounded(base[0], base[1], coup[0], left[...], in_re, in_im)
     f_re, f_im, powers, scale = corner(a_re, a_im, right[...])
     face_out[:, :faces] = f_re
     face_out[:, faces:] = f_im
-    message_out[...] = message_of(f_re, f_im, None, None, coup[...], left[...], right[...], width)
+    message_out[...] = message_of(f_re, f_im, None, None, coup[0], left[...], right[...], width)
     for turn, (e, q) in enumerate(powers):
         e_out[turn] = e
         q_out[turn] = q
@@ -180,11 +282,11 @@
     scale_out[0] = scale
 
 
-def message_kernel(face, message, coup, left, right, width_like, message_out):
-    faces = coup.shape[0]
+def message_kernel(face, message, coup, left, right, base, message_out):
+    faces = coup.shape[1]
     message_out[...] = message_of(
         face[:, :faces], face[:, faces:], message[:, :faces], message[:, faces:],
-        coup[...], left[...], right[...], width_like.shape[0],
+        coup[0], left[...], right[...], base.shape[1],
     )
 
 
@@ -238,27 +340,40 @@
     )(*scalars, *arrays)
 
 
-def passed_along(value, axis, steps):
-    count = lax.axis_size(axis)
+def exchange(green_prev, phonon_weights, source, weight_index):
+    count = lax.axis_size("energy")
+    width = green_prev.shape[-1]
+    scalars = [source, weight_index, phonon_weights]
+    block, tagged = (width, width), (width + ROWS, width)
+    all_twin, all_x = pairs_of(twin, count), pairs_of(over_x, count)
+    all_1, all_2 = pairs_of(group_1, count), pairs_of(group_2, count)
+    groups = count // 4
+    near_pairs = [(4 * k, 4 * k - 1) for k in range(2, groups)] + [(4 * k + 3, 4 * k + 4) for k in range(groups - 2)]
+    far_pairs = [p for k in range(1, groups - 1) for p in ((4 * k, 4 * k - 1), (4 * k + 3, 4 * k + 4))]
+    pair = sent(green_prev, all_twin)
+    re, im = call(pack_kernel, [tagged, tagged], scalars, green_prev)
+    x = sent(im, all_x)
+    one = sent(re, all_1)
+    two = sent(re, all_2)
+    near = sent(im, near_pairs)
+    pair_x = sent(x, all_twin)
+    pair_one = sent(one, all_twin)
+    pair_two = sent(two, all_twin)
+    far = sent(two, far_pairs)
+    over_x_sum, sum_1, sum_2 = call(
+        outward_kernel, [block] * 3, [], green_prev, pair, one, two, pair_one, pair_two, x, pair_x, near
+    )
+    from_x = sent(over_x_sum, all_x)
+    from_1 = sent(sum_1, all_1)
+    from_2 = sent(sum_2, all_2)
+    (own,) = call(own_kernel, [(2, *block)], scalars, green_prev, pair, one, two, pair_one, pair_two, x, pair_x)
+    return own, from_x, far, from_1, from_2
+
+
+def passed_along(value, steps):
+    count = lax.axis_size("slab")
     initial, last = (max(0, -steps), min(count, count - steps))
-    return lax.ppermute(value, axis, [(source, source + steps) for source in range(initial, last)])
-
-
-def exchange(green_prev, phonon_weights, source, weight_index):
-    base = lax.axis_index("energy")
-    table_size = phonon_weights.shape[0]
-    chosen = jnp.sum(
-        phonon_weights[None, :] * (weight_index[0][:, None] == jnp.arange(table_size, dtype=jnp.int32)[None, :]),
-        axis=1,
-    )
-    pieces = [(green_prev, base)]
-    for offset in range(1, SPAN + 1):
-        pieces.append((passed_along(green_prev, "energy", -offset), base + offset))
-        pieces.append((passed_along(green_prev, "energy", offset), base - offset))
-    total = 0.0
-    for piece, position in pieces:
-        total = total + jnp.sum(chosen * (source[0] == position)) * piece[0, 0]
-    return total
+    return lax.ppermute(value, "slab", [(start, start + steps) for start in range(initial, last)])
 
 
 def on_device(
@@ -266,25 +381,24 @@
 ):
     width, faces = hamiltonian.shape[1], coupling.shape[1]
     slab_count = lax.axis_size("slab")
-    first = (lax.axis_index("slab") == 0).astype(jnp.int32)[None]
-    sig = exchange(green_prev, phonon_weights, source, weight_index)
-    block = (width, width)
-    face = (faces, 2 * faces)
-    ham, coup = hamiltonian[0], coupling[0]
-    (sent,) = call(first_kernel, [face], [energies], ham, profile, sig, coup, left_face, right_face)
+    block, face = (width, width), (faces, 2 * faces)
+    own, from_x, far, from_1, from_2 = exchange(green_prev, phonon_weights, source, weight_index)
+    face_sent, base = call(
+        first_kernel, [face, (2, *block)], [energies, source, weight_index, phonon_weights],
+        hamiltonian, profile, own, from_x, far, from_1, from_2, coupling, left_face, right_face,
+    )
     for turn in range(1, slab_count):
-        incoming = passed_along(sent, "slab", 1)
-        sent, message, e, q, a, scale = call(
+        incoming = passed_along(face_sent, 1)
+        face_sent, message, e, q, a, scale = call(
             next_kernel,
             [face, face, (DOUBLINGS, *block), (DOUBLINGS, *block), (2, *block)],
-            [energies, first],
-            ham, profile, sig, coup, left_face, right_face, incoming,
+            [], base, coupling, left_face, right_face, incoming,
             scalar_outs=[(1,)],
         )
-    incoming = passed_along(message, "slab", -1)
+    incoming = passed_along(message, -1)
     for turn in range(2, slab_count):
-        (message,) = call(message_kernel, [face], [], sent, incoming, coup, left_face, right_face, ham)
-        incoming = passed_along(message, "slab", -1)
+        (message,) = call(message_kernel, [face], [], face_sent, incoming, coupling, left_face, right_face, base)
+        incoming = passed_along(message, -1)
     g, cols, rows = call(
         full_kernel, [(2, *block), (2 * width, faces), (faces, 2 * width)], [scale], e, q, a, right_face
     )

time: 110 us -> 61.6 us (0.56)
  the two profiles are of different devices: /device:TPU:28 before, /device:TPU:12 now
where the time goes in v2:
time: 61.6 us; the launch traced here: 61.3 us
  starting transfers between devices  20.9 us (34%)
  waiting for transfers between devices  18.4 us (30%)
  Pallas kernels  18.1 us (29%)
  local copies, waits for them, and re-layouts  3.04 us (5%)
  between operations  0.86 us (1%)
    pallas_call x7, Pallas kernels, call(): pl.pallas_call(kernel, out_shape=[jax.ShapeDtypeStruct(shape, f32) for sh...  18.1 us
    ppermute x12, starting transfers between devices, sent(): return lax.ppermute(value, 'energy', pairs)  18 us
    ppermute x12, waiting for transfers between devices, sent(): return lax.ppermute(value, 'energy', pairs)  13.8 us
    ppermute x2, waiting for transfers between devices, passed_along(): lax.ppermute(value, 'slab', [(start, start + steps) for start in range(in...  4.51 us
    unnamed x20, local copies, waits for them, and re-layouts  3.04 us
    ppermute x2, starting transfers between devices, passed_along(): lax.ppermute(value, 'slab', [(start, start + steps) for start in range(in...  2.9 us
  transfers between devices with their start and end apart: 14, of which 8 were waited for; matrix products, arithmetic and copies ran while one was open for 0% of the time, Pallas kernels for 9%

profile of v2, /device:TPU:12, one launch (start us, length us, event | category | flops | bytes accessed | tf_op | source)
XLA Modules:
  0.0 61.3 jit_solution(4410566677407485325)
XLA Ops:
  0.0 1.0 %copy-done = f32[1,1,2,256,256]{4,3,2,1,0:T(8,128)S(1)} copy-done((f32[1,1,2,256,256]{4,3,2,1,0:T(8,128)S(1)}, f32[1,1,2,256,256]{4,3,2,1,0:T(8,128)}, u32[]{:S(2)}) %copy-start) | copy-done | bytes 524312
  1.0 0.7 %copy-done.5 = s32[1,2]{1,0:T(1,128)S(1)} copy-done((s32[1,2]{1,0:T(1,128)S(1)}, s32[1,2]{1,0:T(1,128)}, u32[]{:S(2)}) %copy-start.5) | copy-done | bytes 32
  1.7 0.7 %copy-done.6 = s32[1,2]{1,0:T(1,128)S(1)} copy-done((s32[1,2]{1,0:T(1,128)S(1)}, s32[1,2]{1,0:T(1,128)}, u32[]{:S(2)}) %copy-start.6) | copy-done | bytes 32
  2.4 0.7 %copy-done.7 = f32[8]{0:T(128)S(1)} copy-done((f32[8]{0:T(128)S(1)}, f32[8]{0:T(128)}, u32[]{:S(2)}) %copy-start.7) | copy-done | bytes 56
  3.6 2.4 %collective-permute-start.2 = (f32[264,256]{1,0:T(8,128)S(1)}, f32[264,256]{1,0:T(8,128)S(1)}, u32[]{:S(2)}, u32[]{:S(2)}) collective-permute-start(f32[264,256]{1,0:T(8,128)S(1)} %get-tuple-element.20), channel_id=1, source_target_pairs={{2,10},{6,14},{8,0},{10,18},{12,4},{14,22},{16,8},{18,26},{20,12},... | collective-permute-start | bytes 811016 | tf_op jit(solution)/shard_map/ppermute | solution.py:157
  6.0 3.5 %collective-permute-start.1 = (f32[264,256]{1,0:T(8,128)S(1)}, f32[264,256]{1,0:T(8,128)S(1)}, u32[]{:S(2)}, u32[]{:S(2)}) collective-permute-start(f32[264,256]{1,0:T(8,128)S(1)} %get-tuple-element.20), channel_id=1, source_target_pairs={{0,8},{4,12},{8,16},{10,2},{12,20},{14,6},{16,24},{18,10},{20,28},... | collective-permute-start | bytes 811016 | tf_op jit(solution)/shard_map/ppermute | solution.py:157
  9.5 1.6 %collective-permute-start.5 = (f32[264,256]{1,0:T(8,128)S(1)}, f32[264,256]{1,0:T(8,128)S(1)}, u32[]{:S(2)}, u32[]{:S(2)}) collective-permute-start(f32[264,256]{1,0:T(8,128)S(1)} %get-tuple-element.21), channel_id=1, source_target_pairs={{0,4},{2,6},{4,0},{6,2},{8,12},{10,14},{12,8},{14,10},{16,20},{18,... | collective-permute-start | bytes 811016 | tf_op jit(solution)/shard_map/ppermute | solution.py:157
  11.0 1.3 %collective-permute-start.7 = (f32[264,256]{1,0:T(8,128)S(1)}, f32[264,256]{1,0:T(8,128)S(1)}, u32[]{:S(2)}, u32[]{:S(2)}) collective-permute-start(f32[264,256]{1,0:T(8,128)S(1)} %get-tuple-element.21), channel_id=1, source_target_pairs={{16,14},{24,22},{6,8},{14,16},{17,15},{25,23},{7,9},{15,17}} | collective-permute-start | bytes 811016 | tf_op jit(solution)/shard_map/ppermute | solution.py:157
  12.7 1.6 %collective-permute-done.1.one = f32[264,256]{1,0:T(8,128)S(1)} collective-permute-done((f32[264,256]{1,0:T(8,128)S(1)}, f32[264,256]{1,0:T(8,128)S(1)}, u32[]{:S(2)}, u32[]{:S(2)}) %collective-permute-start.1) | collective-permute-done | bytes 270368 | tf_op jit(solution)/shard_map/ppermute | solution.py:157
  15.0 5.1 %collective-permute-done.5.x = f32[264,256]{1,0:T(8,128)S(1)} collective-permute-done((f32[264,256]{1,0:T(8,128)S(1)}, f32[264,256]{1,0:T(8,128)S(1)}, u32[]{:S(2)}, u32[]{:S(2)}) %collective-permute-start.5) | collective-permute-done | bytes 270368 | tf_op jit(solution)/shard_map/ppermute | solution.py:157
  20.1 1.3 %collective-permute-start.9 = (f32[264,256]{1,0:T(8,128)S(1)}, f32[264,256]{1,0:T(8,128)S(1)}, u32[]{:S(2)}, u32[]{:S(2)}) collective-permute-start(f32[264,256]{1,0:T(8,128)S(1)} %collective-permute-done.2.two), channel_id=1, source_target_pairs={{8,6},{14,16},{16,14},{22,24},{9,7},{15,17},{17,15},{23,25}} | collective-permute-start | bytes 811016 | tf_op jit(solution)/shard_map/ppermute | solution.py:157
  22.0 5.4 %collective-permute-start.10 = (f32[256,256]{1,0:T(8,128)S(1)}, f32[256,256]{1,0:T(8,128)S(1)}, u32[]{:S(2)}, u32[]{:S(2)}) collective-permute-start(f32[256,256]{1,0:T(8,128)S(1)} %get-tuple-element.23), channel_id=1, source_target_pairs={{0,8},{4,12},{8,16},{10,2},{12,20},{14,6},{16,24},{18,10},{20,28},... | collective-permute-start | bytes 786440 | tf_op jit(solution)/shard_map/ppermute | solution.py:157
  27.4 1.9 %collective-permute-start.11 = (f32[256,256]{1,0:T(8,128)S(1)}, f32[256,256]{1,0:T(8,128)S(1)}, u32[]{:S(2)}, u32[]{:S(2)}) collective-permute-start(f32[256,256]{1,0:T(8,128)S(1)} %get-tuple-element.24), channel_id=1, source_target_pairs={{2,10},{6,14},{8,0},{10,18},{12,4},{14,22},{16,8},{18,26},{20,12},... | collective-permute-start | bytes 786440 | tf_op jit(solution)/shard_map/ppermute | solution.py:157
  30.1 0.8 %shard_map.101.own = f32[2,256,256]{2,1,0:T(8,128)S(1)} custom-call(s32[1,2]{1,0:T(1,128)S(1)} %copy-done.5, s32[1,2]{1,0:T(1,128)S(1)} %copy-done.6, f32[8]{0:T(128)S(1)} %copy-done.7, f32[1,1,2,256,256]{4,3,2,1,0:T(8,128)S(1)} %copy-done.1, f32[1,1,2,256,256]{4,3,2,1,0:T(8,128)S(1)} %collective-permute-done.pair, ...), custom_call_target="tpu_custom_call" | custom-call | tf_op jit(solution)/shard_map/pallas_call | solution.py:334
  30.9 2.5 %collective-permute-done.10.over_1 = f32[256,256]{1,0:T(8,128)S(1)} collective-permute-done((f32[256,256]{1,0:T(8,128)S(1)}, f32[256,256]{1,0:T(8,128)S(1)}, u32[]{:S(2)}, u32[]{:S(2)}) %collective-permute-start.10) | collective-permute-done | bytes 262176 | tf_op jit(solution)/shard_map/ppermute | solution.py:157
  33.4 2.2 %collective-permute-done.11.over_2 = f32[256,256]{1,0:T(8,128)S(1)} collective-permute-done((f32[256,256]{1,0:T(8,128)S(1)}, f32[256,256]{1,0:T(8,128)S(1)}, u32[]{:S(2)}, u32[]{:S(2)}) %collective-permute-start.11) | collective-permute-done | bytes 262176 | tf_op jit(solution)/shard_map/ppermute | solution.py:157
  35.7 1.7 %collective-permute-done.8.over_x = f32[256,256]{1,0:T(8,128)S(1)} collective-permute-done((f32[256,256]{1,0:T(8,128)S(1)}, f32[256,256]{1,0:T(8,128)S(1)}, u32[]{:S(2)}, u32[]{:S(2)}) %collective-permute-start.8) | collective-permute-done | bytes 262176 | tf_op jit(solution)/shard_map/ppermute | solution.py:157
  37.4 5.2 %shard_map.103 = (f32[64,128]{1,0:T(8,128)S(1)}, f32[2,256,256]{2,1,0:T(8,128)S(1)}) custom-call(f32[1]{0:T(128)S(6)} %copy.11.energy, s32[1,2]{1,0:T(1,128)S(1)} %copy-done.5, s32[1,2]{1,0:T(1,128)S(1)} %copy-done.6, f32[8]{0:T(128)S(1)} %copy-done.7, f32[1,256,256]{2,1,0:T(8,128)S(1)} %copy-done.2, f32[256,256]{1,0:T(8,128)S(1)} %copy-done.3, ...), custom_call_target="tpu_custom_call" | custom-call | tf_op jit(solution)/shard_map/pallas_call | solution.py:334
  42.6 1.3 %collective-permute-start.12 = (f32[64,128]{1,0:T(8,128)S(1)}, f32[64,128]{1,0:T(8,128)S(1)}, u32[]{:S(2)}, u32[]{:S(2)}) collective-permute-start(f32[64,128]{1,0:T(8,128)S(1)} %get-tuple-element.26), channel_id=1, source_target_pairs={{0,1},{2,3},{4,5},{6,7},{8,9},{10,11},{12,13},{14,15},{16,17},{18,... | collective-permute-start | bytes 98312 | tf_op jit(solution)/shard_map/ppermute | solution.py:376
  43.9 4.5 %collective-permute-done.12.incoming = f32[64,128]{1,0:T(8,128)S(1)} collective-permute-done((f32[64,128]{1,0:T(8,128)S(1)}, f32[64,128]{1,0:T(8,128)S(1)}, u32[]{:S(2)}, u32[]{:S(2)}) %collective-permute-start.12) | collective-permute-done | bytes 32800 | tf_op jit(solution)/shard_map/ppermute | solution.py:376
  48.4 5.4 %shard_map.104 = (f32[64,128]{1,0:T(8,128)}, f32[64,128]{1,0:T(8,128)S(1)}, f32[4,256,256]{2,1,0:T(8,128)S(1)}, f32[4,256,256]{2,1,0:T(8,128)S(1)}, f32[2,256,256]{2,1,0:T(8,128)S(1)}, /*index=5*/f32[1]{0:T(128)}) custom-call(f32[2,256,256]{2,1,0:T(8,128)S(1)} %get-tuple-element.25.base, f32[1,64,64]{2,1,0:T(8,128)S(1)} %copy-done.4, s32[1,64]{1,0:T(1,128)S(1)} %copy-done.9, ...), custom_call_target="tpu_custom_call" | custom-call | tf_op jit(solution)/shard_map/pallas_call | solution.py:334
  53.9 1.6 %collective-permute-start.13 = (f32[64,128]{1,0:T(8,128)S(1)}, f32[64,128]{1,0:T(8,128)S(1)}, u32[]{:S(2)}, u32[]{:S(2)}) collective-permute-start(f32[64,128]{1,0:T(8,128)S(1)} %get-tuple-element.34), channel_id=1, source_target_pairs={{1,0},{3,2},{5,4},{7,6},{9,8},{11,10},{13,12},{15,14},{17,16},{19,... | collective-permute-start | bytes 98312 | tf_op jit(solution)/shard_map/ppermute | solution.py:376
  55.5 4.4 %shard_map.105 = (f32[2,256,256]{2,1,0:T(8,128)S(1)}, f32[512,64]{1,0:T(8,128)S(1)}, f32[64,512]{1,0:T(8,128)S(1)}) custom-call(f32[1]{0:T(128)} %get-tuple-element.27.scale, f32[4,256,256]{2,1,0:T(8,128)S(1)} %get-tuple-element.28.e_in, f32[4,256,256]{2,1,0:T(8,128)S(1)} %get-tuple-element.29.q_in, f32[2,256,256]{2,1,0:T(8,128)S(1)} %get-tuple-element.30.a_in, ...), custom_call_target="tpu_custom_call" | custom-call | tf_op jit(solution)/shard_map/pallas_call | solution.py:334
  59.9 1.4 %shard_map.106 = f32[1,1,2,256,256]{4,3,2,1,0:T(8,128)} custom-call(f32[2,256,256]{2,1,0:T(8,128)S(1)} %get-tuple-element.31.g, f32[512,64]{1,0:T(8,128)S(1)} %get-tuple-element.32.cols, f32[64,512]{1,0:T(8,128)S(1)} %get-tuple-element.33.rows, f32[64,128]{1,0:T(8,128)S(1)} %collective-permute-done.13.message), custom_call_target="tpu_custom_call" | custom-call | tf_op jit(solution)/shard_map/pallas_call | solution.py:334
  (31 shorter events, 2.3 us)
Async XLA Ops:
  0.0 1.0 %copy-start = (f32[1,1,2,256,256]{4,3,2,1,0:T(8,128)S(1)}, f32[1,1,2,256,256]{4,3,2,1,0:T(8,128)}, u32[]{:S(2)}) copy-start(f32[1,1,2,256,256]{4,3,2,1,0:T(8,128)} %mine.3) | copy-start | bytes 1572868
  1.0 0.7 %copy-start.5 = (s32[1,2]{1,0:T(1,128)S(1)}, s32[1,2]{1,0:T(1,128)}, u32[]{:S(2)}) copy-start(s32[1,2]{1,0:T(1,128)} %source.5) | copy-start | bytes 28
  1.7 0.7 %copy-start.6 = (s32[1,2]{1,0:T(1,128)S(1)}, s32[1,2]{1,0:T(1,128)}, u32[]{:S(2)}) copy-start(s32[1,2]{1,0:T(1,128)} %weight_index.5) | copy-start | bytes 28
  2.4 0.7 %copy-start.7 = (f32[8]{0:T(128)S(1)}, f32[8]{0:T(128)}, u32[]{:S(2)}) copy-start(f32[8]{0:T(128)} %table.5) | copy-start | bytes 100
  3.0 18.6 %copy-start.1 = (f32[1,1,2,256,256]{4,3,2,1,0:T(8,128)S(1)}, f32[1,1,2,256,256]{4,3,2,1,0:T(8,128)}, u32[]{:S(2)}) copy-start(f32[1,1,2,256,256]{4,3,2,1,0:T(8,128)} %mine.3) | copy-start | bytes 1572868
  3.6 9.1 %collective-permute-start.2 = (f32[264,256]{1,0:T(8,128)S(1)}, f32[264,256]{1,0:T(8,128)S(1)}, u32[]{:S(2)}, u32[]{:S(2)}) collective-permute-start(f32[264,256]{1,0:T(8,128)S(1)} %get-tuple-element.20), channel_id=1, source_target_pairs={{2,10},{6,14},{8,0},{10,18},{12,4},{14,22},{16,8},{18,26},{20,12},... | collective-permute-start | bytes 811016 | tf_op jit(solution)/shard_map/ppermute | solution.py:157
  6.0 8.4 %collective-permute-start.1 = (f32[264,256]{1,0:T(8,128)S(1)}, f32[264,256]{1,0:T(8,128)S(1)}, u32[]{:S(2)}, u32[]{:S(2)}) collective-permute-start(f32[264,256]{1,0:T(8,128)S(1)} %get-tuple-element.20), channel_id=1, source_target_pairs={{0,8},{4,12},{8,16},{10,2},{12,20},{14,6},{16,24},{18,10},{20,28},... | collective-permute-start | bytes 811016 | tf_op jit(solution)/shard_map/ppermute | solution.py:157
  9.5 10.6 %collective-permute-start.5 = (f32[264,256]{1,0:T(8,128)S(1)}, f32[264,256]{1,0:T(8,128)S(1)}, u32[]{:S(2)}, u32[]{:S(2)}) collective-permute-start(f32[264,256]{1,0:T(8,128)S(1)} %get-tuple-element.21), channel_id=1, source_target_pairs={{0,4},{2,6},{4,0},{6,2},{8,12},{10,14},{12,8},{14,10},{16,20},{18,... | collective-permute-start | bytes 811016 | tf_op jit(solution)/shard_map/ppermute | solution.py:157
  11.0 10.4 %collective-permute-start = (f32[1,1,2,256,256]{4,3,2,1,0:T(8,128)S(1)}, f32[1,1,2,256,256]{4,3,2,1,0:T(8,128)S(1)}, u32[]{:S(2)}, u32[]{:S(2)}) collective-permute-start(f32[1,1,2,256,256]{4,3,2,1,0:T(8,128)S(1)} %copy-done), channel_id=1, source_target_pairs={{0,2},{2,0},{4,6},{6,4},{8,10},{10,8},{12,14},{14,12},{16,18},{18,... | collective-permute-start | bytes 1572872 | tf_op jit(solution)/shard_map/ppermute | solution.py:157
  11.0 9.1 %collective-permute-start.7 = (f32[264,256]{1,0:T(8,128)S(1)}, f32[264,256]{1,0:T(8,128)S(1)}, u32[]{:S(2)}, u32[]{:S(2)}) collective-permute-start(f32[264,256]{1,0:T(8,128)S(1)} %get-tuple-element.21), channel_id=1, source_target_pairs={{16,14},{24,22},{6,8},{14,16},{17,15},{25,23},{7,9},{15,17}} | collective-permute-start | bytes 811016 | tf_op jit(solution)/shard_map/ppermute | solution.py:157
  12.7 8.7 %collective-permute-start.4 = (f32[264,256]{1,0:T(8,128)S(1)}, f32[264,256]{1,0:T(8,128)S(1)}, u32[]{:S(2)}, u32[]{:S(2)}) collective-permute-start(f32[264,256]{1,0:T(8,128)S(1)} %collective-permute-done.2.two), channel_id=1, source_target_pairs={{0,2},{2,0},{4,6},{6,4},{8,10},{10,8},{12,14},{14,12},{16,18},{18,... | collective-permute-start | bytes 811016 | tf_op jit(solution)/shard_map/ppermute | solution.py:157
  14.3 7.1 %collective-permute-start.3 = (f32[264,256]{1,0:T(8,128)S(1)}, f32[264,256]{1,0:T(8,128)S(1)}, u32[]{:S(2)}, u32[]{:S(2)}) collective-permute-start(f32[264,256]{1,0:T(8,128)S(1)} %collective-permute-done.1.one), channel_id=1, source_target_pairs={{0,2},{2,0},{4,6},{6,4},{8,10},{10,8},{12,14},{14,12},{16,18},{18,... | collective-permute-start | bytes 811016 | tf_op jit(solution)/shard_map/ppermute | solution.py:157
  20.1 1.5 %collective-permute-start.6 = (f32[264,256]{1,0:T(8,128)S(1)}, f32[264,256]{1,0:T(8,128)S(1)}, u32[]{:S(2)}, u32[]{:S(2)}) collective-permute-start(f32[264,256]{1,0:T(8,128)S(1)} %collective-permute-done.5.x), channel_id=1, source_target_pairs={{0,2},{2,0},{4,6},{6,4},{8,10},{10,8},{12,14},{14,12},{16,18},{18,... | collective-permute-start | bytes 811016 | tf_op jit(solution)/shard_map/ppermute | solution.py:157
  20.1 10.8 %collective-permute-start.9 = (f32[264,256]{1,0:T(8,128)S(1)}, f32[264,256]{1,0:T(8,128)S(1)}, u32[]{:S(2)}, u32[]{:S(2)}) collective-permute-start(f32[264,256]{1,0:T(8,128)S(1)} %collective-permute-done.2.two), channel_id=1, source_target_pairs={{8,6},{14,16},{16,14},{22,24},{9,7},{15,17},{17,15},{23,25}} | collective-permute-start | bytes 811016 | tf_op jit(solution)/shard_map/ppermute | solution.py:157
  22.0 11.4 %collective-permute-start.10 = (f32[256,256]{1,0:T(8,128)S(1)}, f32[256,256]{1,0:T(8,128)S(1)}, u32[]{:S(2)}, u32[]{:S(2)}) collective-permute-start(f32[256,256]{1,0:T(8,128)S(1)} %get-tuple-element.23), channel_id=1, source_target_pairs={{0,8},{4,12},{8,16},{10,2},{12,20},{14,6},{16,24},{18,10},{20,28},... | collective-permute-start | bytes 786440 | tf_op jit(solution)/shard_map/ppermute | solution.py:157
  27.4 8.3 %collective-permute-start.11 = (f32[256,256]{1,0:T(8,128)S(1)}, f32[256,256]{1,0:T(8,128)S(1)}, u32[]{:S(2)}, u32[]{:S(2)}) collective-permute-start(f32[256,256]{1,0:T(8,128)S(1)} %get-tuple-element.24), channel_id=1, source_target_pairs={{2,10},{6,14},{8,0},{10,18},{12,4},{14,22},{16,8},{18,26},{20,12},... | collective-permute-start | bytes 786440 | tf_op jit(solution)/shard_map/ppermute | solution.py:157
  29.3 8.1 %collective-permute-start.8 = (f32[256,256]{1,0:T(8,128)S(1)}, f32[256,256]{1,0:T(8,128)S(1)}, u32[]{:S(2)}, u32[]{:S(2)}) collective-permute-start(f32[256,256]{1,0:T(8,128)S(1)} %get-tuple-element.22), channel_id=1, source_target_pairs={{0,4},{2,6},{4,0},{6,2},{8,12},{10,14},{12,8},{14,10},{16,20},{18,... | collective-permute-start | bytes 786440 | tf_op jit(solution)/shard_map/ppermute | solution.py:157
  30.1 7.3 %copy-start.2 = (f32[1,256,256]{2,1,0:T(8,128)S(1)}, f32[1,256,256]{2,1,0:T(8,128)}, u32[]{:S(2)}) copy-start(f32[1,256,256]{2,1,0:T(8,128)} %ham.1) | copy-start | bytes 786436
  30.1 7.3 %copy-start.3 = (f32[256,256]{1,0:T(8,128)S(1)}, f32[256,256]{1,0:T(8,128)}, u32[]{:S(2)}) copy-start(f32[256,256]{1,0:T(8,128)} %profile.1) | copy-start | bytes 786436
  30.1 7.3 %copy-start.4 = (f32[1,64,64]{2,1,0:T(8,128)S(1)}, f32[1,64,64]{2,1,0:T(8,128)}, u32[]{:S(2)}) copy-start(f32[1,64,64]{2,1,0:T(8,128)} %coup.3) | copy-start | bytes 49156
  30.1 7.3 %copy-start.8 = (s32[1,64]{1,0:T(1,128)S(1)}, s32[1,64]{1,0:T(1,128)}, u32[]{:S(2)}) copy-start(s32[1,64]{1,0:T(1,128)} %right.5) | copy-start | bytes 772
  30.1 7.3 %copy-start.9 = (s32[1,64]{1,0:T(1,128)S(1)}, s32[1,64]{1,0:T(1,128)}, u32[]{:S(2)}) copy-start(s32[1,64]{1,0:T(1,128)} %left.3) | copy-start | bytes 772
  42.6 5.8 %collective-permute-start.12 = (f32[64,128]{1,0:T(8,128)S(1)}, f32[64,128]{1,0:T(8,128)S(1)}, u32[]{:S(2)}, u32[]{:S(2)}) collective-permute-start(f32[64,128]{1,0:T(8,128)S(1)} %get-tuple-element.26), channel_id=1, source_target_pairs={{0,1},{2,3},{4,5},{6,7},{8,9},{10,11},{12,13},{14,15},{16,17},{18,... | collective-permute-start | bytes 98312 | tf_op jit(solution)/shard_map/ppermute | solution.py:376
  53.9 6.0 %collective-permute-start.13 = (f32[64,128]{1,0:T(8,128)S(1)}, f32[64,128]{1,0:T(8,128)S(1)}, u32[]{:S(2)}, u32[]{:S(2)}) collective-permute-start(f32[64,128]{1,0:T(8,128)S(1)} %get-tuple-element.34), channel_id=1, source_target_pairs={{1,0},{3,2},{5,4},{7,6},{9,8},{11,10},{13,12},{15,14},{17,16},{19,... | collective-permute-start | bytes 98312 | tf_op jit(solution)/shard_map/ppermute | solution.py:376

commit v3 on v2

v3 whole, which is shorter than its diff:
```python
import functools

import jax
import jax.numpy as jnp
from jax import lax
from jax.experimental import pallas as pl
from jax.experimental.pallas import tpu as pltpu
from jax.sharding import PartitionSpec as P

SPAN = 5
BROAD = 0.02
DOUBLINGS = 4

f32 = jnp.float32
bf16 = jnp.bfloat16
NN = (((1,), (0,)), ((), ()))
NT = (((1,), (1,)), ((), ()))
TN = (((0,), (0,)), ((), ()))


def split(x):
    high = x.astype(bf16)
    return high, (x - high.astype(f32)).astype(bf16)


def mm(a, b, dims=NN):
    return lax.dot_general(a, b, dims, preferred_element_type=f32)


def left3(*terms):
    out = []
    for x in terms:
        high, low = split(x)
        out += [high, high, low]
    return jnp.concatenate(out, axis=1)


def right3(*terms, axis=0):
    out = []
    for x in terms:
        high, low = split(x)
        out += [high, low, high]
    return jnp.concatenate(out, axis=axis)


def pair(x, axis):
    return jnp.concatenate(split(x), axis=axis)


def twice(x, axis):
    return jnp.concatenate([x, x], axis=axis)


def both(x_re, x_im):
    return jnp.concatenate([x_re, x_im], axis=0)


def skew(e):
    return 0.5 * (e - e.T)


def stack(*parts):
    return jnp.concatenate(parts, axis=0)


def left_of(high, low):
    return jnp.concatenate([high, high, low], axis=1)


def right_of(high, low):
    return jnp.concatenate([high, low, high], axis=0)


def herm(e, q):
    return split(e), split(q)


def times(s, h):
    return mm(left_of(*s[0]), right_of(*h[0])) - 2.0 * mm(left_of(*s[1]), right_of(*h[1]))


def rows_times(e_rows, q_rows, h):
    count = e_rows.shape[0]
    e_high, e_low = split(e_rows)
    q_high, q_low = split(q_rows)
    from_e = mm(stack(e_high, e_low), h[0][0])
    from_q = mm(stack(q_high, q_low), h[1][0])
    lows = mm(e_high, h[0][1]) + mm(q_high, h[1][1])
    return (from_e[:count] + from_e[count:]) + (from_q[:count] + from_q[count:]) + lows


def thin_times(y_re, y_im, h):
    out = rows_times(stack(y_re, y_im), stack(-(y_re + y_im), y_re - y_im), h)
    return out[:y_re.shape[0]], out[y_re.shape[0]:]


def complex_mm(a_re, a_im, b_re, b_im):
    rows = a_re.shape[0]
    out = mm(stack(left3(a_re, -a_im), left3(a_im, a_re)), right3(b_re, b_im))
    return out[:rows], out[rows:]


def one_hot(width, face):
    return (lax.broadcasted_iota(jnp.int32, (width, face.shape[1]), 0) == face).astype(bf16)


def unit_of(width):
    row = lax.broadcasted_iota(jnp.int32, (width, width), 0)
    return (row == lax.broadcasted_iota(jnp.int32, (width, width), 1)).astype(f32)


def begin(a_re, a_im):
    total = a_re + a_im
    gram = mm(left3(total), right3(total, axis=1), NT) - mm(left3(2.0 * a_re), right3(a_im, axis=1), NT)
    modulus = jnp.sqrt(a_re * a_re + a_im * a_im)
    col_norm = jnp.max(jnp.sum(modulus, axis=0))
    row_norm = jnp.max(jnp.sum(modulus, axis=1))
    scale = 1.0 / (col_norm * row_norm)
    return unit_of(a_re.shape[0]) - scale * gram, (-scale) * skew(gram), scale


def corner(a_re, a_im, proj, series=False):
    width, faces = proj.shape
    e, q, scale = begin(a_re, a_im)
    proj_t = proj.T
    y = scale * mm(left3(proj_t), right3(both(a_re, a_im), axis=1), NT)
    y_re, y_im = y[:, :width], -y[:, width:]
    s_e, s_q = unit_of(width) + e, q
    for turn in range(1, DOUBLINGS):
        h = herm(e, q)
        if series and turn > 1:
            s_e = s_e + times(herm(s_e, s_q), h)
            s_q = skew(s_e)
        e = times(h, h)
        q = skew(e)
        c_re, c_im = thin_times(y_re, y_im, h)
        y_re, y_im = y_re + c_re, y_im + c_im
    h = herm(e, q)
    c_re, c_im = thin_times(y_re, y_im, h)
    y_re, y_im = y_re + c_re, y_im + c_im
    none = jnp.zeros_like(proj_t)
    t_re, t_im = thin_times(proj_t, none, h)
    u_re, u_im = thin_times(y_re, y_im, h)
    out = mm(left3(both(y_re, y_im)), right3(proj))
    out += mm(stack(left3(u_re, u_im), left3(u_im, -u_re)), right3(t_re, t_im, axis=1), NT)
    return out[:faces], out[faces:], (s_e, s_q, e, q), scale


def series_of(e, q):
    s_e, s_q = unit_of(e.shape[0]) + e, q
    for turn in range(1, DOUBLINGS):
        h = herm(e, q)
        if turn > 1:
            s_e = s_e + times(herm(s_e, s_q), h)
            s_q = skew(s_e)
        e = times(h, h)
        q = skew(e)
    return s_e, s_q, e, q


def full(a_re, a_im, s_e, s_q, e, q, scale):
    h = herm(e, q)
    s_e = s_e + times(herm(s_e, s_q), h)
    e = times(h, h)
    s_e = s_e + times(herm(s_e, skew(s_e)), herm(e, skew(e)))
    s_q = skew(s_e)
    s_p = s_e - s_q
    b, c = a_re.T, a_im.T
    one = mm(left3(b - c), right3(s_p))
    g_re = one + mm(left3(c), right3(s_e))
    g_im = one + mm(left3(b), right3(s_q - s_p))
    return scale * g_re, scale * g_im


ROWS = 8


def over_x(e):
    return e ^ 2


def twin(e):
    return e ^ 1


def group_1(e):
    return e + 4 if e % 2 == 0 else e - 4


def group_2(e):
    return e - 4 if e % 2 == 0 else e + 4


def sent(value, pairs):
    return lax.ppermute(value, "energy", pairs)


def pairs_of(target, count):
    return [(e, target(e)) for e in range(count) if 0 <= target(e) < count]


def pack_kernel(energy_hbm, source_hbm, index_hbm, table_hbm, green, im_out, re_out, energy, source, index, table, sems):
    width = green.shape[3]
    copies = [
        pltpu.make_async_copy(start, end, sems.at[k])
        for k, (start, end) in enumerate((
            (energy_hbm, energy), (source_hbm, source), (index_hbm, index), (table_hbm, table),
            (green.at[0, 0, 1], im_out.at[pl.ds(0, width)]), (green.at[0, 0, 0], re_out.at[pl.ds(0, width)]),
        ))
    ]
    for copy in copies:
        copy.start()
    for copy in copies[:4]:
        copy.wait()
    row = lax.broadcasted_iota(jnp.int32, (ROWS, width), 0)
    rows = jnp.where(row == 4, energy[0], 0.0)
    for term in range(2):
        rows = jnp.where(row == term, source[0, term].astype(f32), rows)
        rows = jnp.where(row == 2 + term, table[index[0, term]], rows)
    im_out[width:] = rows
    re_out[width:] = rows
    for copy in copies[4:]:
        copy.wait()


def pack(green_prev, energies, source, weight_index, table):
    width = green_prev.shape[-1]
    hbm, vmem = pl.BlockSpec(memory_space=pltpu.HBM), pl.BlockSpec(memory_space=pltpu.VMEM)
    return pl.pallas_call(
        pack_kernel,
        out_shape=[jax.ShapeDtypeStruct((width + ROWS, width), f32)] * 2,
        in_specs=[hbm] * 5,
        out_specs=[vmem] * 2,
        scratch_shapes=[
            pltpu.SMEM(energies.shape, f32), pltpu.SMEM(source.shape, jnp.int32),
            pltpu.SMEM(weight_index.shape, jnp.int32), pltpu.SMEM(table.shape, f32),
            pltpu.SemaphoreType.DMA((6,)),
        ],
        compiler_params=pltpu.CompilerParams(vmem_limit_bytes=40 * 2**20),
    )(energies, source, weight_index, table, green_prev)


def coef(rows, index):
    at = index.astype(f32)
    return jnp.where(rows[0:1] == at, rows[2:3], 0.0) + jnp.where(rows[1:2] == at, rows[3:4], 0.0)


def held(e):
    step = jnp.where(e % 2 == 0, 4, -4)
    other = e + 1 - 2 * (e % 2)
    return other, e - step, e + step, other + step, other - step


def over_x_kernel(re, twin_block, one, two, pair_one, pair_two, x, out):
    width = re.shape[1]
    e = lax.axis_index("energy")
    other, at_one, at_two, at_pair_one, at_pair_two = held(e)
    rows = x[width:]
    total = coef(rows, e) * re[:width] + coef(rows, other) * twin_block[0, 0, 0]
    total += coef(rows, at_one) * one[:width] + coef(rows, at_two) * two[:width]
    out[...] = total + coef(rows, at_pair_one) * pair_one[:width] + coef(rows, at_pair_two) * pair_two[:width]


def groups_kernel(im, twin_block, x, pair_x, near, one, two, out_1, out_2):
    width = im.shape[1]
    e = lax.axis_index("energy")
    other, at_one, at_two, _, _ = held(e)
    across = e + 2 - 4 * ((e // 2) % 2)
    pair_across = other + 2 - 4 * ((other // 2) % 2)
    for target, rows, out in ((at_two, two[width:], out_1), (at_one, one[width:], out_2)):
        upward = target > e
        near_index = jnp.where(upward, e - 1, e + 1)
        counts = e % 4 == jnp.where(upward, 0, 3)
        total = coef(rows, e) * im[:width] + coef(rows, other) * twin_block[0, 0, 1]
        total += coef(rows, across) * x[:width] + coef(rows, pair_across) * pair_x[:width]
        out[...] = total + jnp.where(counts, coef(rows, near_index), 0.0) * near[:width]


def own_kernel(re, im, twin_block, one, two, pair_one, pair_two, x, pair_x, ham, profile, coup, left, base_out, placed_out):
    width = re.shape[1]
    e = lax.axis_index("energy")
    other, at_one, at_two, at_pair_one, at_pair_two = held(e)
    across = e + 2 - 4 * ((e // 2) % 2)
    pair_across = other + 2 - 4 * ((other // 2) % 2)
    rows = re[width:]
    total = coef(rows, e) * re[:width] + coef(rows, other) * twin_block[0, 0, 0]
    total += coef(rows, at_one) * one[:width] + coef(rows, at_two) * two[:width]
    total += coef(rows, at_pair_one) * pair_one[:width] + coef(rows, at_pair_two) * pair_two[:width]
    unit = unit_of(width)
    base_out[0] = rows[4:5] * unit - ham[0] - profile[...] * total
    total = coef(rows, e) * im[:width] + coef(rows, other) * twin_block[0, 0, 1]
    total += coef(rows, across) * x[:width] + coef(rows, pair_across) * pair_x[:width]
    placed = mm(twice(one_hot(width, left[...]), 1), pair(coup[0], 1), NT)
    placed_out[...] = placed
    lead = jnp.where(lax.axis_index("slab") == 0, -0.5, 0.0) * mm(left3(placed), right3(placed, axis=1), NT)
    base_out[1] = BROAD * unit - profile[...] * total - lead


def first_kernel(own, re, profile, from_x, far, from_1, from_2, right, face_out, base_out):
    width, faces = profile.shape[0], right.shape[1]
    e = lax.axis_index("energy")
    weight = coef(re[width:], jnp.where(e % 4 == 3, e + SPAN, e - SPAN))
    base_re = own[0] - profile[...] * (from_x[...] + weight * far[:width])
    base_im = own[1] - profile[...] * (from_1[...] + from_2[...])
    base_out[0] = base_re
    base_out[1] = base_im

    @pl.when(lax.axis_index("slab") == 0)
    def _():
        f_re, f_im, _, _ = corner(base_re, base_im, one_hot(width, right[...]).astype(f32))
        face_out[:, :faces] = f_re
        face_out[:, faces:] = f_im


def bounded(base, placed, incoming):
    width, faces = placed.shape
    is_first = lax.axis_index("slab") == 0
    face = jnp.where(is_first, 0.0, incoming[...])
    split_placed = left3(placed[...])
    t = mm(split_placed, right3(face))
    bound = mm(stack(left3(t[:, :faces]), left3(t[:, faces:])), right3(placed[...], axis=1), NT)
    return base[0] - bound[:width], base[1] - bound[width:]


def face_kernel(base, placed, incoming, right, face_out):
    width, faces = placed.shape
    a_re, a_im = bounded(base, placed, incoming)
    f_re, f_im, _, _ = corner(a_re, a_im, one_hot(width, right[...]).astype(f32))
    face_out[:, :faces] = f_re
    face_out[:, faces:] = f_im


def face_parts(g_re, g_im, right, cols_out, rows_out):
    width = g_re.shape[0]
    hot = one_hot(width, right[...])
    high, low = split(both(g_re, g_im))
    cols_out[...] = mm(jnp.concatenate([high, low], axis=1), twice(hot, 0))
    wide_high = jnp.concatenate([high[:width], high[width:]], axis=1)
    wide_low = jnp.concatenate([low[:width], low[width:]], axis=1)
    rows_out[...] = mm(twice(hot.T, 1), stack(wide_high, wide_low))


def whole(a_re, a_im, right, g_out, cols_out, rows_out):
    e, q, scale = begin(a_re, a_im)
    g_re, g_im = full(a_re, a_im, *series_of(e, q), scale)
    g_out[0] = g_re
    g_out[1] = g_im
    face_parts(g_re, g_im, right, cols_out, rows_out)


def slab_0_kernel(base, right, g_out, cols_out, rows_out):
    @pl.when(lax.axis_index("slab") == 0)
    def _():
        whole(base[0], base[1], right, g_out, cols_out, rows_out)


def middle_kernel(slabs, base, placed, incoming, right, g, cols, rows, g_out, cols_out, rows_out):
    slab = lax.axis_index("slab")

    @pl.when((slab != 0) & (slab != slabs - 1))
    def _():
        a_re, a_im = bounded(base, placed, incoming)
        whole(a_re, a_im, right, g_out, cols_out, rows_out)

    @pl.when((slab == 0) | (slab == slabs - 1))
    def _():
        g_out[...] = g[...]
        cols_out[...] = cols[...]
        rows_out[...] = rows[...]


def turn_kernel(slabs, base, placed, incoming, message_out, series_out, a_out, scale_out):
    @pl.when(lax.axis_index("slab") == slabs - 1)
    def _():
        width, faces = placed.shape
        a_re, a_im = bounded(base, placed, incoming)
        m_re, m_im, series, scale = corner(a_re, a_im, placed[...], series=True)
        message_out[:, :faces] = m_re
        message_out[:, faces:] = m_im
        for k, part in enumerate(series):
            series_out[k] = part
        a_out[0] = a_re
        a_out[1] = a_im
        scale_out[0] = scale


def message_kernel(slabs, cols, rows, message, coup, left, right, base, message_out):
    width, faces = base.shape[1], coup.shape[1]
    hot = one_hot(width, right[...])
    f = mm(twice(hot.T, 1), pair(cols[...].reshape(2 * width, faces)[:width], 0))
    f_im = mm(twice(hot.T, 1), pair(cols[width:], 0))
    order = mm(one_hot(width, left[...]), hot, TN).astype(bf16)
    mixed = mm(pair(coup[0], 1), twice(order, 0))
    t_re, t_im = complex_mm(f, f_im, message[:, :faces], message[:, faces:])
    c_re, c_im = complex_mm(t_re, t_im, f, f_im)
    t = mm(left3(both(f + c_re, f_im + c_im)), right3(mixed, axis=1), NT)
    wide = jnp.concatenate([t[:faces], t[faces:]], axis=1)
    is_last = lax.axis_index("slab") == slabs - 1

    @pl.when(jnp.logical_not(is_last))
    def _():
        message_out[...] = mm(left3(mixed), right3(wide))

    @pl.when(is_last)
    def _():
        message_out[...] = message[...]


def last_full_kernel(slabs, scale, series, a_in, green_out, block, sems):
    @pl.when(lax.axis_index("slab") == slabs - 1)
    def _():
        block[0], block[1] = full(a_in[0], a_in[1], *(series[k] for k in range(4)), scale[0])
        copies = [pltpu.make_async_copy(block.at[k], green_out.at[0, 0, k], sems.at[k]) for k in range(2)]
        for copy in copies:
            copy.start()
        for copy in copies:
            copy.wait()


def last_kernel(slabs, g, cols, rows, message, given, green_out, block, sems):
    @pl.when(lax.axis_index("slab") != slabs - 1)
    def _():
        width, faces = g.shape[1], message.shape[0]
        t_re, t_im = complex_mm(message[:, :faces], message[:, faces:], rows[:, :width], rows[:, width:])
        c_re, c_im = complex_mm(cols[:width], cols[width:], t_re, t_im)
        copies = []
        for k, change in enumerate((c_re, c_im)):
            block[k] = g[k] + change
            copies.append(pltpu.make_async_copy(block.at[k], green_out.at[0, 0, k], sems.at[k]))
            copies[k].start()
        for copy in copies:
            copy.wait()


def write_green(kernel, scalars, arrays, shape, given=None):
    smem, vmem, hbm = (pl.BlockSpec(memory_space=space) for space in (pltpu.SMEM, pltpu.VMEM, pltpu.HBM))
    more = [] if given is None else [given]
    inputs = len(scalars) + len(arrays)
    return pl.pallas_call(
        kernel,
        out_shape=jax.ShapeDtypeStruct(shape, f32),
        in_specs=[smem] * len(scalars) + [vmem] * len(arrays) + [hbm] * len(more),
        out_specs=hbm,
        scratch_shapes=[pltpu.VMEM(shape[2:], f32), pltpu.SemaphoreType.DMA((2,))],
        input_output_aliases={inputs: 0} if more else {},
        compiler_params=pltpu.CompilerParams(vmem_limit_bytes=40 * 2**20),
    )(*scalars, *arrays, *more)


def call(kernel, outs, scalars, *arrays, scalar_outs=()):
    smem = pl.BlockSpec(memory_space=pltpu.SMEM)
    vmem = pl.BlockSpec(memory_space=pltpu.VMEM)
    return pl.pallas_call(
        kernel,
        out_shape=[jax.ShapeDtypeStruct(shape, f32) for shape in (*outs, *scalar_outs)],
        in_specs=[smem] * len(scalars) + [vmem] * len(arrays),
        out_specs=[vmem] * len(outs) + [smem] * len(scalar_outs),
        compiler_params=pltpu.CompilerParams(vmem_limit_bytes=40 * 2**20),
    )(*scalars, *arrays)


def exchange(energies, hamiltonian, coupling, green_prev, profile, phonon_weights, source, weight_index, left_face):
    count = lax.axis_size("energy")
    width = green_prev.shape[-1]
    block = (width, width)
    all_twin, all_x = pairs_of(twin, count), pairs_of(over_x, count)
    all_1, all_2 = pairs_of(group_1, count), pairs_of(group_2, count)
    groups = count // 4
    near_pairs = [(4 * k, 4 * k - 1) for k in range(2, groups)] + [(4 * k + 3, 4 * k + 4) for k in range(groups - 2)]
    far_pairs = [p for k in range(1, groups - 1) for p in ((4 * k, 4 * k - 1), (4 * k + 3, 4 * k + 4))]
    pair = sent(green_prev, all_twin)
    im, re = pack(green_prev, energies, source, weight_index, phonon_weights)
    x = sent(im, all_x)
    one = sent(re, all_1)
    two = sent(re, all_2)
    near = sent(im, near_pairs)
    pair_one = sent(one, all_twin)
    pair_two = sent(two, all_twin)
    far = sent(two, far_pairs)
    pair_x = sent(x, all_twin)
    (over_x_sum,) = call(over_x_kernel, [block], [], re, pair, one, two, pair_one, pair_two, x)
    from_x = sent(over_x_sum, all_x)
    sum_1, sum_2 = call(
        groups_kernel, [block] * 2, [], im, pair, x, pair_x, near, one, two
    )
    from_1 = sent(sum_1, all_1)
    from_2 = sent(sum_2, all_2)
    own, placed = call(
        own_kernel, [(2, *block), (width, coupling.shape[1])], [],
        re, im, pair, one, two, pair_one, pair_two, x, pair_x, hamiltonian, profile, coupling, left_face,
    )
    return placed, (own, re, profile, from_x, far, from_1, from_2)


def passed_along(value, steps):
    count = lax.axis_size("slab")
    return lax.ppermute(value, "slab", [(start, (start + steps) % count) for start in range(count)])


def on_device(
    energies, hamiltonian, coupling, green_prev, profile, phonon_weights, source, weight_index, left_face, right_face,
):
    width, faces = hamiltonian.shape[1], coupling.shape[1]
    slabs = lax.axis_size("slab")
    block, face = (width, width), (faces, 2 * faces)
    parts_of_g = [(2, *block), (2 * width, faces), (faces, 2 * width)]
    placed, parts = exchange(
        energies, hamiltonian, coupling, green_prev, profile, phonon_weights, source, weight_index, left_face
    )
    face_sent, base = call(first_kernel, [face, (2, *block)], [], *parts, right_face)
    incoming = passed_along(face_sent, 1)
    for turn in range(1, slabs - 1):
        (face_sent,) = call(face_kernel, [face], [], base, placed, incoming, right_face)
        incoming = passed_along(face_sent, 1)
    g, cols, rows = call(slab_0_kernel, parts_of_g, [], base, right_face)
    placed, g = lax.optimization_barrier((placed, g))
    if slabs > 2:
        g, cols, rows = call(
            functools.partial(middle_kernel, slabs), parts_of_g, [], base, placed, incoming, right_face, g, cols, rows
        )
    message, series, a, scale = call(
        functools.partial(turn_kernel, slabs), [face, (4, *block), (2, *block)], [], base, placed, incoming,
        scalar_outs=[(1,)],
    )
    incoming = passed_along(message, -1)
    green = write_green(functools.partial(last_full_kernel, slabs), [scale], [series, a], green_prev.shape)
    for turn in range(2, slabs):
        (message,) = call(
            functools.partial(message_kernel, slabs), [face], [],
            cols, rows, incoming, coupling, left_face, right_face, base,
        )
        incoming = passed_along(message, -1)
    return write_green(functools.partial(last_kernel, slabs), [], [g, cols, rows, incoming], green_prev.shape, green)


def solution(mesh):
    in_specs = (
        P("energy"),
        P("slab", None, None),
        P("slab", None, None),
        P("energy", "slab", None, None, None),
        P(),
        P(),
        P("energy", None),
        P("energy", None),
        P("slab", None),
        P("slab", None),
    )
    out_specs = P("energy", "slab", None, None, None)
    return jax.shard_map(on_device, mesh=mesh, in_specs=in_specs, out_specs=out_specs, check_vma=False)
```

time: 61.6 us -> 50.6 us (0.82)
  the two profiles are of different devices: /device:TPU:12 before, /device:TPU:0 now
where the time goes in v3:
time: 50.6 us; the launch traced here: 50.3 us
  starting transfers between devices  26.3 us (52%)
  Pallas kernels  11.3 us (22%)
  waiting for transfers between devices  10.6 us (21%)
  local copies, waits for them, and re-layouts  1.08 us (2%)
  between operations  0.94 us (2%)
    ppermute x12, starting transfers between devices, sent(): return lax.ppermute(value, 'energy', pairs)  22.8 us
    ppermute x12, waiting for transfers between devices, sent(): return lax.ppermute(value, 'energy', pairs)  9.4 us
    pallas_call x6, Pallas kernels, call(): pl.pallas_call(kernel, out_shape=[jax.ShapeDtypeStruct(shape, f32) for sh...  8.74 us
    ppermute x2, starting transfers between devices, passed_along(): lax.ppermute(value, 'slab', [(start, (start + steps) % count) for start i...  3.5 us
    pallas_call x2, Pallas kernels, write_green(): pl.pallas_call(kernel, out_shape=jax.ShapeDtypeStruct(shape, f32), in_spe...  1.97 us
    ppermute x2, waiting for transfers between devices, passed_along(): lax.ppermute(value, 'slab', [(start, (start + steps) % count) for start i...  1.23 us
    unnamed x20, local copies, waits for them, and re-layouts  1.08 us
  transfers between devices with their start and end apart: 14, of which 7 were waited for; matrix products, arithmetic and copies ran while one was open for 0% of the time, Pallas kernels for 12%

profile of v3, /device:TPU:0, one launch (start us, length us, event | category | flops | bytes accessed | tf_op | source)
XLA Modules:
  0.0 50.3 jit_solution(6619152161327848019)
XLA Ops:
  0.7 1.0 %copy-done.1 = f32[1,1,2,256,256]{4,3,2,1,0:T(8,128)S(1)} copy-done((f32[1,1,2,256,256]{4,3,2,1,0:T(8,128)S(1)}, f32[1,1,2,256,256]{4,3,2,1,0:T(8,128)}, u32[]{:S(2)}) %copy-start.1) | copy-done | bytes 524312
  1.8 0.6 %shard_map.100 = (f32[264,256]{1,0:T(8,128)S(1)}, f32[264,256]{1,0:T(8,128)S(1)}) custom-call(f32[1]{0:T(128)S(6)} %copy.13.energy_hbm, s32[1,2]{1,0:T(1,128)S(1)} %copy-done.6, s32[1,2]{1,0:T(1,128)S(1)} %copy-done.7, f32[8]{0:T(128)S(1)} %copy-done.8, f32[1,1,2,256,256]{4,3,2,1,0:T(8,128)S(1)} %copy-done.1), custom_call_target="tpu_custom_call" | custom-call | tf_op jit(solution)/shard_map/pallas_call | solution.py:229
  2.4 1.3 %collective-permute-start.2 = (f32[264,256]{1,0:T(8,128)S(1)}, f32[264,256]{1,0:T(8,128)S(1)}, u32[]{:S(2)}, u32[]{:S(2)}) collective-permute-start(f32[264,256]{1,0:T(8,128)S(1)} %get-tuple-element.22.re), channel_id=1, source_target_pairs={{2,10},{6,14},{8,0},{10,18},{12,4},{14,22},{16,8},{18,26},{20,12},... | collective-permute-start | bytes 811016 | tf_op jit(solution)/shard_map/ppermute | solution.py:195
  3.7 5.6 %collective-permute-start.1 = (f32[264,256]{1,0:T(8,128)S(1)}, f32[264,256]{1,0:T(8,128)S(1)}, u32[]{:S(2)}, u32[]{:S(2)}) collective-permute-start(f32[264,256]{1,0:T(8,128)S(1)} %get-tuple-element.22.re), channel_id=1, source_target_pairs={{0,8},{4,12},{8,16},{10,2},{12,20},{14,6},{16,24},{18,10},{20,28},... | collective-permute-start | bytes 811016 | tf_op jit(solution)/shard_map/ppermute | solution.py:195
  9.3 2.0 %collective-permute-start.5 = (f32[264,256]{1,0:T(8,128)S(1)}, f32[264,256]{1,0:T(8,128)S(1)}, u32[]{:S(2)}, u32[]{:S(2)}) collective-permute-start(f32[264,256]{1,0:T(8,128)S(1)} %get-tuple-element.23.im), channel_id=1, source_target_pairs={{0,4},{2,6},{4,0},{6,2},{8,12},{10,14},{12,8},{14,10},{16,20},{18,... | collective-permute-start | bytes 811016 | tf_op jit(solution)/shard_map/ppermute | solution.py:195
  11.3 0.8 %collective-permute-done.2.two = f32[264,256]{1,0:T(8,128)S(1)} collective-permute-done((f32[264,256]{1,0:T(8,128)S(1)}, f32[264,256]{1,0:T(8,128)S(1)}, u32[]{:S(2)}, u32[]{:S(2)}) %collective-permute-start.2) | collective-permute-done | bytes 270368 | tf_op jit(solution)/shard_map/ppermute | solution.py:195
  12.1 1.2 %collective-permute-done.1.one = f32[264,256]{1,0:T(8,128)S(1)} collective-permute-done((f32[264,256]{1,0:T(8,128)S(1)}, f32[264,256]{1,0:T(8,128)S(1)}, u32[]{:S(2)}, u32[]{:S(2)}) %collective-permute-start.1) | collective-permute-done | bytes 270368 | tf_op jit(solution)/shard_map/ppermute | solution.py:195
  13.2 1.6 %collective-permute-start.3 = (f32[264,256]{1,0:T(8,128)S(1)}, f32[264,256]{1,0:T(8,128)S(1)}, u32[]{:S(2)}, u32[]{:S(2)}) collective-permute-start(f32[264,256]{1,0:T(8,128)S(1)} %collective-permute-done.1.one), channel_id=1, source_target_pairs={{0,2},{2,0},{4,6},{6,4},{8,10},{10,8},{12,14},{14,12},{16,18},{18,... | collective-permute-start | bytes 811016 | tf_op jit(solution)/shard_map/ppermute | solution.py:195
  14.8 0.7 %collective-permute-start.9 = (f32[264,256]{1,0:T(8,128)S(1)}, f32[264,256]{1,0:T(8,128)S(1)}, u32[]{:S(2)}, u32[]{:S(2)}) collective-permute-start(f32[264,256]{1,0:T(8,128)S(1)} %get-tuple-element.23.im), channel_id=1, source_target_pairs={{16,14},{24,22},{6,8},{14,16},{17,15},{25,23},{7,9},{15,17}} | collective-permute-start | bytes 811016 | tf_op jit(solution)/shard_map/ppermute | solution.py:195
  15.5 1.2 %collective-permute-done.5.x = f32[264,256]{1,0:T(8,128)S(1)} collective-permute-done((f32[264,256]{1,0:T(8,128)S(1)}, f32[264,256]{1,0:T(8,128)S(1)}, u32[]{:S(2)}, u32[]{:S(2)}) %collective-permute-start.5) | collective-permute-done | bytes 270368 | tf_op jit(solution)/shard_map/ppermute | solution.py:195
  16.7 0.7 %collective-permute-start.8 = (f32[264,256]{1,0:T(8,128)S(1)}, f32[264,256]{1,0:T(8,128)S(1)}, u32[]{:S(2)}, u32[]{:S(2)}) collective-permute-start(f32[264,256]{1,0:T(8,128)S(1)} %collective-permute-done.2.two), channel_id=1, source_target_pairs={{8,6},{14,16},{16,14},{22,24},{9,7},{15,17},{17,15},{23,25}} | collective-permute-start | bytes 811016 | tf_op jit(solution)/shard_map/ppermute | solution.py:195
  17.6 3.8 %collective-permute-start.7 = (f32[256,256]{1,0:T(8,128)S(1)}, f32[256,256]{1,0:T(8,128)S(1)}, u32[]{:S(2)}, u32[]{:S(2)}) collective-permute-start(f32[256,256]{1,0:T(8,128)S(1)} %shard_map.102), channel_id=1, source_target_pairs={{0,4},{2,6},{4,0},{6,2},{8,12},{10,14},{12,8},{14,10},{16,20},{18,... | collective-permute-start | bytes 786440 | tf_op jit(solution)/shard_map/ppermute | solution.py:195
  21.6 6.0 %collective-permute-start.10 = (f32[256,256]{1,0:T(8,128)S(1)}, f32[256,256]{1,0:T(8,128)S(1)}, u32[]{:S(2)}, u32[]{:S(2)}) collective-permute-start(f32[256,256]{1,0:T(8,128)S(1)} %get-tuple-element.26), channel_id=1, source_target_pairs={{0,8},{4,12},{8,16},{10,2},{12,20},{14,6},{16,24},{18,10},{20,28},... | collective-permute-start | bytes 786440 | tf_op jit(solution)/shard_map/ppermute | solution.py:195
  27.6 1.3 %collective-permute-start.11 = (f32[256,256]{1,0:T(8,128)S(1)}, f32[256,256]{1,0:T(8,128)S(1)}, u32[]{:S(2)}, u32[]{:S(2)}) collective-permute-start(f32[256,256]{1,0:T(8,128)S(1)} %get-tuple-element.27), channel_id=1, source_target_pairs={{2,10},{6,14},{8,0},{10,18},{12,4},{14,22},{16,8},{18,26},{20,12},... | collective-permute-start | bytes 786440 | tf_op jit(solution)/shard_map/ppermute | solution.py:195
  28.9 0.7 %shard_map.101 = (f32[2,256,256]{2,1,0:T(8,128)S(1)}, f32[256,64]{1,0:T(8,128)S(1)}) custom-call(f32[264,256]{1,0:T(8,128)S(1)} %get-tuple-element.22.re, f32[264,256]{1,0:T(8,128)S(1)} %get-tuple-element.23.im, f32[1,1,2,256,256]{4,3,2,1,0:T(8,128)S(1)} %collective-permute-done.twin_block, f32[264,256]{1,0:T(8,128)S(1)} %collective-permute-done.1.one, ...), custom_call_target="tpu_custom_call" | custom-call | tf_op jit(solution)/shard_map/pallas_call | solution.py:453
  29.6 1.0 %collective-permute-done.7.from_x = f32[256,256]{1,0:T(8,128)S(1)} collective-permute-done((f32[256,256]{1,0:T(8,128)S(1)}, f32[256,256]{1,0:T(8,128)S(1)}, u32[]{:S(2)}, u32[]{:S(2)}) %collective-permute-start.7) | collective-permute-done | bytes 262176 | tf_op jit(solution)/shard_map/ppermute | solution.py:195
  30.6 3.4 %collective-permute-done.10.from_1 = f32[256,256]{1,0:T(8,128)S(1)} collective-permute-done((f32[256,256]{1,0:T(8,128)S(1)}, f32[256,256]{1,0:T(8,128)S(1)}, u32[]{:S(2)}, u32[]{:S(2)}) %collective-permute-start.10) | collective-permute-done | bytes 262176 | tf_op jit(solution)/shard_map/ppermute | solution.py:195
  34.0 1.9 %collective-permute-done.11.from_2 = f32[256,256]{1,0:T(8,128)S(1)} collective-permute-done((f32[256,256]{1,0:T(8,128)S(1)}, f32[256,256]{1,0:T(8,128)S(1)}, u32[]{:S(2)}, u32[]{:S(2)}) %collective-permute-start.11) | collective-permute-done | bytes 262176 | tf_op jit(solution)/shard_map/ppermute | solution.py:195
  35.9 3.0 %shard_map.104 = (f32[64,128]{1,0:T(8,128)S(1)}, f32[2,256,256]{2,1,0:T(8,128)S(1)}) custom-call(f32[2,256,256]{2,1,0:T(8,128)S(1)} %get-tuple-element.25.own, f32[264,256]{1,0:T(8,128)S(1)} %get-tuple-element.22.re, f32[256,256]{1,0:T(8,128)S(1)} %copy-done, f32[256,256]{1,0:T(8,128)S(1)} %collective-permute-done.7.from_x, ...), custom_call_target="tpu_custom_call" | custom-call | tf_op jit(solution)/shard_map/pallas_call | solution.py:453
  38.9 4.2 %shard_map.105 = (f32[2,256,256]{2,1,0:T(8,128)S(1)}, f32[512,64]{1,0:T(8,128)S(1)}, f32[64,512]{1,0:T(8,128)S(1)}) custom-call(f32[2,256,256]{2,1,0:T(8,128)S(1)} %get-tuple-element.28.base, s32[1,64]{1,0:T(1,128)S(1)} %copy-done.5), custom_call_target="tpu_custom_call" | custom-call | tf_op jit(solution)/shard_map/pallas_call | solution.py:453
  43.7 3.5 %collective-permute-start.13 = (f32[64,128]{1,0:T(8,128)S(1)}, f32[64,128]{1,0:T(8,128)S(1)}, u32[]{:S(2)}, u32[]{:S(2)}) collective-permute-start(f32[64,128]{1,0:T(8,128)S(1)} %get-tuple-element.35), channel_id=1, source_target_pairs={{0,1},{1,0},{2,3},{3,2},{4,5},{5,4},{6,7},{7,6},{8,9},{9,8},{10,11... | collective-permute-start | bytes 98312 | tf_op jit(solution)/shard_map/ppermute | solution.py:497
  47.1 0.7 %shard_map.107.given = f32[1,1,2,256,256]{4,3,2,1,0:T(8,128)} custom-call(f32[1]{0:T(128)} %get-tuple-element.36.scale, f32[4,256,256]{2,1,0:T(8,128)S(1)} %get-tuple-element.37.series, f32[2,256,256]{2,1,0:T(8,128)S(1)} %get-tuple-element.38.a_in), custom_call_target="tpu_custom_call" | custom-call | tf_op jit(solution)/shard_map/pallas_call | solution.py:439
  47.8 1.2 %collective-permute-done.13.message = f32[64,128]{1,0:T(8,128)S(1)} collective-permute-done((f32[64,128]{1,0:T(8,128)S(1)}, f32[64,128]{1,0:T(8,128)S(1)}, u32[]{:S(2)}, u32[]{:S(2)}) %collective-permute-start.13) | collective-permute-done | bytes 32800 | tf_op jit(solution)/shard_map/ppermute | solution.py:497
  49.0 1.3 %shard_map.108 = f32[1,1,2,256,256]{4,3,2,1,0:T(8,128)} custom-call(f32[2,256,256]{2,1,0:T(8,128)S(1)} %get-tuple-element.30.g, f32[512,64]{1,0:T(8,128)S(1)} %get-tuple-element.31.cols, f32[64,512]{1,0:T(8,128)S(1)} %get-tuple-element.32.rows, f32[64,128]{1,0:T(8,128)S(1)} %collective-permute-done.13.message, ...), custom_call_target="tpu_custom_call", output_to_operand_aliasing={{}: (4, {})} | custom-call | tf_op jit(solution)/shard_map/pallas_call | solution.py:439
  (33 shorter events, 1.0 us)
Async XLA Ops:
  0.0 0.7 %copy-start.8 = (f32[8]{0:T(128)S(1)}, f32[8]{0:T(128)}, u32[]{:S(2)}) copy-start(f32[8]{0:T(128)} %table_hbm.1) | copy-start | bytes 100
  0.0 0.7 %copy-start.6 = (s32[1,2]{1,0:T(1,128)S(1)}, s32[1,2]{1,0:T(1,128)}, u32[]{:S(2)}) copy-start(s32[1,2]{1,0:T(1,128)} %source_hbm.1) | copy-start | bytes 28
  0.0 0.7 %copy-start.7 = (s32[1,2]{1,0:T(1,128)S(1)}, s32[1,2]{1,0:T(1,128)}, u32[]{:S(2)}) copy-start(s32[1,2]{1,0:T(1,128)} %index_hbm.1) | copy-start | bytes 28
  0.7 1.0 %copy-start.1 = (f32[1,1,2,256,256]{4,3,2,1,0:T(8,128)S(1)}, f32[1,1,2,256,256]{4,3,2,1,0:T(8,128)}, u32[]{:S(2)}) copy-start(f32[1,1,2,256,256]{4,3,2,1,0:T(8,128)} %green.1) | copy-start | bytes 1572868
  1.8 9.5 %copy-start.2 = (f32[1,1,2,256,256]{4,3,2,1,0:T(8,128)S(1)}, f32[1,1,2,256,256]{4,3,2,1,0:T(8,128)}, u32[]{:S(2)}) copy-start(f32[1,1,2,256,256]{4,3,2,1,0:T(8,128)} %green.1) | copy-start | bytes 1572868
  2.4 9.7 %collective-permute-start.2 = (f32[264,256]{1,0:T(8,128)S(1)}, f32[264,256]{1,0:T(8,128)S(1)}, u32[]{:S(2)}, u32[]{:S(2)}) collective-permute-start(f32[264,256]{1,0:T(8,128)S(1)} %get-tuple-element.22.re), channel_id=1, source_target_pairs={{2,10},{6,14},{8,0},{10,18},{12,4},{14,22},{16,8},{18,26},{20,12},... | collective-permute-start | bytes 811016 | tf_op jit(solution)/shard_map/ppermute | solution.py:195
  3.7 9.5 %collective-permute-start.1 = (f32[264,256]{1,0:T(8,128)S(1)}, f32[264,256]{1,0:T(8,128)S(1)}, u32[]{:S(2)}, u32[]{:S(2)}) collective-permute-start(f32[264,256]{1,0:T(8,128)S(1)} %get-tuple-element.22.re), channel_id=1, source_target_pairs={{0,8},{4,12},{8,16},{10,2},{12,20},{14,6},{16,24},{18,10},{20,28},... | collective-permute-start | bytes 811016 | tf_op jit(solution)/shard_map/ppermute | solution.py:195
  9.3 7.4 %collective-permute-start.5 = (f32[264,256]{1,0:T(8,128)S(1)}, f32[264,256]{1,0:T(8,128)S(1)}, u32[]{:S(2)}, u32[]{:S(2)}) collective-permute-start(f32[264,256]{1,0:T(8,128)S(1)} %get-tuple-element.23.im), channel_id=1, source_target_pairs={{0,4},{2,6},{4,0},{6,2},{8,12},{10,14},{12,8},{14,10},{16,20},{18,... | collective-permute-start | bytes 811016 | tf_op jit(solution)/shard_map/ppermute | solution.py:195
  11.3 5.4 %collective-permute-start = (f32[1,1,2,256,256]{4,3,2,1,0:T(8,128)S(1)}, f32[1,1,2,256,256]{4,3,2,1,0:T(8,128)S(1)}, u32[]{:S(2)}, u32[]{:S(2)}) collective-permute-start(f32[1,1,2,256,256]{4,3,2,1,0:T(8,128)S(1)} %copy-done.2), channel_id=1, source_target_pairs={{0,2},{2,0},{4,6},{6,4},{8,10},{10,8},{12,14},{14,12},{16,18},{18,... | collective-permute-start | bytes 1572872 | tf_op jit(solution)/shard_map/ppermute | solution.py:195
  12.1 5.3 %collective-permute-start.4 = (f32[264,256]{1,0:T(8,128)S(1)}, f32[264,256]{1,0:T(8,128)S(1)}, u32[]{:S(2)}, u32[]{:S(2)}) collective-permute-start(f32[264,256]{1,0:T(8,128)S(1)} %collective-permute-done.2.two), channel_id=1, source_target_pairs={{0,2},{2,0},{4,6},{6,4},{8,10},{10,8},{12,14},{14,12},{16,18},{18,... | collective-permute-start | bytes 811016 | tf_op jit(solution)/shard_map/ppermute | solution.py:195
  13.2 4.1 %collective-permute-start.3 = (f32[264,256]{1,0:T(8,128)S(1)}, f32[264,256]{1,0:T(8,128)S(1)}, u32[]{:S(2)}, u32[]{:S(2)}) collective-permute-start(f32[264,256]{1,0:T(8,128)S(1)} %collective-permute-done.1.one), channel_id=1, source_target_pairs={{0,2},{2,0},{4,6},{6,4},{8,10},{10,8},{12,14},{14,12},{16,18},{18,... | collective-permute-start | bytes 811016 | tf_op jit(solution)/shard_map/ppermute | solution.py:195
  14.8 6.6 %collective-permute-start.9 = (f32[264,256]{1,0:T(8,128)S(1)}, f32[264,256]{1,0:T(8,128)S(1)}, u32[]{:S(2)}, u32[]{:S(2)}) collective-permute-start(f32[264,256]{1,0:T(8,128)S(1)} %get-tuple-element.23.im), channel_id=1, source_target_pairs={{16,14},{24,22},{6,8},{14,16},{17,15},{25,23},{7,9},{15,17}} | collective-permute-start | bytes 811016 | tf_op jit(solution)/shard_map/ppermute | solution.py:195
  16.7 4.7 %collective-permute-start.6 = (f32[264,256]{1,0:T(8,128)S(1)}, f32[264,256]{1,0:T(8,128)S(1)}, u32[]{:S(2)}, u32[]{:S(2)}) collective-permute-start(f32[264,256]{1,0:T(8,128)S(1)} %collective-permute-done.5.x), channel_id=1, source_target_pairs={{0,2},{2,0},{4,6},{6,4},{8,10},{10,8},{12,14},{14,12},{16,18},{18,... | collective-permute-start | bytes 811016 | tf_op jit(solution)/shard_map/ppermute | solution.py:195
  16.7 12.9 %collective-permute-start.8 = (f32[264,256]{1,0:T(8,128)S(1)}, f32[264,256]{1,0:T(8,128)S(1)}, u32[]{:S(2)}, u32[]{:S(2)}) collective-permute-start(f32[264,256]{1,0:T(8,128)S(1)} %collective-permute-done.2.two), channel_id=1, source_target_pairs={{8,6},{14,16},{16,14},{22,24},{9,7},{15,17},{17,15},{23,25}} | collective-permute-start | bytes 811016 | tf_op jit(solution)/shard_map/ppermute | solution.py:195
  17.5 11.4 %copy-start = (f32[256,256]{1,0:T(8,128)S(1)}, f32[256,256]{1,0:T(8,128)}, u32[]{:S(2)}) copy-start(f32[256,256]{1,0:T(8,128)} %profile.3) | copy-start | bytes 786436
  17.6 11.4 %copy-start.3 = (f32[1,256,256]{2,1,0:T(8,128)S(1)}, f32[1,256,256]{2,1,0:T(8,128)}, u32[]{:S(2)}) copy-start(f32[1,256,256]{2,1,0:T(8,128)} %ham.1) | copy-start | bytes 786436
  17.6 11.4 %copy-start.4 = (f32[1,64,64]{2,1,0:T(8,128)S(1)}, f32[1,64,64]{2,1,0:T(8,128)}, u32[]{:S(2)}) copy-start(f32[1,64,64]{2,1,0:T(8,128)} %coup.1) | copy-start | bytes 49156
  17.6 13.0 %collective-permute-start.7 = (f32[256,256]{1,0:T(8,128)S(1)}, f32[256,256]{1,0:T(8,128)S(1)}, u32[]{:S(2)}, u32[]{:S(2)}) collective-permute-start(f32[256,256]{1,0:T(8,128)S(1)} %shard_map.102), channel_id=1, source_target_pairs={{0,4},{2,6},{4,0},{6,2},{8,12},{10,14},{12,8},{14,10},{16,20},{18,... | collective-permute-start | bytes 786440 | tf_op jit(solution)/shard_map/ppermute | solution.py:195
  21.5 7.4 %copy-start.9 = (s32[1,64]{1,0:T(1,128)S(1)}, s32[1,64]{1,0:T(1,128)}, u32[]{:S(2)}) copy-start(s32[1,64]{1,0:T(1,128)} %left.1) | copy-start | bytes 772
  21.6 12.4 %collective-permute-start.10 = (f32[256,256]{1,0:T(8,128)S(1)}, f32[256,256]{1,0:T(8,128)S(1)}, u32[]{:S(2)}, u32[]{:S(2)}) collective-permute-start(f32[256,256]{1,0:T(8,128)S(1)} %get-tuple-element.26), channel_id=1, source_target_pairs={{0,8},{4,12},{8,16},{10,2},{12,20},{14,6},{16,24},{18,10},{20,28},... | collective-permute-start | bytes 786440 | tf_op jit(solution)/shard_map/ppermute | solution.py:195
  27.6 8.3 %collective-permute-start.11 = (f32[256,256]{1,0:T(8,128)S(1)}, f32[256,256]{1,0:T(8,128)S(1)}, u32[]{:S(2)}, u32[]{:S(2)}) collective-permute-start(f32[256,256]{1,0:T(8,128)S(1)} %get-tuple-element.27), channel_id=1, source_target_pairs={{2,10},{6,14},{8,0},{10,18},{12,4},{14,22},{16,8},{18,26},{20,12},... | collective-permute-start | bytes 786440 | tf_op jit(solution)/shard_map/ppermute | solution.py:195
  29.6 6.3 %copy-start.5 = (s32[1,64]{1,0:T(1,128)S(1)}, s32[1,64]{1,0:T(1,128)}, u32[]{:S(2)}) copy-start(s32[1,64]{1,0:T(1,128)} %right.3) | copy-start | bytes 772
  38.8 4.3 %collective-permute-start.12 = (f32[64,128]{1,0:T(8,128)S(1)}, f32[64,128]{1,0:T(8,128)S(1)}, u32[]{:S(2)}, u32[]{:S(2)}) collective-permute-start(f32[64,128]{1,0:T(8,128)S(1)} %get-tuple-element.34), channel_id=1, source_target_pairs={{0,1},{1,0},{2,3},{3,2},{4,5},{5,4},{6,7},{7,6},{8,9},{9,8},{10,11... | collective-permute-start | bytes 98312 | tf_op jit(solution)/shard_map/ppermute | solution.py:497
  43.7 5.4 %collective-permute-start.13 = (f32[64,128]{1,0:T(8,128)S(1)}, f32[64,128]{1,0:T(8,128)S(1)}, u32[]{:S(2)}, u32[]{:S(2)}) collective-permute-start(f32[64,128]{1,0:T(8,128)S(1)} %get-tuple-element.35), channel_id=1, source_target_pairs={{0,1},{1,0},{2,3},{3,2},{4,5},{5,4},{6,7},{7,6},{8,9},{9,8},{10,11... | collective-permute-start | bytes 98312 | tf_op jit(solution)/shard_map/ppermute | solution.py:497

commit v4 on v3

--- a/solution.py
+++ b/solution.py
@@ -119,20 +119,18 @@
     return unit_of(a_re.shape[0]) - scale * gram, (-scale) * skew(gram), scale
 
 
-def corner(a_re, a_im, proj, series=False):
+def corner(a_re, a_im, proj):
     width, faces = proj.shape
     e, q, scale = begin(a_re, a_im)
     proj_t = proj.T
     y = scale * mm(left3(proj_t), right3(both(a_re, a_im), axis=1), NT)
     y_re, y_im = y[:, :width], -y[:, width:]
-    s_e, s_q = unit_of(width) + e, q
+    powers = [e]
     for turn in range(1, DOUBLINGS):
         h = herm(e, q)
-        if series and turn > 1:
-            s_e = s_e + times(herm(s_e, s_q), h)
-            s_q = skew(s_e)
         e = times(h, h)
         q = skew(e)
+        powers.append(e)
         c_re, c_im = thin_times(y_re, y_im, h)
         y_re, y_im = y_re + c_re, y_im + c_im
     h = herm(e, q)
@@ -143,7 +141,7 @@
     u_re, u_im = thin_times(y_re, y_im, h)
     out = mm(left3(both(y_re, y_im)), right3(proj))
     out += mm(stack(left3(u_re, u_im), left3(u_im, -u_re)), right3(t_re, t_im, axis=1), NT)
-    return out[:faces], out[faces:], (s_e, s_q, e, q), scale
+    return out[:faces], out[faces:], powers, scale
 
 
 def series_of(e, q):
@@ -374,7 +372,7 @@
     def _():
         width, faces = placed.shape
         a_re, a_im = bounded(base, placed, incoming)
-        m_re, m_im, series, scale = corner(a_re, a_im, placed[...], series=True)
+        m_re, m_im, series, scale = corner(a_re, a_im, placed[...])
         message_out[:, :faces] = m_re
         message_out[:, faces:] = m_im
         for k, part in enumerate(series):
@@ -409,7 +407,12 @@
 def last_full_kernel(slabs, scale, series, a_in, green_out, block, sems):
     @pl.when(lax.axis_index("slab") == slabs - 1)
     def _():
-        block[0], block[1] = full(a_in[0], a_in[1], *(series[k] for k in range(4)), scale[0])
+        e, s_e = series[0], unit_of(a_in.shape[1]) + series[0]
+        for turn in range(1, DOUBLINGS - 1):
+            e = series[turn]
+            s_e = s_e + times(herm(s_e, skew(s_e)), herm(e, skew(e)))
+        e = series[DOUBLINGS - 1]
+        block[0], block[1] = full(a_in[0], a_in[1], s_e, skew(s_e), e, skew(e), scale[0])
         copies = [pltpu.make_async_copy(block.at[k], green_out.at[0, 0, k], sems.at[k]) for k in range(2)]
         for copy in copies:
             copy.start()
@@ -474,17 +477,19 @@
     one = sent(re, all_1)
     two = sent(re, all_2)
     near = sent(im, near_pairs)
+    x, near = lax.optimization_barrier((x, near))
     pair_one = sent(one, all_twin)
     pair_two = sent(two, all_twin)
-    far = sent(two, far_pairs)
     pair_x = sent(x, all_twin)
     (over_x_sum,) = call(over_x_kernel, [block], [], re, pair, one, two, pair_one, pair_two, x)
-    from_x = sent(over_x_sum, all_x)
     sum_1, sum_2 = call(
         groups_kernel, [block] * 2, [], im, pair, x, pair_x, near, one, two
     )
+    two_later, sum_1, sum_2, over_x_sum = lax.optimization_barrier((two, sum_1, sum_2, over_x_sum))
+    from_x = sent(over_x_sum, all_x)
     from_1 = sent(sum_1, all_1)
     from_2 = sent(sum_2, all_2)
+    far = sent(two_later, far_pairs)
     own, placed = call(
         own_kernel, [(2, *block), (width, coupling.shape[1])], [],
         re, im, pair, one, two, pair_one, pair_two, x, pair_x, hamiltonian, profile, coupling, left_face,

time: 50.6 us -> 49.1 us (0.970)
  starting transfers between devices: 26.3 us -> 25.3 us
  waiting for transfers between devices: 10.6 us -> 9.74 us
    ppermute x12, waiting for transfers between devices: 9.4 us -> 8.69 us  [sent(): return lax.ppermute(value, 'energy', pairs)]
    ppermute x12, starting transfers between devices: 22.8 us -> 22.2 us  [sent(): return lax.ppermute(value, 'energy', pairs)]
  transfers between devices with their start and end apart: 14 -> 14, of which waited for: 7 -> 6; matrix products, arithmetic and copies ran while one was open for 0% -> 0% of each run, Pallas kernels for 12% -> 12%
where the time goes in v4:
time: 49.1 us; the launch traced here: 48.8 us
  starting transfers between devices  25.3 us (52%)
  Pallas kernels  11.6 us (24%)
  waiting for transfers between devices  9.74 us (20%)
  between operations  1.09 us (2%)
  local copies, waits for them, and re-layouts  1.08 us (2%)
    ppermute x12, starting transfers between devices, sent(): return lax.ppermute(value, 'energy', pairs)  22.2 us
    pallas_call x6, Pallas kernels, call(): pl.pallas_call(kernel, out_shape=[jax.ShapeDtypeStruct(shape, f32) for sh...  8.81 us
    ppermute x12, waiting for transfers between devices, sent(): return lax.ppermute(value, 'energy', pairs)  8.69 us
    ppermute x2, starting transfers between devices, passed_along(): lax.ppermute(value, 'slab', [(start, (start + steps) % count) for start i...  3.08 us
    pallas_call x2, Pallas kernels, write_green(): pl.pallas_call(kernel, out_shape=jax.ShapeDtypeStruct(shape, f32), in_spe...  2.15 us
    unnamed x20, local copies, waits for them, and re-layouts  1.08 us
    ppermute x2, waiting for transfers between devices, passed_along(): lax.ppermute(value, 'slab', [(start, (start + steps) % count) for start i...  1.05 us
  transfers between devices with their start and end apart: 14, of which 6 were waited for; matrix products, arithmetic and copies ran while one was open for 0% of the time, Pallas kernels for 12%

profile of v4, /device:TPU:0, one launch (start us, length us, event | category | flops | bytes accessed | tf_op | source)
XLA Modules:
  0.0 48.8 jit_solution(489345803513399120)
XLA Ops:
  0.7 1.0 %copy-done.1 = f32[1,1,2,256,256]{4,3,2,1,0:T(8,128)S(1)} copy-done((f32[1,1,2,256,256]{4,3,2,1,0:T(8,128)S(1)}, f32[1,1,2,256,256]{4,3,2,1,0:T(8,128)}, u32[]{:S(2)}) %copy-start.1) | copy-done | bytes 524312
  1.8 0.6 %shard_map.100 = (f32[264,256]{1,0:T(8,128)S(1)}, f32[264,256]{1,0:T(8,128)S(1)}) custom-call(f32[1]{0:T(128)S(6)} %copy.13.energy_hbm, s32[1,2]{1,0:T(1,128)S(1)} %copy-done.6, s32[1,2]{1,0:T(1,128)S(1)} %copy-done.7, f32[8]{0:T(128)S(1)} %copy-done.8, f32[1,1,2,256,256]{4,3,2,1,0:T(8,128)S(1)} %copy-done.1), custom_call_target="tpu_custom_call" | custom-call | tf_op jit(solution)/shard_map/pallas_call | solution.py:227
  2.4 0.7 %collective-permute-start.6 = (f32[264,256]{1,0:T(8,128)S(1)}, f32[264,256]{1,0:T(8,128)S(1)}, u32[]{:S(2)}, u32[]{:S(2)}) collective-permute-start(f32[264,256]{1,0:T(8,128)S(1)} %get-tuple-element.29.im), channel_id=1, source_target_pairs={{16,14},{24,22},{6,8},{14,16},{17,15},{25,23},{7,9},{15,17}} | collective-permute-start | bytes 811016 | tf_op jit(solution)/shard_map/ppermute | solution.py:193
  3.1 3.0 %collective-permute-start.5 = (f32[264,256]{1,0:T(8,128)S(1)}, f32[264,256]{1,0:T(8,128)S(1)}, u32[]{:S(2)}, u32[]{:S(2)}) collective-permute-start(f32[264,256]{1,0:T(8,128)S(1)} %get-tuple-element.29.im), channel_id=1, source_target_pairs={{0,4},{2,6},{4,0},{6,2},{8,12},{10,14},{12,8},{14,10},{16,20},{18,... | collective-permute-start | bytes 811016 | tf_op jit(solution)/shard_map/ppermute | solution.py:193
  6.1 1.3 %collective-permute-start.2 = (f32[264,256]{1,0:T(8,128)S(1)}, f32[264,256]{1,0:T(8,128)S(1)}, u32[]{:S(2)}, u32[]{:S(2)}) collective-permute-start(f32[264,256]{1,0:T(8,128)S(1)} %get-tuple-element.28.re), channel_id=1, source_target_pairs={{2,10},{6,14},{8,0},{10,18},{12,4},{14,22},{16,8},{18,26},{20,12},... | collective-permute-start | bytes 811016 | tf_op jit(solution)/shard_map/ppermute | solution.py:193
  7.4 4.6 %collective-permute-start.1 = (f32[264,256]{1,0:T(8,128)S(1)}, f32[264,256]{1,0:T(8,128)S(1)}, u32[]{:S(2)}, u32[]{:S(2)}) collective-permute-start(f32[264,256]{1,0:T(8,128)S(1)} %get-tuple-element.28.re), channel_id=1, source_target_pairs={{0,8},{4,12},{8,16},{10,2},{12,20},{14,6},{16,24},{18,10},{20,28},... | collective-permute-start | bytes 811016 | tf_op jit(solution)/shard_map/ppermute | solution.py:193
  12.0 1.3 %collective-permute-start = (f32[1,1,2,256,256]{4,3,2,1,0:T(8,128)S(1)}, f32[1,1,2,256,256]{4,3,2,1,0:T(8,128)S(1)}, u32[]{:S(2)}, u32[]{:S(2)}) collective-permute-start(f32[1,1,2,256,256]{4,3,2,1,0:T(8,128)S(1)} %copy-done.2), channel_id=1, source_target_pairs={{0,2},{2,0},{4,6},{6,4},{8,10},{10,8},{12,14},{14,12},{16,18},{18,... | collective-permute-start | bytes 1572872 | tf_op jit(solution)/shard_map/ppermute | solution.py:193
  13.6 0.9 %collective-permute-done.2.two = f32[264,256]{1,0:T(8,128)S(1)} collective-permute-done((f32[264,256]{1,0:T(8,128)S(1)}, f32[264,256]{1,0:T(8,128)S(1)}, u32[]{:S(2)}, u32[]{:S(2)}) %collective-permute-start.2) | collective-permute-done | bytes 270368 | tf_op jit(solution)/shard_map/ppermute | solution.py:193
  14.4 3.1 %collective-permute-start.4 = (f32[264,256]{1,0:T(8,128)S(1)}, f32[264,256]{1,0:T(8,128)S(1)}, u32[]{:S(2)}, u32[]{:S(2)}) collective-permute-start(f32[264,256]{1,0:T(8,128)S(1)} %collective-permute-done.2.two), channel_id=1, source_target_pairs={{0,2},{2,0},{4,6},{6,4},{8,10},{10,8},{12,14},{14,12},{16,18},{18,... | collective-permute-start | bytes 811016 | tf_op jit(solution)/shard_map/ppermute | solution.py:193
  17.5 0.6 %collective-permute-done.1.one = f32[264,256]{1,0:T(8,128)S(1)} collective-permute-done((f32[264,256]{1,0:T(8,128)S(1)}, f32[264,256]{1,0:T(8,128)S(1)}, u32[]{:S(2)}, u32[]{:S(2)}) %collective-permute-start.1) | collective-permute-done | bytes 270368 | tf_op jit(solution)/shard_map/ppermute | solution.py:193
  18.1 1.1 %collective-permute-start.3 = (f32[264,256]{1,0:T(8,128)S(1)}, f32[264,256]{1,0:T(8,128)S(1)}, u32[]{:S(2)}, u32[]{:S(2)}) collective-permute-start(f32[264,256]{1,0:T(8,128)S(1)} %collective-permute-done.1.one), channel_id=1, source_target_pairs={{0,2},{2,0},{4,6},{6,4},{8,10},{10,8},{12,14},{14,12},{16,18},{18,... | collective-permute-start | bytes 811016 | tf_op jit(solution)/shard_map/ppermute | solution.py:193
  19.4 0.9 %collective-permute-done.3.pair_one = f32[264,256]{1,0:T(8,128)S(1)} collective-permute-done((f32[264,256]{1,0:T(8,128)S(1)}, f32[264,256]{1,0:T(8,128)S(1)}, u32[]{:S(2)}, u32[]{:S(2)}) %collective-permute-start.3) | collective-permute-done | bytes 270368 | tf_op jit(solution)/shard_map/ppermute | solution.py:193
  20.5 0.7 %collective-permute-start.9 = (f32[264,256]{1,0:T(8,128)S(1)}, f32[264,256]{1,0:T(8,128)S(1)}, u32[]{:S(2)}, u32[]{:S(2)}) collective-permute-start(f32[264,256]{1,0:T(8,128)S(1)} %collective-permute-done.2.two), channel_id=1, source_target_pairs={{8,6},{14,16},{16,14},{22,24},{9,7},{15,17},{17,15},{23,25}} | collective-permute-start | bytes 811016 | tf_op jit(solution)/shard_map/ppermute | solution.py:193
  21.5 4.6 %collective-permute-start.10 = (f32[256,256]{1,0:T(8,128)S(1)}, f32[256,256]{1,0:T(8,128)S(1)}, u32[]{:S(2)}, u32[]{:S(2)}) collective-permute-start(f32[256,256]{1,0:T(8,128)S(1)} %get-tuple-element.38), channel_id=1, source_target_pairs={{0,8},{4,12},{8,16},{10,2},{12,20},{14,6},{16,24},{18,10},{20,28},... | collective-permute-start | bytes 786440 | tf_op jit(solution)/shard_map/ppermute | solution.py:193
  26.2 1.3 %collective-permute-start.11 = (f32[256,256]{1,0:T(8,128)S(1)}, f32[256,256]{1,0:T(8,128)S(1)}, u32[]{:S(2)}, u32[]{:S(2)}) collective-permute-start(f32[256,256]{1,0:T(8,128)S(1)} %get-tuple-element.39), channel_id=1, source_target_pairs={{2,10},{6,14},{8,0},{10,18},{12,4},{14,22},{16,8},{18,26},{20,12},... | collective-permute-start | bytes 786440 | tf_op jit(solution)/shard_map/ppermute | solution.py:193
  27.5 0.7 %shard_map.101 = (f32[2,256,256]{2,1,0:T(8,128)S(1)}, f32[256,64]{1,0:T(8,128)S(1)}) custom-call(f32[264,256]{1,0:T(8,128)S(1)} %get-tuple-element.28.re, f32[264,256]{1,0:T(8,128)S(1)} %get-tuple-element.29.im, f32[1,1,2,256,256]{4,3,2,1,0:T(8,128)S(1)} %collective-permute-done.twin_block, f32[264,256]{1,0:T(8,128)S(1)} %collective-permute-done.1.one, ...), custom_call_target="tpu_custom_call" | custom-call | tf_op jit(solution)/shard_map/pallas_call | solution.py:456
  28.2 2.9 %collective-permute-done.8.from_x = f32[256,256]{1,0:T(8,128)S(1)} collective-permute-done((f32[256,256]{1,0:T(8,128)S(1)}, f32[256,256]{1,0:T(8,128)S(1)}, u32[]{:S(2)}, u32[]{:S(2)}) %collective-permute-start.8) | collective-permute-done | bytes 262176 | tf_op jit(solution)/shard_map/ppermute | solution.py:193
  31.1 3.4 %collective-permute-done.11.from_2 = f32[256,256]{1,0:T(8,128)S(1)} collective-permute-done((f32[256,256]{1,0:T(8,128)S(1)}, f32[256,256]{1,0:T(8,128)S(1)}, u32[]{:S(2)}, u32[]{:S(2)}) %collective-permute-start.11) | collective-permute-done | bytes 262176 | tf_op jit(solution)/shard_map/ppermute | solution.py:193
  34.5 3.0 %shard_map.104 = (f32[64,128]{1,0:T(8,128)S(1)}, f32[2,256,256]{2,1,0:T(8,128)S(1)}) custom-call(f32[2,256,256]{2,1,0:T(8,128)S(1)} %get-tuple-element.32.own, f32[264,256]{1,0:T(8,128)S(1)} %get-tuple-element.28.re, f32[256,256]{1,0:T(8,128)S(1)} %copy-done, f32[256,256]{1,0:T(8,128)S(1)} %collective-permute-done.8.from_x, ...), custom_call_target="tpu_custom_call" | custom-call | tf_op jit(solution)/shard_map/pallas_call | solution.py:456
  37.6 4.2 %shard_map.105 = (f32[2,256,256]{2,1,0:T(8,128)S(1)}, f32[512,64]{1,0:T(8,128)S(1)}, f32[64,512]{1,0:T(8,128)S(1)}) custom-call(f32[2,256,256]{2,1,0:T(8,128)S(1)} %get-tuple-element.40.base, s32[1,64]{1,0:T(1,128)S(1)} %copy-done.5), custom_call_target="tpu_custom_call" | custom-call | tf_op jit(solution)/shard_map/pallas_call | solution.py:456
  42.4 3.0 %collective-permute-start.13 = (f32[64,128]{1,0:T(8,128)S(1)}, f32[64,128]{1,0:T(8,128)S(1)}, u32[]{:S(2)}, u32[]{:S(2)}) collective-permute-start(f32[64,128]{1,0:T(8,128)S(1)} %get-tuple-element.47), channel_id=1, source_target_pairs={{0,1},{1,0},{2,3},{3,2},{4,5},{5,4},{6,7},{7,6},{8,9},{9,8},{10,11... | collective-permute-start | bytes 98312 | tf_op jit(solution)/shard_map/ppermute | solution.py:502
  45.4 0.8 %shard_map.107.given = f32[1,1,2,256,256]{4,3,2,1,0:T(8,128)} custom-call(f32[1]{0:T(128)} %get-tuple-element.48.scale, f32[4,256,256]{2,1,0:T(8,128)S(1)} %get-tuple-element.49.series, f32[2,256,256]{2,1,0:T(8,128)S(1)} %get-tuple-element.50.a_in), custom_call_target="tpu_custom_call" | custom-call | tf_op jit(solution)/shard_map/pallas_call | solution.py:442
  46.3 1.0 %collective-permute-done.13.message = f32[64,128]{1,0:T(8,128)S(1)} collective-permute-done((f32[64,128]{1,0:T(8,128)S(1)}, f32[64,128]{1,0:T(8,128)S(1)}, u32[]{:S(2)}, u32[]{:S(2)}) %collective-permute-start.13) | collective-permute-done | bytes 32800 | tf_op jit(solution)/shard_map/ppermute | solution.py:502
  47.3 1.3 %shard_map.108 = f32[1,1,2,256,256]{4,3,2,1,0:T(8,128)} custom-call(f32[2,256,256]{2,1,0:T(8,128)S(1)} %get-tuple-element.42.g, f32[512,64]{1,0:T(8,128)S(1)} %get-tuple-element.43.cols, f32[64,512]{1,0:T(8,128)S(1)} %get-tuple-element.44.rows, f32[64,128]{1,0:T(8,128)S(1)} %collective-permute-done.13.message, ...), custom_call_target="tpu_custom_call", output_to_operand_aliasing={{}: (4, {})} | custom-call | tf_op jit(solution)/shard_map/pallas_call | solution.py:442
  (33 shorter events, 1.7 us)
Async XLA Ops:
  0.0 0.7 %copy-start.7 = (s32[1,2]{1,0:T(1,128)S(1)}, s32[1,2]{1,0:T(1,128)}, u32[]{:S(2)}) copy-start(s32[1,2]{1,0:T(1,128)} %index_hbm.1) | copy-start | bytes 28
  0.0 0.7 %copy-start.6 = (s32[1,2]{1,0:T(1,128)S(1)}, s32[1,2]{1,0:T(1,128)}, u32[]{:S(2)}) copy-start(s32[1,2]{1,0:T(1,128)} %source_hbm.1) | copy-start | bytes 28
  0.0 0.7 %copy-start.8 = (f32[8]{0:T(128)S(1)}, f32[8]{0:T(128)}, u32[]{:S(2)}) copy-start(f32[8]{0:T(128)} %table_hbm.1) | copy-start | bytes 100
  0.7 1.0 %copy-start.1 = (f32[1,1,2,256,256]{4,3,2,1,0:T(8,128)S(1)}, f32[1,1,2,256,256]{4,3,2,1,0:T(8,128)}, u32[]{:S(2)}) copy-start(f32[1,1,2,256,256]{4,3,2,1,0:T(8,128)} %green.1) | copy-start | bytes 1572868
  1.8 10.2 %copy-start.2 = (f32[1,1,2,256,256]{4,3,2,1,0:T(8,128)S(1)}, f32[1,1,2,256,256]{4,3,2,1,0:T(8,128)}, u32[]{:S(2)}) copy-start(f32[1,1,2,256,256]{4,3,2,1,0:T(8,128)} %green.1) | copy-start | bytes 1572868
  2.4 10.9 %collective-permute-start.6 = (f32[264,256]{1,0:T(8,128)S(1)}, f32[264,256]{1,0:T(8,128)S(1)}, u32[]{:S(2)}, u32[]{:S(2)}) collective-permute-start(f32[264,256]{1,0:T(8,128)S(1)} %get-tuple-element.29.im), channel_id=1, source_target_pairs={{16,14},{24,22},{6,8},{14,16},{17,15},{25,23},{7,9},{15,17}} | collective-permute-start | bytes 811016 | tf_op jit(solution)/shard_map/ppermute | solution.py:193
  3.1 10.2 %collective-permute-start.5 = (f32[264,256]{1,0:T(8,128)S(1)}, f32[264,256]{1,0:T(8,128)S(1)}, u32[]{:S(2)}, u32[]{:S(2)}) collective-permute-start(f32[264,256]{1,0:T(8,128)S(1)} %get-tuple-element.29.im), channel_id=1, source_target_pairs={{0,4},{2,6},{4,0},{6,2},{8,12},{10,14},{12,8},{14,10},{16,20},{18,... | collective-permute-start | bytes 811016 | tf_op jit(solution)/shard_map/ppermute | solution.py:193
  6.1 8.3 %collective-permute-start.2 = (f32[264,256]{1,0:T(8,128)S(1)}, f32[264,256]{1,0:T(8,128)S(1)}, u32[]{:S(2)}, u32[]{:S(2)}) collective-permute-start(f32[264,256]{1,0:T(8,128)S(1)} %get-tuple-element.28.re), channel_id=1, source_target_pairs={{2,10},{6,14},{8,0},{10,18},{12,4},{14,22},{16,8},{18,26},{20,12},... | collective-permute-start | bytes 811016 | tf_op jit(solution)/shard_map/ppermute | solution.py:193
  7.4 10.7 %collective-permute-start.1 = (f32[264,256]{1,0:T(8,128)S(1)}, f32[264,256]{1,0:T(8,128)S(1)}, u32[]{:S(2)}, u32[]{:S(2)}) collective-permute-start(f32[264,256]{1,0:T(8,128)S(1)} %get-tuple-element.28.re), channel_id=1, source_target_pairs={{0,8},{4,12},{8,16},{10,2},{12,20},{14,6},{16,24},{18,10},{20,28},... | collective-permute-start | bytes 811016 | tf_op jit(solution)/shard_map/ppermute | solution.py:193
  12.0 7.2 %collective-permute-start = (f32[1,1,2,256,256]{4,3,2,1,0:T(8,128)S(1)}, f32[1,1,2,256,256]{4,3,2,1,0:T(8,128)S(1)}, u32[]{:S(2)}, u32[]{:S(2)}) collective-permute-start(f32[1,1,2,256,256]{4,3,2,1,0:T(8,128)S(1)} %copy-done.2), channel_id=1, source_target_pairs={{0,2},{2,0},{4,6},{6,4},{8,10},{10,8},{12,14},{14,12},{16,18},{18,... | collective-permute-start | bytes 1572872 | tf_op jit(solution)/shard_map/ppermute | solution.py:193
  13.3 5.8 %collective-permute-start.7 = (f32[264,256]{1,0:T(8,128)S(1)}, f32[264,256]{1,0:T(8,128)S(1)}, u32[]{:S(2)}, u32[]{:S(2)}) collective-permute-start(f32[264,256]{1,0:T(8,128)S(1)} %collective-permute-done.5.x), channel_id=1, source_target_pairs={{0,2},{2,0},{4,6},{6,4},{8,10},{10,8},{12,14},{14,12},{16,18},{18,... | collective-permute-start | bytes 811016 | tf_op jit(solution)/shard_map/ppermute | solution.py:193
  14.4 5.0 %collective-permute-start.4 = (f32[264,256]{1,0:T(8,128)S(1)}, f32[264,256]{1,0:T(8,128)S(1)}, u32[]{:S(2)}, u32[]{:S(2)}) collective-permute-start(f32[264,256]{1,0:T(8,128)S(1)} %collective-permute-done.2.two), channel_id=1, source_target_pairs={{0,2},{2,0},{4,6},{6,4},{8,10},{10,8},{12,14},{14,12},{16,18},{18,... | collective-permute-start | bytes 811016 | tf_op jit(solution)/shard_map/ppermute | solution.py:193
  18.1 2.2 %collective-permute-start.3 = (f32[264,256]{1,0:T(8,128)S(1)}, f32[264,256]{1,0:T(8,128)S(1)}, u32[]{:S(2)}, u32[]{:S(2)}) collective-permute-start(f32[264,256]{1,0:T(8,128)S(1)} %collective-permute-done.1.one), channel_id=1, source_target_pairs={{0,2},{2,0},{4,6},{6,4},{8,10},{10,8},{12,14},{14,12},{16,18},{18,... | collective-permute-start | bytes 811016 | tf_op jit(solution)/shard_map/ppermute | solution.py:193
  19.4 8.1 %copy-start = (f32[256,256]{1,0:T(8,128)S(1)}, f32[256,256]{1,0:T(8,128)}, u32[]{:S(2)}) copy-start(f32[256,256]{1,0:T(8,128)} %profile.3) | copy-start | bytes 786436
  19.4 8.1 %copy-start.3 = (f32[1,256,256]{2,1,0:T(8,128)S(1)}, f32[1,256,256]{2,1,0:T(8,128)}, u32[]{:S(2)}) copy-start(f32[1,256,256]{2,1,0:T(8,128)} %ham.1) | copy-start | bytes 786436
  19.4 8.1 %copy-start.4 = (f32[1,64,64]{2,1,0:T(8,128)S(1)}, f32[1,64,64]{2,1,0:T(8,128)}, u32[]{:S(2)}) copy-start(f32[1,64,64]{2,1,0:T(8,128)} %coup.1) | copy-start | bytes 49156
  20.5 7.0 %copy-start.9 = (s32[1,64]{1,0:T(1,128)S(1)}, s32[1,64]{1,0:T(1,128)}, u32[]{:S(2)}) copy-start(s32[1,64]{1,0:T(1,128)} %left.1) | copy-start | bytes 772
  20.5 14.1 %collective-permute-start.9 = (f32[264,256]{1,0:T(8,128)S(1)}, f32[264,256]{1,0:T(8,128)S(1)}, u32[]{:S(2)}, u32[]{:S(2)}) collective-permute-start(f32[264,256]{1,0:T(8,128)S(1)} %collective-permute-done.2.two), channel_id=1, source_target_pairs={{8,6},{14,16},{16,14},{22,24},{9,7},{15,17},{17,15},{23,25}} | collective-permute-start | bytes 811016 | tf_op jit(solution)/shard_map/ppermute | solution.py:193
  21.2 9.9 %collective-permute-start.8 = (f32[256,256]{1,0:T(8,128)S(1)}, f32[256,256]{1,0:T(8,128)S(1)}, u32[]{:S(2)}, u32[]{:S(2)}) collective-permute-start(f32[256,256]{1,0:T(8,128)S(1)} %shard_map.103), channel_id=1, source_target_pairs={{0,4},{2,6},{4,0},{6,2},{8,12},{10,14},{12,8},{14,10},{16,20},{18,... | collective-permute-start | bytes 786440 | tf_op jit(solution)/shard_map/ppermute | solution.py:193
  21.5 9.6 %collective-permute-start.10 = (f32[256,256]{1,0:T(8,128)S(1)}, f32[256,256]{1,0:T(8,128)S(1)}, u32[]{:S(2)}, u32[]{:S(2)}) collective-permute-start(f32[256,256]{1,0:T(8,128)S(1)} %get-tuple-element.38), channel_id=1, source_target_pairs={{0,8},{4,12},{8,16},{10,2},{12,20},{14,6},{16,24},{18,10},{20,28},... | collective-permute-start | bytes 786440 | tf_op jit(solution)/shard_map/ppermute | solution.py:193
  26.2 8.4 %collective-permute-start.11 = (f32[256,256]{1,0:T(8,128)S(1)}, f32[256,256]{1,0:T(8,128)S(1)}, u32[]{:S(2)}, u32[]{:S(2)}) collective-permute-start(f32[256,256]{1,0:T(8,128)S(1)} %get-tuple-element.39), channel_id=1, source_target_pairs={{2,10},{6,14},{8,0},{10,18},{12,4},{14,22},{16,8},{18,26},{20,12},... | collective-permute-start | bytes 786440 | tf_op jit(solution)/shard_map/ppermute | solution.py:193
  28.2 6.4 %copy-start.5 = (s32[1,64]{1,0:T(1,128)S(1)}, s32[1,64]{1,0:T(1,128)}, u32[]{:S(2)}) copy-start(s32[1,64]{1,0:T(1,128)} %right.3) | copy-start | bytes 772
  37.5 4.3 %collective-permute-start.12 = (f32[64,128]{1,0:T(8,128)S(1)}, f32[64,128]{1,0:T(8,128)S(1)}, u32[]{:S(2)}, u32[]{:S(2)}) collective-permute-start(f32[64,128]{1,0:T(8,128)S(1)} %get-tuple-element.46), channel_id=1, source_target_pairs={{0,1},{1,0},{2,3},{3,2},{4,5},{5,4},{6,7},{7,6},{8,9},{9,8},{10,11... | collective-permute-start | bytes 98312 | tf_op jit(solution)/shard_map/ppermute | solution.py:502
  42.4 4.9 %collective-permute-start.13 = (f32[64,128]{1,0:T(8,128)S(1)}, f32[64,128]{1,0:T(8,128)S(1)}, u32[]{:S(2)}, u32[]{:S(2)}) collective-permute-start(f32[64,128]{1,0:T(8,128)S(1)} %get-tuple-element.47), channel_id=1, source_target_pairs={{0,1},{1,0},{2,3},{3,2},{4,5},{5,4},{6,7},{7,6},{8,9},{9,8},{10,11... | collective-permute-start | bytes 98312 | tf_op jit(solution)/shard_map/ppermute | solution.py:502

commit v5 on v4

--- a/solution.py
+++ b/solution.py
@@ -156,7 +156,7 @@
     return s_e, s_q, e, q
 
 
-def full(a_re, a_im, s_e, s_q, e, q, scale):
+def full(a_re, a_im, s_e, s_q, e, q, store):
     h = herm(e, q)
     s_e = s_e + times(herm(s_e, s_q), h)
     e = times(h, h)
@@ -165,9 +165,8 @@
     s_p = s_e - s_q
     b, c = a_re.T, a_im.T
     one = mm(left3(b - c), right3(s_p))
-    g_re = one + mm(left3(c), right3(s_e))
-    g_im = one + mm(left3(b), right3(s_q - s_p))
-    return scale * g_re, scale * g_im
+    store(0, one + mm(left3(c), right3(s_e)))
+    store(1, one + mm(left3(b), right3(s_q - s_p)))
 
 
 ROWS = 8
@@ -235,7 +234,7 @@
             pltpu.SemaphoreType.DMA((6,)),
         ],
         compiler_params=pltpu.CompilerParams(vmem_limit_bytes=40 * 2**20),
-    )(energies, source, weight_index, table, green_prev)
+    )(energies, source, weight_index, table, pltpu.with_memory_space_constraint(green_prev, pltpu.HBM))
 
 
 def coef(rows, index):
@@ -340,10 +339,12 @@
 
 def whole(a_re, a_im, right, g_out, cols_out, rows_out):
     e, q, scale = begin(a_re, a_im)
-    g_re, g_im = full(a_re, a_im, *series_of(e, q), scale)
-    g_out[0] = g_re
-    g_out[1] = g_im
-    face_parts(g_re, g_im, right, cols_out, rows_out)
+
+    def store(k, part):
+        g_out[k] = part
+
+    full(scale * a_re, scale * a_im, *series_of(e, q), store)
+    face_parts(g_out[0], g_out[1], right, cols_out, rows_out)
 
 
 def slab_0_kernel(base, right, g_out, cols_out, rows_out):
@@ -367,7 +368,7 @@
         rows_out[...] = rows[...]
 
 
-def turn_kernel(slabs, base, placed, incoming, message_out, series_out, a_out, scale_out):
+def turn_kernel(slabs, base, placed, incoming, message_out, series_out, a_out):
     @pl.when(lax.axis_index("slab") == slabs - 1)
     def _():
         width, faces = placed.shape
@@ -377,9 +378,8 @@
         message_out[:, faces:] = m_im
         for k, part in enumerate(series):
             series_out[k] = part
-        a_out[0] = a_re
-        a_out[1] = a_im
-        scale_out[0] = scale
+        a_out[0] = scale * a_re
+        a_out[1] = scale * a_im
 
 
 def message_kernel(slabs, cols, rows, message, coup, left, right, base, message_out):
@@ -404,18 +404,21 @@
         message_out[...] = message[...]
 
 
-def last_full_kernel(slabs, scale, series, a_in, green_out, block, sems):
+def last_full_kernel(slabs, series, scaled, green_out, block, sems):
     @pl.when(lax.axis_index("slab") == slabs - 1)
     def _():
-        e, s_e = series[0], unit_of(a_in.shape[1]) + series[0]
+        e, s_e = series[0], unit_of(scaled.shape[1]) + series[0]
         for turn in range(1, DOUBLINGS - 1):
             e = series[turn]
             s_e = s_e + times(herm(s_e, skew(s_e)), herm(e, skew(e)))
         e = series[DOUBLINGS - 1]
-        block[0], block[1] = full(a_in[0], a_in[1], s_e, skew(s_e), e, skew(e), scale[0])
         copies = [pltpu.make_async_copy(block.at[k], green_out.at[0, 0, k], sems.at[k]) for k in range(2)]
-        for copy in copies:
-            copy.start()
+
+        def store(k, part):
+            block[k] = part
+            copies[k].start()
+
+        full(scaled[0], scaled[1], s_e, skew(s_e), e, skew(e), store)
         for copy in copies:
             copy.wait()
 
@@ -435,31 +438,29 @@
             copy.wait()
 
 
-def write_green(kernel, scalars, arrays, shape, given=None):
-    smem, vmem, hbm = (pl.BlockSpec(memory_space=space) for space in (pltpu.SMEM, pltpu.VMEM, pltpu.HBM))
+def write_green(kernel, arrays, shape, given=None):
+    vmem, hbm = (pl.BlockSpec(memory_space=space) for space in (pltpu.VMEM, pltpu.HBM))
     more = [] if given is None else [given]
-    inputs = len(scalars) + len(arrays)
     return pl.pallas_call(
         kernel,
         out_shape=jax.ShapeDtypeStruct(shape, f32),
-        in_specs=[smem] * len(scalars) + [vmem] * len(arrays) + [hbm] * len(more),
+        in_specs=[vmem] * len(arrays) + [hbm] * len(more),
         out_specs=hbm,
         scratch_shapes=[pltpu.VMEM(shape[2:], f32), pltpu.SemaphoreType.DMA((2,))],
-        input_output_aliases={inputs: 0} if more else {},
+        input_output_aliases={len(arrays): 0} if more else {},
         compiler_params=pltpu.CompilerParams(vmem_limit_bytes=40 * 2**20),
-    )(*scalars, *arrays, *more)
-
-
-def call(kernel, outs, scalars, *arrays, scalar_outs=()):
-    smem = pl.BlockSpec(memory_space=pltpu.SMEM)
+    )(*arrays, *more)
+
+
+def call(kernel, outs, *arrays):
     vmem = pl.BlockSpec(memory_space=pltpu.VMEM)
     return pl.pallas_call(
         kernel,
-        out_shape=[jax.ShapeDtypeStruct(shape, f32) for shape in (*outs, *scalar_outs)],
-        in_specs=[smem] * len(scalars) + [vmem] * len(arrays),
-        out_specs=[vmem] * len(outs) + [smem] * len(scalar_outs),
+        out_shape=[jax.ShapeDtypeStruct(shape, f32) for shape in outs],
+        in_specs=[vmem] * len(arrays),
+        out_specs=[vmem] * len(outs),
         compiler_params=pltpu.CompilerParams(vmem_limit_bytes=40 * 2**20),
-    )(*scalars, *arrays)
+    )(*arrays)
 
 
 def exchange(energies, hamiltonian, coupling, green_prev, profile, phonon_weights, source, weight_index, left_face):
@@ -481,9 +482,9 @@
     pair_one = sent(one, all_twin)
     pair_two = sent(two, all_twin)
     pair_x = sent(x, all_twin)
-    (over_x_sum,) = call(over_x_kernel, [block], [], re, pair, one, two, pair_one, pair_two, x)
+    (over_x_sum,) = call(over_x_kernel, [block], re, pair, one, two, pair_one, pair_two, x)
     sum_1, sum_2 = call(
-        groups_kernel, [block] * 2, [], im, pair, x, pair_x, near, one, two
+        groups_kernel, [block] * 2, im, pair, x, pair_x, near, one, two
     )
     two_later, sum_1, sum_2, over_x_sum = lax.optimization_barrier((two, sum_1, sum_2, over_x_sum))
     from_x = sent(over_x_sum, all_x)
@@ -491,7 +492,7 @@
     from_2 = sent(sum_2, all_2)
     far = sent(two_later, far_pairs)
     own, placed = call(
-        own_kernel, [(2, *block), (width, coupling.shape[1])], [],
+        own_kernel, [(2, *block), (width, coupling.shape[1])],
         re, im, pair, one, two, pair_one, pair_two, x, pair_x, hamiltonian, profile, coupling, left_face,
     )
     return placed, (own, re, profile, from_x, far, from_1, from_2)
@@ -512,30 +513,29 @@
     placed, parts = exchange(
         energies, hamiltonian, coupling, green_prev, profile, phonon_weights, source, weight_index, left_face
     )
-    face_sent, base = call(first_kernel, [face, (2, *block)], [], *parts, right_face)
+    face_sent, base = call(first_kernel, [face, (2, *block)], *parts, right_face)
     incoming = passed_along(face_sent, 1)
     for turn in range(1, slabs - 1):
-        (face_sent,) = call(face_kernel, [face], [], base, placed, incoming, right_face)
+        (face_sent,) = call(face_kernel, [face], base, placed, incoming, right_face)
         incoming = passed_along(face_sent, 1)
-    g, cols, rows = call(slab_0_kernel, parts_of_g, [], base, right_face)
+    g, cols, rows = call(slab_0_kernel, parts_of_g, base, right_face)
     placed, g = lax.optimization_barrier((placed, g))
     if slabs > 2:
         g, cols, rows = call(
-            functools.partial(middle_kernel, slabs), parts_of_g, [], base, placed, incoming, right_face, g, cols, rows
+            functools.partial(middle_kernel, slabs), parts_of_g, base, placed, incoming, right_face, g, cols, rows
         )
-    message, series, a, scale = call(
-        functools.partial(turn_kernel, slabs), [face, (4, *block), (2, *block)], [], base, placed, incoming,
-        scalar_outs=[(1,)],
+    message, series, scaled = call(
+        functools.partial(turn_kernel, slabs), [face, (DOUBLINGS, *block), (2, *block)], base, placed, incoming
     )
     incoming = passed_along(message, -1)
-    green = write_green(functools.partial(last_full_kernel, slabs), [scale], [series, a], green_prev.shape)
+    green = write_green(functools.partial(last_full_kernel, slabs), [series, scaled], green_prev.shape)
     for turn in range(2, slabs):
         (message,) = call(
-            functools.partial(message_kernel, slabs), [face], [],
+            functools.partial(message_kernel, slabs), [face],
             cols, rows, incoming, coupling, left_face, right_face, base,
         )
         incoming = passed_along(message, -1)
-    return write_green(functools.partial(last_kernel, slabs), [], [g, cols, rows, incoming], green_prev.shape, green)
+    return write_green(functools.partial(last_kernel, slabs), [g, cols, rows, incoming], green_prev.shape, green)
 
 
 def solution(mesh):

time: 49.1 us -> 47.9 us (0.976)
  local copies, waits for them, and re-layouts: 1.08 us -> 0.05 us
  Pallas kernels: 11.6 us -> 10.7 us
  waiting for transfers between devices: 9.74 us -> 10.6 us
    unnamed x20 -> x18, local copies, waits for them, and re-layouts: 1.08 us -> 0.05 us
    pallas_call x2, Pallas kernels: 2.15 us -> 1.32 us  [write_green(): pl.pallas_call(kernel, out_shape=jax.ShapeDtypeStruct(shape, f32), in_spe...]
    ppermute x2, waiting for transfers between devices: 1.05 us -> 1.87 us  [passed_along(): lax.ppermute(value, 'slab', [(start, (start + steps) % count) for start i...]
    pallas_call x6, Pallas kernels: 8.81 us -> 8.27 us  [call(): pl.pallas_call(kernel, out_shape=[jax.ShapeDtypeStruct(shape, f32) for sh...]
  transfers between devices with their start and end apart: 14 -> 14, of which waited for: 6 -> 6; matrix products, arithmetic and copies ran while one was open for 0% -> 0% of each run, Pallas kernels for 12% -> 11%
where the time goes in v5:
time: 47.9 us; the launch traced here: 47.7 us
  starting transfers between devices  25.3 us (53%)
  Pallas kernels  10.7 us (22%)
  waiting for transfers between devices  10.6 us (22%)
  between operations  1.1 us (2%)
    ppermute x12, starting transfers between devices, sent(): return lax.ppermute(value, 'energy', pairs)  22.2 us
    ppermute x12, waiting for transfers between devices, sent(): return lax.ppermute(value, 'energy', pairs)  8.69 us
    pallas_call x6, Pallas kernels, call(): pl.pallas_call(kernel, out_shape=[jax.ShapeDtypeStruct(shape, f32) for sh...  8.27 us
    ppermute x2, starting transfers between devices, passed_along(): lax.ppermute(value, 'slab', [(start, (start + steps) % count) for start i...  3.08 us
    ppermute x2, waiting for transfers between devices, passed_along(): lax.ppermute(value, 'slab', [(start, (start + steps) % count) for start i...  1.87 us
    pallas_call x2, Pallas kernels, write_green(): pl.pallas_call(kernel, out_shape=jax.ShapeDtypeStruct(shape, f32), in_spe...  1.32 us
    pallas_call x1, Pallas kernels, pack(): pl.pallas_call(pack_kernel, out_shape=[jax.ShapeDtypeStruct((width + ROWS...  1.09 us
  transfers between devices with their start and end apart: 14, of which 6 were waited for; matrix products, arithmetic and copies ran while one was open for 0% of the time, Pallas kernels for 11%

profile of v5, /device:TPU:0, one launch (start us, length us, event | category | flops | bytes accessed | tf_op | source)
XLA Modules:
  0.0 47.7 jit_solution(18109700374438880664)
XLA Ops:
  0.7 1.1 %shard_map.100 = (f32[264,256]{1,0:T(8,128)S(1)}, f32[264,256]{1,0:T(8,128)S(1)}) custom-call(f32[1]{0:T(128)S(6)} %copy.13.energy_hbm, s32[1,2]{1,0:T(1,128)S(1)} %copy-done.4, s32[1,2]{1,0:T(1,128)S(1)} %copy-done.5, f32[8]{0:T(128)S(1)} %copy-done.6, f32[1,1,2,256,256]{4,3,2,1,0:T(8,128)} %green.1), custom_call_target="tpu_custom_call" | custom-call | tf_op jit(solution)/shard_map/pallas_call | solution.py:226
  1.8 0.7 %collective-permute-start.6 = (f32[264,256]{1,0:T(8,128)S(1)}, f32[264,256]{1,0:T(8,128)S(1)}, u32[]{:S(2)}, u32[]{:S(2)}) collective-permute-start(f32[264,256]{1,0:T(8,128)S(1)} %get-tuple-element.28.im), channel_id=1, source_target_pairs={{16,14},{24,22},{6,8},{14,16},{17,15},{25,23},{7,9},{15,17}} | collective-permute-start | bytes 811016 | tf_op jit(solution)/shard_map/ppermute | solution.py:192
  2.5 3.0 %collective-permute-start.5 = (f32[264,256]{1,0:T(8,128)S(1)}, f32[264,256]{1,0:T(8,128)S(1)}, u32[]{:S(2)}, u32[]{:S(2)}) collective-permute-start(f32[264,256]{1,0:T(8,128)S(1)} %get-tuple-element.28.im), channel_id=1, source_target_pairs={{0,4},{2,6},{4,0},{6,2},{8,12},{10,14},{12,8},{14,10},{16,20},{18,... | collective-permute-start | bytes 811016 | tf_op jit(solution)/shard_map/ppermute | solution.py:192
  5.5 1.3 %collective-permute-start.2 = (f32[264,256]{1,0:T(8,128)S(1)}, f32[264,256]{1,0:T(8,128)S(1)}, u32[]{:S(2)}, u32[]{:S(2)}) collective-permute-start(f32[264,256]{1,0:T(8,128)S(1)} %get-tuple-element.27.re), channel_id=1, source_target_pairs={{2,10},{6,14},{8,0},{10,18},{12,4},{14,22},{16,8},{18,26},{20,12},... | collective-permute-start | bytes 811016 | tf_op jit(solution)/shard_map/ppermute | solution.py:192
  6.8 4.6 %collective-permute-start.1 = (f32[264,256]{1,0:T(8,128)S(1)}, f32[264,256]{1,0:T(8,128)S(1)}, u32[]{:S(2)}, u32[]{:S(2)}) collective-permute-start(f32[264,256]{1,0:T(8,128)S(1)} %get-tuple-element.27.re), channel_id=1, source_target_pairs={{0,8},{4,12},{8,16},{10,2},{12,20},{14,6},{16,24},{18,10},{20,28},... | collective-permute-start | bytes 811016 | tf_op jit(solution)/shard_map/ppermute | solution.py:192
  11.4 1.3 %collective-permute-start = (f32[1,1,2,256,256]{4,3,2,1,0:T(8,128)S(1)}, f32[1,1,2,256,256]{4,3,2,1,0:T(8,128)S(1)}, u32[]{:S(2)}, u32[]{:S(2)}) collective-permute-start(f32[1,1,2,256,256]{4,3,2,1,0:T(8,128)S(1)} %copy-done.8), channel_id=1, source_target_pairs={{0,2},{2,0},{4,6},{6,4},{8,10},{10,8},{12,14},{14,12},{16,18},{18,... | collective-permute-start | bytes 1572872 | tf_op jit(solution)/shard_map/ppermute | solution.py:192
  13.0 0.9 %collective-permute-done.2.two = f32[264,256]{1,0:T(8,128)S(1)} collective-permute-done((f32[264,256]{1,0:T(8,128)S(1)}, f32[264,256]{1,0:T(8,128)S(1)}, u32[]{:S(2)}, u32[]{:S(2)}) %collective-permute-start.2) | collective-permute-done | bytes 270368 | tf_op jit(solution)/shard_map/ppermute | solution.py:192
  13.9 3.1 %collective-permute-start.4 = (f32[264,256]{1,0:T(8,128)S(1)}, f32[264,256]{1,0:T(8,128)S(1)}, u32[]{:S(2)}, u32[]{:S(2)}) collective-permute-start(f32[264,256]{1,0:T(8,128)S(1)} %collective-permute-done.2.two), channel_id=1, source_target_pairs={{0,2},{2,0},{4,6},{6,4},{8,10},{10,8},{12,14},{14,12},{16,18},{18,... | collective-permute-start | bytes 811016 | tf_op jit(solution)/shard_map/ppermute | solution.py:192
  17.0 0.6 %collective-permute-done.1.one = f32[264,256]{1,0:T(8,128)S(1)} collective-permute-done((f32[264,256]{1,0:T(8,128)S(1)}, f32[264,256]{1,0:T(8,128)S(1)}, u32[]{:S(2)}, u32[]{:S(2)}) %collective-permute-start.1) | collective-permute-done | bytes 270368 | tf_op jit(solution)/shard_map/ppermute | solution.py:192
  17.5 1.1 %collective-permute-start.3 = (f32[264,256]{1,0:T(8,128)S(1)}, f32[264,256]{1,0:T(8,128)S(1)}, u32[]{:S(2)}, u32[]{:S(2)}) collective-permute-start(f32[264,256]{1,0:T(8,128)S(1)} %collective-permute-done.1.one), channel_id=1, source_target_pairs={{0,2},{2,0},{4,6},{6,4},{8,10},{10,8},{12,14},{14,12},{16,18},{18,... | collective-permute-start | bytes 811016 | tf_op jit(solution)/shard_map/ppermute | solution.py:192
  18.6 0.2 shard_map.102
  18.9 0.9 %collective-permute-done.3.pair_one = f32[264,256]{1,0:T(8,128)S(1)} collective-permute-done((f32[264,256]{1,0:T(8,128)S(1)}, f32[264,256]{1,0:T(8,128)S(1)}, u32[]{:S(2)}, u32[]{:S(2)}) %collective-permute-start.3) | collective-permute-done | bytes 270368 | tf_op jit(solution)/shard_map/ppermute | solution.py:192
  19.9 0.7 %collective-permute-start.9 = (f32[264,256]{1,0:T(8,128)S(1)}, f32[264,256]{1,0:T(8,128)S(1)}, u32[]{:S(2)}, u32[]{:S(2)}) collective-permute-start(f32[264,256]{1,0:T(8,128)S(1)} %collective-permute-done.2.two), channel_id=1, source_target_pairs={{8,6},{14,16},{16,14},{22,24},{9,7},{15,17},{17,15},{23,25}} | collective-permute-start | bytes 811016 | tf_op jit(solution)/shard_map/ppermute | solution.py:192
  20.6 0.4 collective-permute-start.8
  21.0 4.6 %collective-permute-start.10 = (f32[256,256]{1,0:T(8,128)S(1)}, f32[256,256]{1,0:T(8,128)S(1)}, u32[]{:S(2)}, u32[]{:S(2)}) collective-permute-start(f32[256,256]{1,0:T(8,128)S(1)} %get-tuple-element.37), channel_id=1, source_target_pairs={{0,8},{4,12},{8,16},{10,2},{12,20},{14,6},{16,24},{18,10},{20,28},... | collective-permute-start | bytes 786440 | tf_op jit(solution)/shard_map/ppermute | solution.py:192
  25.6 1.3 %collective-permute-start.11 = (f32[256,256]{1,0:T(8,128)S(1)}, f32[256,256]{1,0:T(8,128)S(1)}, u32[]{:S(2)}, u32[]{:S(2)}) collective-permute-start(f32[256,256]{1,0:T(8,128)S(1)} %get-tuple-element.38), channel_id=1, source_target_pairs={{2,10},{6,14},{8,0},{10,18},{12,4},{14,22},{16,8},{18,26},{20,12},... | collective-permute-start | bytes 786440 | tf_op jit(solution)/shard_map/ppermute | solution.py:192
  26.9 0.7 %shard_map.101 = (f32[2,256,256]{2,1,0:T(8,128)S(1)}, f32[256,64]{1,0:T(8,128)S(1)}) custom-call(f32[264,256]{1,0:T(8,128)S(1)} %get-tuple-element.27.re, f32[264,256]{1,0:T(8,128)S(1)} %get-tuple-element.28.im, f32[1,1,2,256,256]{4,3,2,1,0:T(8,128)S(1)} %collective-permute-done.twin_block, f32[264,256]{1,0:T(8,128)S(1)} %collective-permute-done.1.one, ...), custom_call_target="tpu_custom_call" | custom-call | tf_op jit(solution)/shard_map/pallas_call | solution.py:457
  27.6 2.9 %collective-permute-done.8.from_x = f32[256,256]{1,0:T(8,128)S(1)} collective-permute-done((f32[256,256]{1,0:T(8,128)S(1)}, f32[256,256]{1,0:T(8,128)S(1)}, u32[]{:S(2)}, u32[]{:S(2)}) %collective-permute-start.8) | collective-permute-done | bytes 262176 | tf_op jit(solution)/shard_map/ppermute | solution.py:192
  30.6 3.4 %collective-permute-done.11.from_2 = f32[256,256]{1,0:T(8,128)S(1)} collective-permute-done((f32[256,256]{1,0:T(8,128)S(1)}, f32[256,256]{1,0:T(8,128)S(1)}, u32[]{:S(2)}, u32[]{:S(2)}) %collective-permute-start.11) | collective-permute-done | bytes 262176 | tf_op jit(solution)/shard_map/ppermute | solution.py:192
  34.0 3.0 %shard_map.104 = (f32[64,128]{1,0:T(8,128)S(1)}, f32[2,256,256]{2,1,0:T(8,128)S(1)}) custom-call(f32[2,256,256]{2,1,0:T(8,128)S(1)} %get-tuple-element.31.own, f32[264,256]{1,0:T(8,128)S(1)} %get-tuple-element.27.re, f32[256,256]{1,0:T(8,128)S(1)} %copy-done, f32[256,256]{1,0:T(8,128)S(1)} %collective-permute-done.8.from_x, ...), custom_call_target="tpu_custom_call" | custom-call | tf_op jit(solution)/shard_map/pallas_call | solution.py:457
  37.0 4.2 %shard_map.105 = (f32[2,256,256]{2,1,0:T(8,128)S(1)}, f32[512,64]{1,0:T(8,128)S(1)}, f32[64,512]{1,0:T(8,128)S(1)}) custom-call(f32[2,256,256]{2,1,0:T(8,128)S(1)} %get-tuple-element.39.base, s32[1,64]{1,0:T(1,128)S(1)} %copy-done.3), custom_call_target="tpu_custom_call" | custom-call | tf_op jit(solution)/shard_map/pallas_call | solution.py:457
  41.3 3.0 %collective-permute-start.13 = (f32[64,128]{1,0:T(8,128)S(1)}, f32[64,128]{1,0:T(8,128)S(1)}, u32[]{:S(2)}, u32[]{:S(2)}) collective-permute-start(f32[64,128]{1,0:T(8,128)S(1)} %get-tuple-element.46), channel_id=1, source_target_pairs={{0,1},{1,0},{2,3},{3,2},{4,5},{5,4},{6,7},{7,6},{8,9},{9,8},{10,11... | collective-permute-start | bytes 98312 | tf_op jit(solution)/shard_map/ppermute | solution.py:503
  44.3 1.9 %collective-permute-done.13.message = f32[64,128]{1,0:T(8,128)S(1)} collective-permute-done((f32[64,128]{1,0:T(8,128)S(1)}, f32[64,128]{1,0:T(8,128)S(1)}, u32[]{:S(2)}, u32[]{:S(2)}) %collective-permute-start.13) | collective-permute-done | bytes 32800 | tf_op jit(solution)/shard_map/ppermute | solution.py:503
  46.2 1.3 %shard_map.108 = f32[1,1,2,256,256]{4,3,2,1,0:T(8,128)} custom-call(f32[2,256,256]{2,1,0:T(8,128)S(1)} %get-tuple-element.41.g, f32[512,64]{1,0:T(8,128)S(1)} %get-tuple-element.42.cols, f32[64,512]{1,0:T(8,128)S(1)} %get-tuple-element.43.rows, f32[64,128]{1,0:T(8,128)S(1)} %collective-permute-done.13.message, ...), custom_call_target="tpu_custom_call", output_to_operand_aliasing={{}: (4, {})} | custom-call | tf_op jit(solution)/shard_map/pallas_call | solution.py:444
  (31 shorter events, 0.5 us)
Async XLA Ops:
  0.0 0.7 %copy-start.5 = (s32[1,2]{1,0:T(1,128)S(1)}, s32[1,2]{1,0:T(1,128)}, u32[]{:S(2)}) copy-start(s32[1,2]{1,0:T(1,128)} %index_hbm.1) | copy-start | bytes 28
  0.0 0.7 %copy-start.4 = (s32[1,2]{1,0:T(1,128)S(1)}, s32[1,2]{1,0:T(1,128)}, u32[]{:S(2)}) copy-start(s32[1,2]{1,0:T(1,128)} %source_hbm.1) | copy-start | bytes 28
  0.0 0.7 %copy-start.6 = (f32[8]{0:T(128)S(1)}, f32[8]{0:T(128)}, u32[]{:S(2)}) copy-start(f32[8]{0:T(128)} %table_hbm.1) | copy-start | bytes 100
  0.0 11.4 %copy-start.8 = (f32[1,1,2,256,256]{4,3,2,1,0:T(8,128)S(1)}, f32[1,1,2,256,256]{4,3,2,1,0:T(8,128)}, u32[]{:S(2)}) copy-start(f32[1,1,2,256,256]{4,3,2,1,0:T(8,128)} %green.1) | copy-start | bytes 1572868
  1.8 10.9 %collective-permute-start.6 = (f32[264,256]{1,0:T(8,128)S(1)}, f32[264,256]{1,0:T(8,128)S(1)}, u32[]{:S(2)}, u32[]{:S(2)}) collective-permute-start(f32[264,256]{1,0:T(8,128)S(1)} %get-tuple-element.28.im), channel_id=1, source_target_pairs={{16,14},{24,22},{6,8},{14,16},{17,15},{25,23},{7,9},{15,17}} | collective-permute-start | bytes 811016 | tf_op jit(solution)/shard_map/ppermute | solution.py:192
  2.5 10.2 %collective-permute-start.5 = (f32[264,256]{1,0:T(8,128)S(1)}, f32[264,256]{1,0:T(8,128)S(1)}, u32[]{:S(2)}, u32[]{:S(2)}) collective-permute-start(f32[264,256]{1,0:T(8,128)S(1)} %get-tuple-element.28.im), channel_id=1, source_target_pairs={{0,4},{2,6},{4,0},{6,2},{8,12},{10,14},{12,8},{14,10},{16,20},{18,... | collective-permute-start | bytes 811016 | tf_op jit(solution)/shard_map/ppermute | solution.py:192
  5.5 8.3 %collective-permute-start.2 = (f32[264,256]{1,0:T(8,128)S(1)}, f32[264,256]{1,0:T(8,128)S(1)}, u32[]{:S(2)}, u32[]{:S(2)}) collective-permute-start(f32[264,256]{1,0:T(8,128)S(1)} %get-tuple-element.27.re), channel_id=1, source_target_pairs={{2,10},{6,14},{8,0},{10,18},{12,4},{14,22},{16,8},{18,26},{20,12},... | collective-permute-start | bytes 811016 | tf_op jit(solution)/shard_map/ppermute | solution.py:192
  6.8 10.7 %collective-permute-start.1 = (f32[264,256]{1,0:T(8,128)S(1)}, f32[264,256]{1,0:T(8,128)S(1)}, u32[]{:S(2)}, u32[]{:S(2)}) collective-permute-start(f32[264,256]{1,0:T(8,128)S(1)} %get-tuple-element.27.re), channel_id=1, source_target_pairs={{0,8},{4,12},{8,16},{10,2},{12,20},{14,6},{16,24},{18,10},{20,28},... | collective-permute-start | bytes 811016 | tf_op jit(solution)/shard_map/ppermute | solution.py:192
  11.4 7.2 %collective-permute-start = (f32[1,1,2,256,256]{4,3,2,1,0:T(8,128)S(1)}, f32[1,1,2,256,256]{4,3,2,1,0:T(8,128)S(1)}, u32[]{:S(2)}, u32[]{:S(2)}) collective-permute-start(f32[1,1,2,256,256]{4,3,2,1,0:T(8,128)S(1)} %copy-done.8), channel_id=1, source_target_pairs={{0,2},{2,0},{4,6},{6,4},{8,10},{10,8},{12,14},{14,12},{16,18},{18,... | collective-permute-start | bytes 1572872 | tf_op jit(solution)/shard_map/ppermute | solution.py:192
  12.7 5.8 %collective-permute-start.7 = (f32[264,256]{1,0:T(8,128)S(1)}, f32[264,256]{1,0:T(8,128)S(1)}, u32[]{:S(2)}, u32[]{:S(2)}) collective-permute-start(f32[264,256]{1,0:T(8,128)S(1)} %collective-permute-done.5.x), channel_id=1, source_target_pairs={{0,2},{2,0},{4,6},{6,4},{8,10},{10,8},{12,14},{14,12},{16,18},{18,... | collective-permute-start | bytes 811016 | tf_op jit(solution)/shard_map/ppermute | solution.py:192
  13.9 5.0 %collective-permute-start.4 = (f32[264,256]{1,0:T(8,128)S(1)}, f32[264,256]{1,0:T(8,128)S(1)}, u32[]{:S(2)}, u32[]{:S(2)}) collective-permute-start(f32[264,256]{1,0:T(8,128)S(1)} %collective-permute-done.2.two), channel_id=1, source_target_pairs={{0,2},{2,0},{4,6},{6,4},{8,10},{10,8},{12,14},{14,12},{16,18},{18,... | collective-permute-start | bytes 811016 | tf_op jit(solution)/shard_map/ppermute | solution.py:192
  17.5 2.2 %collective-permute-start.3 = (f32[264,256]{1,0:T(8,128)S(1)}, f32[264,256]{1,0:T(8,128)S(1)}, u32[]{:S(2)}, u32[]{:S(2)}) collective-permute-start(f32[264,256]{1,0:T(8,128)S(1)} %collective-permute-done.1.one), channel_id=1, source_target_pairs={{0,2},{2,0},{4,6},{6,4},{8,10},{10,8},{12,14},{14,12},{16,18},{18,... | collective-permute-start | bytes 811016 | tf_op jit(solution)/shard_map/ppermute | solution.py:192
  18.8 8.1 %copy-start = (f32[256,256]{1,0:T(8,128)S(1)}, f32[256,256]{1,0:T(8,128)}, u32[]{:S(2)}) copy-start(f32[256,256]{1,0:T(8,128)} %profile.3) | copy-start | bytes 786436
  18.8 8.1 %copy-start.1 = (f32[1,256,256]{2,1,0:T(8,128)S(1)}, f32[1,256,256]{2,1,0:T(8,128)}, u32[]{:S(2)}) copy-start(f32[1,256,256]{2,1,0:T(8,128)} %ham.1) | copy-start | bytes 786436
  18.9 8.1 %copy-start.2 = (f32[1,64,64]{2,1,0:T(8,128)S(1)}, f32[1,64,64]{2,1,0:T(8,128)}, u32[]{:S(2)}) copy-start(f32[1,64,64]{2,1,0:T(8,128)} %coup.1) | copy-start | bytes 49156
  19.9 7.0 %copy-start.7 = (s32[1,64]{1,0:T(1,128)S(1)}, s32[1,64]{1,0:T(1,128)}, u32[]{:S(2)}) copy-start(s32[1,64]{1,0:T(1,128)} %left.1) | copy-start | bytes 772
  19.9 14.1 %collective-permute-start.9 = (f32[264,256]{1,0:T(8,128)S(1)}, f32[264,256]{1,0:T(8,128)S(1)}, u32[]{:S(2)}, u32[]{:S(2)}) collective-permute-start(f32[264,256]{1,0:T(8,128)S(1)} %collective-permute-done.2.two), channel_id=1, source_target_pairs={{8,6},{14,16},{16,14},{22,24},{9,7},{15,17},{17,15},{23,25}} | collective-permute-start | bytes 811016 | tf_op jit(solution)/shard_map/ppermute | solution.py:192
  20.6 9.9 %collective-permute-start.8 = (f32[256,256]{1,0:T(8,128)S(1)}, f32[256,256]{1,0:T(8,128)S(1)}, u32[]{:S(2)}, u32[]{:S(2)}) collective-permute-start(f32[256,256]{1,0:T(8,128)S(1)} %shard_map.103), channel_id=1, source_target_pairs={{0,4},{2,6},{4,0},{6,2},{8,12},{10,14},{12,8},{14,10},{16,20},{18,... | collective-permute-start | bytes 786440 | tf_op jit(solution)/shard_map/ppermute | solution.py:192
  21.0 9.6 %collective-permute-start.10 = (f32[256,256]{1,0:T(8,128)S(1)}, f32[256,256]{1,0:T(8,128)S(1)}, u32[]{:S(2)}, u32[]{:S(2)}) collective-permute-start(f32[256,256]{1,0:T(8,128)S(1)} %get-tuple-element.37), channel_id=1, source_target_pairs={{0,8},{4,12},{8,16},{10,2},{12,20},{14,6},{16,24},{18,10},{20,28},... | collective-permute-start | bytes 786440 | tf_op jit(solution)/shard_map/ppermute | solution.py:192
  25.6 8.4 %collective-permute-start.11 = (f32[256,256]{1,0:T(8,128)S(1)}, f32[256,256]{1,0:T(8,128)S(1)}, u32[]{:S(2)}, u32[]{:S(2)}) collective-permute-start(f32[256,256]{1,0:T(8,128)S(1)} %get-tuple-element.38), channel_id=1, source_target_pairs={{2,10},{6,14},{8,0},{10,18},{12,4},{14,22},{16,8},{18,26},{20,12},... | collective-permute-start | bytes 786440 | tf_op jit(solution)/shard_map/ppermute | solution.py:192
  27.6 6.4 %copy-start.3 = (s32[1,64]{1,0:T(1,128)S(1)}, s32[1,64]{1,0:T(1,128)}, u32[]{:S(2)}) copy-start(s32[1,64]{1,0:T(1,128)} %right.3) | copy-start | bytes 772
  37.0 4.3 %collective-permute-start.12 = (f32[64,128]{1,0:T(8,128)S(1)}, f32[64,128]{1,0:T(8,128)S(1)}, u32[]{:S(2)}, u32[]{:S(2)}) collective-permute-start(f32[64,128]{1,0:T(8,128)S(1)} %get-tuple-element.45), channel_id=1, source_target_pairs={{0,1},{1,0},{2,3},{3,2},{4,5},{5,4},{6,7},{7,6},{8,9},{9,8},{10,11... | collective-permute-start | bytes 98312 | tf_op jit(solution)/shard_map/ppermute | solution.py:503
  41.3 4.9 %collective-permute-start.13 = (f32[64,128]{1,0:T(8,128)S(1)}, f32[64,128]{1,0:T(8,128)S(1)}, u32[]{:S(2)}, u32[]{:S(2)}) collective-permute-start(f32[64,128]{1,0:T(8,128)S(1)} %get-tuple-element.46), channel_id=1, source_target_pairs={{0,1},{1,0},{2,3},{3,2},{4,5},{5,4},{6,7},{7,6},{8,9},{9,8},{10,11... | collective-permute-start | bytes 98312 | tf_op jit(solution)/shard_map/ppermute | solution.py:503

commit v6 on v5

--- a/solution.py
+++ b/solution.py
@@ -382,10 +382,10 @@
         a_out[1] = scale * a_im
 
 
-def message_kernel(slabs, cols, rows, message, coup, left, right, base, message_out):
+def message_kernel(slabs, cols, message, own, coup, left, right, base, message_out):
     width, faces = base.shape[1], coup.shape[1]
     hot = one_hot(width, right[...])
-    f = mm(twice(hot.T, 1), pair(cols[...].reshape(2 * width, faces)[:width], 0))
+    f = mm(twice(hot.T, 1), pair(cols[:width], 0))
     f_im = mm(twice(hot.T, 1), pair(cols[width:], 0))
     order = mm(one_hot(width, left[...]), hot, TN).astype(bf16)
     mixed = mm(pair(coup[0], 1), twice(order, 0))
@@ -401,7 +401,7 @@
 
     @pl.when(is_last)
     def _():
-        message_out[...] = message[...]
+        message_out[...] = own[...]
 
 
 def last_full_kernel(slabs, series, scaled, green_out, block, sems):
@@ -532,7 +532,7 @@
     for turn in range(2, slabs):
         (message,) = call(
             functools.partial(message_kernel, slabs), [face],
-            cols, rows, incoming, coupling, left_face, right_face, base,
+            cols, incoming, message, coupling, left_face, right_face, base,
         )
         incoming = passed_along(message, -1)
     return write_green(functools.partial(last_kernel, slabs), [g, cols, rows, incoming], green_prev.shape, green)

time: 47.9 us -> 47.9 us (level)
  no operation moved by 1% of the time
where the time goes in v6:
time: 47.9 us; the launch traced here: 47.7 us
  starting transfers between devices  25.3 us (53%)
  Pallas kernels  10.7 us (22%)
  waiting for transfers between devices  10.6 us (22%)
  between operations  1.1 us (2%)
    ppermute x12, starting transfers between devices, sent(): return lax.ppermute(value, 'energy', pairs)  22.2 us
    ppermute x12, waiting for transfers between devices, sent(): return lax.ppermute(value, 'energy', pairs)  8.69 us
    pallas_call x6, Pallas kernels, call(): pl.pallas_call(kernel, out_shape=[jax.ShapeDtypeStruct(shape, f32) for sh...  8.27 us
    ppermute x2, starting transfers between devices, passed_along(): lax.ppermute(value, 'slab', [(start, (start + steps) % count) for start i...  3.08 us
    ppermute x2, waiting for transfers between devices, passed_along(): lax.ppermute(value, 'slab', [(start, (start + steps) % count) for start i...  1.87 us
    pallas_call x2, Pallas kernels, write_green(): pl.pallas_call(kernel, out_shape=jax.ShapeDtypeStruct(shape, f32), in_spe...  1.32 us
    pallas_call x1, Pallas kernels, pack(): pl.pallas_call(pack_kernel, out_shape=[jax.ShapeDtypeStruct((width + ROWS...  1.09 us
  transfers between devices with their start and end apart: 14, of which 6 were waited for; matrix products, arithmetic and copies ran while one was open for 0% of the time, Pallas kernels for 11%

profile of v6, /device:TPU:0, one launch (start us, length us, event | category | flops | bytes accessed | tf_op | source)
XLA Modules:
  0.0 47.7 jit_solution(18109700374438880664)
XLA Ops:
  0.7 1.1 %shard_map.100 = (f32[264,256]{1,0:T(8,128)S(1)}, f32[264,256]{1,0:T(8,128)S(1)}) custom-call(f32[1]{0:T(128)S(6)} %copy.13.energy_hbm, s32[1,2]{1,0:T(1,128)S(1)} %copy-done.4, s32[1,2]{1,0:T(1,128)S(1)} %copy-done.5, f32[8]{0:T(128)S(1)} %copy-done.6, f32[1,1,2,256,256]{4,3,2,1,0:T(8,128)} %green.1), custom_call_target="tpu_custom_call" | custom-call | tf_op jit(solution)/shard_map/pallas_call | solution.py:226
  1.8 0.7 %collective-permute-start.6 = (f32[264,256]{1,0:T(8,128)S(1)}, f32[264,256]{1,0:T(8,128)S(1)}, u32[]{:S(2)}, u32[]{:S(2)}) collective-permute-start(f32[264,256]{1,0:T(8,128)S(1)} %get-tuple-element.28.im), channel_id=1, source_target_pairs={{16,14},{24,22},{6,8},{14,16},{17,15},{25,23},{7,9},{15,17}} | collective-permute-start | bytes 811016 | tf_op jit(solution)/shard_map/ppermute | solution.py:192
  2.5 3.0 %collective-permute-start.5 = (f32[264,256]{1,0:T(8,128)S(1)}, f32[264,256]{1,0:T(8,128)S(1)}, u32[]{:S(2)}, u32[]{:S(2)}) collective-permute-start(f32[264,256]{1,0:T(8,128)S(1)} %get-tuple-element.28.im), channel_id=1, source_target_pairs={{0,4},{2,6},{4,0},{6,2},{8,12},{10,14},{12,8},{14,10},{16,20},{18,... | collective-permute-start | bytes 811016 | tf_op jit(solution)/shard_map/ppermute | solution.py:192
  5.5 1.3 %collective-permute-start.2 = (f32[264,256]{1,0:T(8,128)S(1)}, f32[264,256]{1,0:T(8,128)S(1)}, u32[]{:S(2)}, u32[]{:S(2)}) collective-permute-start(f32[264,256]{1,0:T(8,128)S(1)} %get-tuple-element.27.re), channel_id=1, source_target_pairs={{2,10},{6,14},{8,0},{10,18},{12,4},{14,22},{16,8},{18,26},{20,12},... | collective-permute-start | bytes 811016 | tf_op jit(solution)/shard_map/ppermute | solution.py:192
  6.8 4.6 %collective-permute-start.1 = (f32[264,256]{1,0:T(8,128)S(1)}, f32[264,256]{1,0:T(8,128)S(1)}, u32[]{:S(2)}, u32[]{:S(2)}) collective-permute-start(f32[264,256]{1,0:T(8,128)S(1)} %get-tuple-element.27.re), channel_id=1, source_target_pairs={{0,8},{4,12},{8,16},{10,2},{12,20},{14,6},{16,24},{18,10},{20,28},... | collective-permute-start | bytes 811016 | tf_op jit(solution)/shard_map/ppermute | solution.py:192
  11.4 1.3 %collective-permute-start = (f32[1,1,2,256,256]{4,3,2,1,0:T(8,128)S(1)}, f32[1,1,2,256,256]{4,3,2,1,0:T(8,128)S(1)}, u32[]{:S(2)}, u32[]{:S(2)}) collective-permute-start(f32[1,1,2,256,256]{4,3,2,1,0:T(8,128)S(1)} %copy-done.8), channel_id=1, source_target_pairs={{0,2},{2,0},{4,6},{6,4},{8,10},{10,8},{12,14},{14,12},{16,18},{18,... | collective-permute-start | bytes 1572872 | tf_op jit(solution)/shard_map/ppermute | solution.py:192
  13.0 0.9 %collective-permute-done.2.two = f32[264,256]{1,0:T(8,128)S(1)} collective-permute-done((f32[264,256]{1,0:T(8,128)S(1)}, f32[264,256]{1,0:T(8,128)S(1)}, u32[]{:S(2)}, u32[]{:S(2)}) %collective-permute-start.2) | collective-permute-done | bytes 270368 | tf_op jit(solution)/shard_map/ppermute | solution.py:192
  13.9 3.1 %collective-permute-start.4 = (f32[264,256]{1,0:T(8,128)S(1)}, f32[264,256]{1,0:T(8,128)S(1)}, u32[]{:S(2)}, u32[]{:S(2)}) collective-permute-start(f32[264,256]{1,0:T(8,128)S(1)} %collective-permute-done.2.two), channel_id=1, source_target_pairs={{0,2},{2,0},{4,6},{6,4},{8,10},{10,8},{12,14},{14,12},{16,18},{18,... | collective-permute-start | bytes 811016 | tf_op jit(solution)/shard_map/ppermute | solution.py:192
  17.0 0.6 %collective-permute-done.1.one = f32[264,256]{1,0:T(8,128)S(1)} collective-permute-done((f32[264,256]{1,0:T(8,128)S(1)}, f32[264,256]{1,0:T(8,128)S(1)}, u32[]{:S(2)}, u32[]{:S(2)}) %collective-permute-start.1) | collective-permute-done | bytes 270368 | tf_op jit(solution)/shard_map/ppermute | solution.py:192
  17.5 1.1 %collective-permute-start.3 = (f32[264,256]{1,0:T(8,128)S(1)}, f32[264,256]{1,0:T(8,128)S(1)}, u32[]{:S(2)}, u32[]{:S(2)}) collective-permute-start(f32[264,256]{1,0:T(8,128)S(1)} %collective-permute-done.1.one), channel_id=1, source_target_pairs={{0,2},{2,0},{4,6},{6,4},{8,10},{10,8},{12,14},{14,12},{16,18},{18,... | collective-permute-start | bytes 811016 | tf_op jit(solution)/shard_map/ppermute | solution.py:192
  18.6 0.2 shard_map.102
  18.9 0.9 %collective-permute-done.3.pair_one = f32[264,256]{1,0:T(8,128)S(1)} collective-permute-done((f32[264,256]{1,0:T(8,128)S(1)}, f32[264,256]{1,0:T(8,128)S(1)}, u32[]{:S(2)}, u32[]{:S(2)}) %collective-permute-start.3) | collective-permute-done | bytes 270368 | tf_op jit(solution)/shard_map/ppermute | solution.py:192
  19.9 0.7 %collective-permute-start.9 = (f32[264,256]{1,0:T(8,128)S(1)}, f32[264,256]{1,0:T(8,128)S(1)}, u32[]{:S(2)}, u32[]{:S(2)}) collective-permute-start(f32[264,256]{1,0:T(8,128)S(1)} %collective-permute-done.2.two), channel_id=1, source_target_pairs={{8,6},{14,16},{16,14},{22,24},{9,7},{15,17},{17,15},{23,25}} | collective-permute-start | bytes 811016 | tf_op jit(solution)/shard_map/ppermute | solution.py:192
  20.6 0.4 collective-permute-start.8
  21.0 4.6 %collective-permute-start.10 = (f32[256,256]{1,0:T(8,128)S(1)}, f32[256,256]{1,0:T(8,128)S(1)}, u32[]{:S(2)}, u32[]{:S(2)}) collective-permute-start(f32[256,256]{1,0:T(8,128)S(1)} %get-tuple-element.37), channel_id=1, source_target_pairs={{0,8},{4,12},{8,16},{10,2},{12,20},{14,6},{16,24},{18,10},{20,28},... | collective-permute-start | bytes 786440 | tf_op jit(solution)/shard_map/ppermute | solution.py:192
  25.6 1.3 %collective-permute-start.11 = (f32[256,256]{1,0:T(8,128)S(1)}, f32[256,256]{1,0:T(8,128)S(1)}, u32[]{:S(2)}, u32[]{:S(2)}) collective-permute-start(f32[256,256]{1,0:T(8,128)S(1)} %get-tuple-element.38), channel_id=1, source_target_pairs={{2,10},{6,14},{8,0},{10,18},{12,4},{14,22},{16,8},{18,26},{20,12},... | collective-permute-start | bytes 786440 | tf_op jit(solution)/shard_map/ppermute | solution.py:192
  26.9 0.7 %shard_map.101 = (f32[2,256,256]{2,1,0:T(8,128)S(1)}, f32[256,64]{1,0:T(8,128)S(1)}) custom-call(f32[264,256]{1,0:T(8,128)S(1)} %get-tuple-element.27.re, f32[264,256]{1,0:T(8,128)S(1)} %get-tuple-element.28.im, f32[1,1,2,256,256]{4,3,2,1,0:T(8,128)S(1)} %collective-permute-done.twin_block, f32[264,256]{1,0:T(8,128)S(1)} %collective-permute-done.1.one, ...), custom_call_target="tpu_custom_call" | custom-call | tf_op jit(solution)/shard_map/pallas_call | solution.py:457
  27.6 2.9 %collective-permute-done.8.from_x = f32[256,256]{1,0:T(8,128)S(1)} collective-permute-done((f32[256,256]{1,0:T(8,128)S(1)}, f32[256,256]{1,0:T(8,128)S(1)}, u32[]{:S(2)}, u32[]{:S(2)}) %collective-permute-start.8) | collective-permute-done | bytes 262176 | tf_op jit(solution)/shard_map/ppermute | solution.py:192
  30.6 3.4 %collective-permute-done.11.from_2 = f32[256,256]{1,0:T(8,128)S(1)} collective-permute-done((f32[256,256]{1,0:T(8,128)S(1)}, f32[256,256]{1,0:T(8,128)S(1)}, u32[]{:S(2)}, u32[]{:S(2)}) %collective-permute-start.11) | collective-permute-done | bytes 262176 | tf_op jit(solution)/shard_map/ppermute | solution.py:192
  34.0 3.0 %shard_map.104 = (f32[64,128]{1,0:T(8,128)S(1)}, f32[2,256,256]{2,1,0:T(8,128)S(1)}) custom-call(f32[2,256,256]{2,1,0:T(8,128)S(1)} %get-tuple-element.31.own, f32[264,256]{1,0:T(8,128)S(1)} %get-tuple-element.27.re, f32[256,256]{1,0:T(8,128)S(1)} %copy-done, f32[256,256]{1,0:T(8,128)S(1)} %collective-permute-done.8.from_x, ...), custom_call_target="tpu_custom_call" | custom-call | tf_op jit(solution)/shard_map/pallas_call | solution.py:457
  37.0 4.2 %shard_map.105 = (f32[2,256,256]{2,1,0:T(8,128)S(1)}, f32[512,64]{1,0:T(8,128)S(1)}, f32[64,512]{1,0:T(8,128)S(1)}) custom-call(f32[2,256,256]{2,1,0:T(8,128)S(1)} %get-tuple-element.39.base, s32[1,64]{1,0:T(1,128)S(1)} %copy-done.3), custom_call_target="tpu_custom_call" | custom-call | tf_op jit(solution)/shard_map/pallas_call | solution.py:457
  41.3 3.0 %collective-permute-start.13 = (f32[64,128]{1,0:T(8,128)S(1)}, f32[64,128]{1,0:T(8,128)S(1)}, u32[]{:S(2)}, u32[]{:S(2)}) collective-permute-start(f32[64,128]{1,0:T(8,128)S(1)} %get-tuple-element.46), channel_id=1, source_target_pairs={{0,1},{1,0},{2,3},{3,2},{4,5},{5,4},{6,7},{7,6},{8,9},{9,8},{10,11... | collective-permute-start | bytes 98312 | tf_op jit(solution)/shard_map/ppermute | solution.py:503
  44.3 1.9 %collective-permute-done.13.message = f32[64,128]{1,0:T(8,128)S(1)} collective-permute-done((f32[64,128]{1,0:T(8,128)S(1)}, f32[64,128]{1,0:T(8,128)S(1)}, u32[]{:S(2)}, u32[]{:S(2)}) %collective-permute-start.13) | collective-permute-done | bytes 32800 | tf_op jit(solution)/shard_map/ppermute | solution.py:503
  46.2 1.3 %shard_map.108 = f32[1,1,2,256,256]{4,3,2,1,0:T(8,128)} custom-call(f32[2,256,256]{2,1,0:T(8,128)S(1)} %get-tuple-element.41.g, f32[512,64]{1,0:T(8,128)S(1)} %get-tuple-element.42.cols, f32[64,512]{1,0:T(8,128)S(1)} %get-tuple-element.43.rows, f32[64,128]{1,0:T(8,128)S(1)} %collective-permute-done.13.message, ...), custom_call_target="tpu_custom_call", output_to_operand_aliasing={{}: (4, {})} | custom-call | tf_op jit(solution)/shard_map/pallas_call | solution.py:444
  (31 shorter events, 0.5 us)
Async XLA Ops:
  0.0 0.7 %copy-start.5 = (s32[1,2]{1,0:T(1,128)S(1)}, s32[1,2]{1,0:T(1,128)}, u32[]{:S(2)}) copy-start(s32[1,2]{1,0:T(1,128)} %index_hbm.1) | copy-start | bytes 28
  0.0 0.7 %copy-start.4 = (s32[1,2]{1,0:T(1,128)S(1)}, s32[1,2]{1,0:T(1,128)}, u32[]{:S(2)}) copy-start(s32[1,2]{1,0:T(1,128)} %source_hbm.1) | copy-start | bytes 28
  0.0 0.7 %copy-start.6 = (f32[8]{0:T(128)S(1)}, f32[8]{0:T(128)}, u32[]{:S(2)}) copy-start(f32[8]{0:T(128)} %table_hbm.1) | copy-start | bytes 100
  0.0 11.4 %copy-start.8 = (f32[1,1,2,256,256]{4,3,2,1,0:T(8,128)S(1)}, f32[1,1,2,256,256]{4,3,2,1,0:T(8,128)}, u32[]{:S(2)}) copy-start(f32[1,1,2,256,256]{4,3,2,1,0:T(8,128)} %green.1) | copy-start | bytes 1572868
  1.8 10.9 %collective-permute-start.6 = (f32[264,256]{1,0:T(8,128)S(1)}, f32[264,256]{1,0:T(8,128)S(1)}, u32[]{:S(2)}, u32[]{:S(2)}) collective-permute-start(f32[264,256]{1,0:T(8,128)S(1)} %get-tuple-element.28.im), channel_id=1, source_target_pairs={{16,14},{24,22},{6,8},{14,16},{17,15},{25,23},{7,9},{15,17}} | collective-permute-start | bytes 811016 | tf_op jit(solution)/shard_map/ppermute | solution.py:192
  2.5 10.2 %collective-permute-start.5 = (f32[264,256]{1,0:T(8,128)S(1)}, f32[264,256]{1,0:T(8,128)S(1)}, u32[]{:S(2)}, u32[]{:S(2)}) collective-permute-start(f32[264,256]{1,0:T(8,128)S(1)} %get-tuple-element.28.im), channel_id=1, source_target_pairs={{0,4},{2,6},{4,0},{6,2},{8,12},{10,14},{12,8},{14,10},{16,20},{18,... | collective-permute-start | bytes 811016 | tf_op jit(solution)/shard_map/ppermute | solution.py:192
  5.5 8.3 %collective-permute-start.2 = (f32[264,256]{1,0:T(8,128)S(1)}, f32[264,256]{1,0:T(8,128)S(1)}, u32[]{:S(2)}, u32[]{:S(2)}) collective-permute-start(f32[264,256]{1,0:T(8,128)S(1)} %get-tuple-element.27.re), channel_id=1, source_target_pairs={{2,10},{6,14},{8,0},{10,18},{12,4},{14,22},{16,8},{18,26},{20,12},... | collective-permute-start | bytes 811016 | tf_op jit(solution)/shard_map/ppermute | solution.py:192
  6.8 10.7 %collective-permute-start.1 = (f32[264,256]{1,0:T(8,128)S(1)}, f32[264,256]{1,0:T(8,128)S(1)}, u32[]{:S(2)}, u32[]{:S(2)}) collective-permute-start(f32[264,256]{1,0:T(8,128)S(1)} %get-tuple-element.27.re), channel_id=1, source_target_pairs={{0,8},{4,12},{8,16},{10,2},{12,20},{14,6},{16,24},{18,10},{20,28},... | collective-permute-start | bytes 811016 | tf_op jit(solution)/shard_map/ppermute | solution.py:192
  11.4 7.2 %collective-permute-start = (f32[1,1,2,256,256]{4,3,2,1,0:T(8,128)S(1)}, f32[1,1,2,256,256]{4,3,2,1,0:T(8,128)S(1)}, u32[]{:S(2)}, u32[]{:S(2)}) collective-permute-start(f32[1,1,2,256,256]{4,3,2,1,0:T(8,128)S(1)} %copy-done.8), channel_id=1, source_target_pairs={{0,2},{2,0},{4,6},{6,4},{8,10},{10,8},{12,14},{14,12},{16,18},{18,... | collective-permute-start | bytes 1572872 | tf_op jit(solution)/shard_map/ppermute | solution.py:192
  12.7 5.8 %collective-permute-start.7 = (f32[264,256]{1,0:T(8,128)S(1)}, f32[264,256]{1,0:T(8,128)S(1)}, u32[]{:S(2)}, u32[]{:S(2)}) collective-permute-start(f32[264,256]{1,0:T(8,128)S(1)} %collective-permute-done.5.x), channel_id=1, source_target_pairs={{0,2},{2,0},{4,6},{6,4},{8,10},{10,8},{12,14},{14,12},{16,18},{18,... | collective-permute-start | bytes 811016 | tf_op jit(solution)/shard_map/ppermute | solution.py:192
  13.9 5.0 %collective-permute-start.4 = (f32[264,256]{1,0:T(8,128)S(1)}, f32[264,256]{1,0:T(8,128)S(1)}, u32[]{:S(2)}, u32[]{:S(2)}) collective-permute-start(f32[264,256]{1,0:T(8,128)S(1)} %collective-permute-done.2.two), channel_id=1, source_target_pairs={{0,2},{2,0},{4,6},{6,4},{8,10},{10,8},{12,14},{14,12},{16,18},{18,... | collective-permute-start | bytes 811016 | tf_op jit(solution)/shard_map/ppermute | solution.py:192
  17.5 2.2 %collective-permute-start.3 = (f32[264,256]{1,0:T(8,128)S(1)}, f32[264,256]{1,0:T(8,128)S(1)}, u32[]{:S(2)}, u32[]{:S(2)}) collective-permute-start(f32[264,256]{1,0:T(8,128)S(1)} %collective-permute-done.1.one), channel_id=1, source_target_pairs={{0,2},{2,0},{4,6},{6,4},{8,10},{10,8},{12,14},{14,12},{16,18},{18,... | collective-permute-start | bytes 811016 | tf_op jit(solution)/shard_map/ppermute | solution.py:192
  18.8 8.1 %copy-start = (f32[256,256]{1,0:T(8,128)S(1)}, f32[256,256]{1,0:T(8,128)}, u32[]{:S(2)}) copy-start(f32[256,256]{1,0:T(8,128)} %profile.3) | copy-start | bytes 786436
  18.8 8.1 %copy-start.1 = (f32[1,256,256]{2,1,0:T(8,128)S(1)}, f32[1,256,256]{2,1,0:T(8,128)}, u32[]{:S(2)}) copy-start(f32[1,256,256]{2,1,0:T(8,128)} %ham.1) | copy-start | bytes 786436
  18.9 8.1 %copy-start.2 = (f32[1,64,64]{2,1,0:T(8,128)S(1)}, f32[1,64,64]{2,1,0:T(8,128)}, u32[]{:S(2)}) copy-start(f32[1,64,64]{2,1,0:T(8,128)} %coup.1) | copy-start | bytes 49156
  19.9 7.0 %copy-start.7 = (s32[1,64]{1,0:T(1,128)S(1)}, s32[1,64]{1,0:T(1,128)}, u32[]{:S(2)}) copy-start(s32[1,64]{1,0:T(1,128)} %left.1) | copy-start | bytes 772
  19.9 14.1 %collective-permute-start.9 = (f32[264,256]{1,0:T(8,128)S(1)}, f32[264,256]{1,0:T(8,128)S(1)}, u32[]{:S(2)}, u32[]{:S(2)}) collective-permute-start(f32[264,256]{1,0:T(8,128)S(1)} %collective-permute-done.2.two), channel_id=1, source_target_pairs={{8,6},{14,16},{16,14},{22,24},{9,7},{15,17},{17,15},{23,25}} | collective-permute-start | bytes 811016 | tf_op jit(solution)/shard_map/ppermute | solution.py:192
  20.6 9.9 %collective-permute-start.8 = (f32[256,256]{1,0:T(8,128)S(1)}, f32[256,256]{1,0:T(8,128)S(1)}, u32[]{:S(2)}, u32[]{:S(2)}) collective-permute-start(f32[256,256]{1,0:T(8,128)S(1)} %shard_map.103), channel_id=1, source_target_pairs={{0,4},{2,6},{4,0},{6,2},{8,12},{10,14},{12,8},{14,10},{16,20},{18,... | collective-permute-start | bytes 786440 | tf_op jit(solution)/shard_map/ppermute | solution.py:192
  21.0 9.6 %collective-permute-start.10 = (f32[256,256]{1,0:T(8,128)S(1)}, f32[256,256]{1,0:T(8,128)S(1)}, u32[]{:S(2)}, u32[]{:S(2)}) collective-permute-start(f32[256,256]{1,0:T(8,128)S(1)} %get-tuple-element.37), channel_id=1, source_target_pairs={{0,8},{4,12},{8,16},{10,2},{12,20},{14,6},{16,24},{18,10},{20,28},... | collective-permute-start | bytes 786440 | tf_op jit(solution)/shard_map/ppermute | solution.py:192
  25.6 8.4 %collective-permute-start.11 = (f32[256,256]{1,0:T(8,128)S(1)}, f32[256,256]{1,0:T(8,128)S(1)}, u32[]{:S(2)}, u32[]{:S(2)}) collective-permute-start(f32[256,256]{1,0:T(8,128)S(1)} %get-tuple-element.38), channel_id=1, source_target_pairs={{2,10},{6,14},{8,0},{10,18},{12,4},{14,22},{16,8},{18,26},{20,12},... | collective-permute-start | bytes 786440 | tf_op jit(solution)/shard_map/ppermute | solution.py:192
  27.6 6.4 %copy-start.3 = (s32[1,64]{1,0:T(1,128)S(1)}, s32[1,64]{1,0:T(1,128)}, u32[]{:S(2)}) copy-start(s32[1,64]{1,0:T(1,128)} %right.3) | copy-start | bytes 772
  37.0 4.3 %collective-permute-start.12 = (f32[64,128]{1,0:T(8,128)S(1)}, f32[64,128]{1,0:T(8,128)S(1)}, u32[]{:S(2)}, u32[]{:S(2)}) collective-permute-start(f32[64,128]{1,0:T(8,128)S(1)} %get-tuple-element.45), channel_id=1, source_target_pairs={{0,1},{1,0},{2,3},{3,2},{4,5},{5,4},{6,7},{7,6},{8,9},{9,8},{10,11... | collective-permute-start | bytes 98312 | tf_op jit(solution)/shard_map/ppermute | solution.py:503
  41.3 4.9 %collective-permute-start.13 = (f32[64,128]{1,0:T(8,128)S(1)}, f32[64,128]{1,0:T(8,128)S(1)}, u32[]{:S(2)}, u32[]{:S(2)}) collective-permute-start(f32[64,128]{1,0:T(8,128)S(1)} %get-tuple-element.46), channel_id=1, source_target_pairs={{0,1},{1,0},{2,3},{3,2},{4,5},{5,4},{6,7},{7,6},{8,9},{9,8},{10,11... | collective-permute-start | bytes 98312 | tf_op jit(solution)/shard_map/ppermute | solution.py:503

commit v7 on v6

--- a/solution.py
+++ b/solution.py
@@ -428,12 +428,17 @@
     def _():
         width, faces = g.shape[1], message.shape[0]
         t_re, t_im = complex_mm(message[:, :faces], message[:, faces:], rows[:, :width], rows[:, width:])
-        c_re, c_im = complex_mm(cols[:width], cols[width:], t_re, t_im)
+        half = width // 2
         copies = []
-        for k, change in enumerate((c_re, c_im)):
-            block[k] = g[k] + change
-            copies.append(pltpu.make_async_copy(block.at[k], green_out.at[0, 0, k], sems.at[k]))
-            copies[k].start()
+        for at in (0, half):
+            rows_at = pl.ds(at, half)
+            changes = complex_mm(cols[at:at + half], cols[width + at:width + at + half], t_re, t_im)
+            for k, change in enumerate(changes):
+                block[k, rows_at] = g[k, rows_at] + change
+                copies.append(pltpu.make_async_copy(
+                    block.at[k, rows_at], green_out.at[0, 0, k, rows_at], sems.at[len(copies)]
+                ))
+                copies[-1].start()
         for copy in copies:
             copy.wait()
 
@@ -446,7 +451,7 @@
         out_shape=jax.ShapeDtypeStruct(shape, f32),
         in_specs=[vmem] * len(arrays) + [hbm] * len(more),
         out_specs=hbm,
-        scratch_shapes=[pltpu.VMEM(shape[2:], f32), pltpu.SemaphoreType.DMA((2,))],
+        scratch_shapes=[pltpu.VMEM(shape[2:], f32), pltpu.SemaphoreType.DMA((4,))],
         input_output_aliases={len(arrays): 0} if more else {},
         compiler_params=pltpu.CompilerParams(vmem_limit_bytes=40 * 2**20),
     )(*arrays, *more)

time: 47.9 us -> 47.9 us (level)
  no operation moved by 1% of the time
where the time goes in v7:
time: 47.9 us; the launch traced here: 47.7 us
  starting transfers between devices  25.3 us (53%)
  Pallas kernels  10.7 us (22%)
  waiting for transfers between devices  10.5 us (22%)
  between operations  1.1 us (2%)
    ppermute x12, starting transfers between devices, sent(): return lax.ppermute(value, 'energy', pairs)  22.2 us
    ppermute x12, waiting for transfers between devices, sent(): return lax.ppermute(value, 'energy', pairs)  8.69 us
    pallas_call x6, Pallas kernels, call(): pl.pallas_call(kernel, out_shape=[jax.ShapeDtypeStruct(shape, f32) for sh...  8.27 us
    ppermute x2, starting transfers between devices, passed_along(): lax.ppermute(value, 'slab', [(start, (start + steps) % count) for start i...  3.08 us
    ppermute x2, waiting for transfers between devices, passed_along(): lax.ppermute(value, 'slab', [(start, (start + steps) % count) for start i...  1.85 us
    pallas_call x2, Pallas kernels, write_green(): pl.pallas_call(kernel, out_shape=jax.ShapeDtypeStruct(shape, f32), in_spe...  1.34 us
    pallas_call x1, Pallas kernels, pack(): pl.pallas_call(pack_kernel, out_shape=[jax.ShapeDtypeStruct((width + ROWS...  1.09 us
  transfers between devices with their start and end apart: 14, of which 6 were waited for; matrix products, arithmetic and copies ran while one was open for 0% of the time, Pallas kernels for 11%

profile of v7, /device:TPU:0, one launch (start us, length us, event | category | flops | bytes accessed | tf_op | source)
XLA Modules:
  0.0 47.7 jit_solution(2501094837860974693)
XLA Ops:
  0.7 1.1 %shard_map.100 = (f32[264,256]{1,0:T(8,128)S(1)}, f32[264,256]{1,0:T(8,128)S(1)}) custom-call(f32[1]{0:T(128)S(6)} %copy.13.energy_hbm, s32[1,2]{1,0:T(1,128)S(1)} %copy-done.4, s32[1,2]{1,0:T(1,128)S(1)} %copy-done.5, f32[8]{0:T(128)S(1)} %copy-done.6, f32[1,1,2,256,256]{4,3,2,1,0:T(8,128)} %green.1), custom_call_target="tpu_custom_call" | custom-call | tf_op jit(solution)/shard_map/pallas_call | solution.py:226
  1.8 0.7 %collective-permute-start.6 = (f32[264,256]{1,0:T(8,128)S(1)}, f32[264,256]{1,0:T(8,128)S(1)}, u32[]{:S(2)}, u32[]{:S(2)}) collective-permute-start(f32[264,256]{1,0:T(8,128)S(1)} %get-tuple-element.28.im), channel_id=1, source_target_pairs={{16,14},{24,22},{6,8},{14,16},{17,15},{25,23},{7,9},{15,17}} | collective-permute-start | bytes 811016 | tf_op jit(solution)/shard_map/ppermute | solution.py:192
  2.5 3.0 %collective-permute-start.5 = (f32[264,256]{1,0:T(8,128)S(1)}, f32[264,256]{1,0:T(8,128)S(1)}, u32[]{:S(2)}, u32[]{:S(2)}) collective-permute-start(f32[264,256]{1,0:T(8,128)S(1)} %get-tuple-element.28.im), channel_id=1, source_target_pairs={{0,4},{2,6},{4,0},{6,2},{8,12},{10,14},{12,8},{14,10},{16,20},{18,... | collective-permute-start | bytes 811016 | tf_op jit(solution)/shard_map/ppermute | solution.py:192
  5.5 1.3 %collective-permute-start.2 = (f32[264,256]{1,0:T(8,128)S(1)}, f32[264,256]{1,0:T(8,128)S(1)}, u32[]{:S(2)}, u32[]{:S(2)}) collective-permute-start(f32[264,256]{1,0:T(8,128)S(1)} %get-tuple-element.27.re), channel_id=1, source_target_pairs={{2,10},{6,14},{8,0},{10,18},{12,4},{14,22},{16,8},{18,26},{20,12},... | collective-permute-start | bytes 811016 | tf_op jit(solution)/shard_map/ppermute | solution.py:192
  6.8 4.6 %collective-permute-start.1 = (f32[264,256]{1,0:T(8,128)S(1)}, f32[264,256]{1,0:T(8,128)S(1)}, u32[]{:S(2)}, u32[]{:S(2)}) collective-permute-start(f32[264,256]{1,0:T(8,128)S(1)} %get-tuple-element.27.re), channel_id=1, source_target_pairs={{0,8},{4,12},{8,16},{10,2},{12,20},{14,6},{16,24},{18,10},{20,28},... | collective-permute-start | bytes 811016 | tf_op jit(solution)/shard_map/ppermute | solution.py:192
  11.4 1.3 %collective-permute-start = (f32[1,1,2,256,256]{4,3,2,1,0:T(8,128)S(1)}, f32[1,1,2,256,256]{4,3,2,1,0:T(8,128)S(1)}, u32[]{:S(2)}, u32[]{:S(2)}) collective-permute-start(f32[1,1,2,256,256]{4,3,2,1,0:T(8,128)S(1)} %copy-done.8), channel_id=1, source_target_pairs={{0,2},{2,0},{4,6},{6,4},{8,10},{10,8},{12,14},{14,12},{16,18},{18,... | collective-permute-start | bytes 1572872 | tf_op jit(solution)/shard_map/ppermute | solution.py:192
  13.0 0.9 %collective-permute-done.2.two = f32[264,256]{1,0:T(8,128)S(1)} collective-permute-done((f32[264,256]{1,0:T(8,128)S(1)}, f32[264,256]{1,0:T(8,128)S(1)}, u32[]{:S(2)}, u32[]{:S(2)}) %collective-permute-start.2) | collective-permute-done | bytes 270368 | tf_op jit(solution)/shard_map/ppermute | solution.py:192
  13.9 3.1 %collective-permute-start.4 = (f32[264,256]{1,0:T(8,128)S(1)}, f32[264,256]{1,0:T(8,128)S(1)}, u32[]{:S(2)}, u32[]{:S(2)}) collective-permute-start(f32[264,256]{1,0:T(8,128)S(1)} %collective-permute-done.2.two), channel_id=1, source_target_pairs={{0,2},{2,0},{4,6},{6,4},{8,10},{10,8},{12,14},{14,12},{16,18},{18,... | collective-permute-start | bytes 811016 | tf_op jit(solution)/shard_map/ppermute | solution.py:192
  17.0 0.6 %collective-permute-done.1.one = f32[264,256]{1,0:T(8,128)S(1)} collective-permute-done((f32[264,256]{1,0:T(8,128)S(1)}, f32[264,256]{1,0:T(8,128)S(1)}, u32[]{:S(2)}, u32[]{:S(2)}) %collective-permute-start.1) | collective-permute-done | bytes 270368 | tf_op jit(solution)/shard_map/ppermute | solution.py:192
  17.5 1.1 %collective-permute-start.3 = (f32[264,256]{1,0:T(8,128)S(1)}, f32[264,256]{1,0:T(8,128)S(1)}, u32[]{:S(2)}, u32[]{:S(2)}) collective-permute-start(f32[264,256]{1,0:T(8,128)S(1)} %collective-permute-done.1.one), channel_id=1, source_target_pairs={{0,2},{2,0},{4,6},{6,4},{8,10},{10,8},{12,14},{14,12},{16,18},{18,... | collective-permute-start | bytes 811016 | tf_op jit(solution)/shard_map/ppermute | solution.py:192
  18.6 0.2 shard_map.102
  18.9 0.9 %collective-permute-done.3.pair_one = f32[264,256]{1,0:T(8,128)S(1)} collective-permute-done((f32[264,256]{1,0:T(8,128)S(1)}, f32[264,256]{1,0:T(8,128)S(1)}, u32[]{:S(2)}, u32[]{:S(2)}) %collective-permute-start.3) | collective-permute-done | bytes 270368 | tf_op jit(solution)/shard_map/ppermute | solution.py:192
  19.9 0.7 %collective-permute-start.9 = (f32[264,256]{1,0:T(8,128)S(1)}, f32[264,256]{1,0:T(8,128)S(1)}, u32[]{:S(2)}, u32[]{:S(2)}) collective-permute-start(f32[264,256]{1,0:T(8,128)S(1)} %collective-permute-done.2.two), channel_id=1, source_target_pairs={{8,6},{14,16},{16,14},{22,24},{9,7},{15,17},{17,15},{23,25}} | collective-permute-start | bytes 811016 | tf_op jit(solution)/shard_map/ppermute | solution.py:192
  20.6 0.4 collective-permute-start.8
  21.0 4.6 %collective-permute-start.10 = (f32[256,256]{1,0:T(8,128)S(1)}, f32[256,256]{1,0:T(8,128)S(1)}, u32[]{:S(2)}, u32[]{:S(2)}) collective-permute-start(f32[256,256]{1,0:T(8,128)S(1)} %get-tuple-element.37), channel_id=1, source_target_pairs={{0,8},{4,12},{8,16},{10,2},{12,20},{14,6},{16,24},{18,10},{20,28},... | collective-permute-start | bytes 786440 | tf_op jit(solution)/shard_map/ppermute | solution.py:192
  25.6 1.3 %collective-permute-start.11 = (f32[256,256]{1,0:T(8,128)S(1)}, f32[256,256]{1,0:T(8,128)S(1)}, u32[]{:S(2)}, u32[]{:S(2)}) collective-permute-start(f32[256,256]{1,0:T(8,128)S(1)} %get-tuple-element.38), channel_id=1, source_target_pairs={{2,10},{6,14},{8,0},{10,18},{12,4},{14,22},{16,8},{18,26},{20,12},... | collective-permute-start | bytes 786440 | tf_op jit(solution)/shard_map/ppermute | solution.py:192
  26.9 0.7 %shard_map.101 = (f32[2,256,256]{2,1,0:T(8,128)S(1)}, f32[256,64]{1,0:T(8,128)S(1)}) custom-call(f32[264,256]{1,0:T(8,128)S(1)} %get-tuple-element.27.re, f32[264,256]{1,0:T(8,128)S(1)} %get-tuple-element.28.im, f32[1,1,2,256,256]{4,3,2,1,0:T(8,128)S(1)} %collective-permute-done.twin_block, f32[264,256]{1,0:T(8,128)S(1)} %collective-permute-done.1.one, ...), custom_call_target="tpu_custom_call" | custom-call | tf_op jit(solution)/shard_map/pallas_call | solution.py:462
  27.6 2.9 %collective-permute-done.8.from_x = f32[256,256]{1,0:T(8,128)S(1)} collective-permute-done((f32[256,256]{1,0:T(8,128)S(1)}, f32[256,256]{1,0:T(8,128)S(1)}, u32[]{:S(2)}, u32[]{:S(2)}) %collective-permute-start.8) | collective-permute-done | bytes 262176 | tf_op jit(solution)/shard_map/ppermute | solution.py:192
  30.6 3.4 %collective-permute-done.11.from_2 = f32[256,256]{1,0:T(8,128)S(1)} collective-permute-done((f32[256,256]{1,0:T(8,128)S(1)}, f32[256,256]{1,0:T(8,128)S(1)}, u32[]{:S(2)}, u32[]{:S(2)}) %collective-permute-start.11) | collective-permute-done | bytes 262176 | tf_op jit(solution)/shard_map/ppermute | solution.py:192
  34.0 3.0 %shard_map.104 = (f32[64,128]{1,0:T(8,128)S(1)}, f32[2,256,256]{2,1,0:T(8,128)S(1)}) custom-call(f32[2,256,256]{2,1,0:T(8,128)S(1)} %get-tuple-element.31.own, f32[264,256]{1,0:T(8,128)S(1)} %get-tuple-element.27.re, f32[256,256]{1,0:T(8,128)S(1)} %copy-done, f32[256,256]{1,0:T(8,128)S(1)} %collective-permute-done.8.from_x, ...), custom_call_target="tpu_custom_call" | custom-call | tf_op jit(solution)/shard_map/pallas_call | solution.py:462
  37.0 4.2 %shard_map.105 = (f32[2,256,256]{2,1,0:T(8,128)S(1)}, f32[512,64]{1,0:T(8,128)S(1)}, f32[64,512]{1,0:T(8,128)S(1)}) custom-call(f32[2,256,256]{2,1,0:T(8,128)S(1)} %get-tuple-element.39.base, s32[1,64]{1,0:T(1,128)S(1)} %copy-done.3), custom_call_target="tpu_custom_call" | custom-call | tf_op jit(solution)/shard_map/pallas_call | solution.py:462
  41.3 3.0 %collective-permute-start.13 = (f32[64,128]{1,0:T(8,128)S(1)}, f32[64,128]{1,0:T(8,128)S(1)}, u32[]{:S(2)}, u32[]{:S(2)}) collective-permute-start(f32[64,128]{1,0:T(8,128)S(1)} %get-tuple-element.46), channel_id=1, source_target_pairs={{0,1},{1,0},{2,3},{3,2},{4,5},{5,4},{6,7},{7,6},{8,9},{9,8},{10,11... | collective-permute-start | bytes 98312 | tf_op jit(solution)/shard_map/ppermute | solution.py:508
  44.3 1.9 %collective-permute-done.13.message = f32[64,128]{1,0:T(8,128)S(1)} collective-permute-done((f32[64,128]{1,0:T(8,128)S(1)}, f32[64,128]{1,0:T(8,128)S(1)}, u32[]{:S(2)}, u32[]{:S(2)}) %collective-permute-start.13) | collective-permute-done | bytes 32800 | tf_op jit(solution)/shard_map/ppermute | solution.py:508
  46.2 1.3 %shard_map.108 = f32[1,1,2,256,256]{4,3,2,1,0:T(8,128)} custom-call(f32[2,256,256]{2,1,0:T(8,128)S(1)} %get-tuple-element.41.g, f32[512,64]{1,0:T(8,128)S(1)} %get-tuple-element.42.cols, f32[64,512]{1,0:T(8,128)S(1)} %get-tuple-element.43.rows, f32[64,128]{1,0:T(8,128)S(1)} %collective-permute-done.13.message, ...), custom_call_target="tpu_custom_call", output_to_operand_aliasing={{}: (4, {})} | custom-call | tf_op jit(solution)/shard_map/pallas_call | solution.py:449
  (31 shorter events, 0.6 us)
Async XLA Ops:
  0.0 0.7 %copy-start.5 = (s32[1,2]{1,0:T(1,128)S(1)}, s32[1,2]{1,0:T(1,128)}, u32[]{:S(2)}) copy-start(s32[1,2]{1,0:T(1,128)} %index_hbm.1) | copy-start | bytes 28
  0.0 0.7 %copy-start.4 = (s32[1,2]{1,0:T(1,128)S(1)}, s32[1,2]{1,0:T(1,128)}, u32[]{:S(2)}) copy-start(s32[1,2]{1,0:T(1,128)} %source_hbm.1) | copy-start | bytes 28
  0.0 0.7 %copy-start.6 = (f32[8]{0:T(128)S(1)}, f32[8]{0:T(128)}, u32[]{:S(2)}) copy-start(f32[8]{0:T(128)} %table_hbm.1) | copy-start | bytes 100
  0.0 11.4 %copy-start.8 = (f32[1,1,2,256,256]{4,3,2,1,0:T(8,128)S(1)}, f32[1,1,2,256,256]{4,3,2,1,0:T(8,128)}, u32[]{:S(2)}) copy-start(f32[1,1,2,256,256]{4,3,2,1,0:T(8,128)} %green.1) | copy-start | bytes 1572868
  1.8 10.9 %collective-permute-start.6 = (f32[264,256]{1,0:T(8,128)S(1)}, f32[264,256]{1,0:T(8,128)S(1)}, u32[]{:S(2)}, u32[]{:S(2)}) collective-permute-start(f32[264,256]{1,0:T(8,128)S(1)} %get-tuple-element.28.im), channel_id=1, source_target_pairs={{16,14},{24,22},{6,8},{14,16},{17,15},{25,23},{7,9},{15,17}} | collective-permute-start | bytes 811016 | tf_op jit(solution)/shard_map/ppermute | solution.py:192
  2.5 10.2 %collective-permute-start.5 = (f32[264,256]{1,0:T(8,128)S(1)}, f32[264,256]{1,0:T(8,128)S(1)}, u32[]{:S(2)}, u32[]{:S(2)}) collective-permute-start(f32[264,256]{1,0:T(8,128)S(1)} %get-tuple-element.28.im), channel_id=1, source_target_pairs={{0,4},{2,6},{4,0},{6,2},{8,12},{10,14},{12,8},{14,10},{16,20},{18,... | collective-permute-start | bytes 811016 | tf_op jit(solution)/shard_map/ppermute | solution.py:192
  5.5 8.3 %collective-permute-start.2 = (f32[264,256]{1,0:T(8,128)S(1)}, f32[264,256]{1,0:T(8,128)S(1)}, u32[]{:S(2)}, u32[]{:S(2)}) collective-permute-start(f32[264,256]{1,0:T(8,128)S(1)} %get-tuple-element.27.re), channel_id=1, source_target_pairs={{2,10},{6,14},{8,0},{10,18},{12,4},{14,22},{16,8},{18,26},{20,12},... | collective-permute-start | bytes 811016 | tf_op jit(solution)/shard_map/ppermute | solution.py:192
  6.8 10.7 %collective-permute-start.1 = (f32[264,256]{1,0:T(8,128)S(1)}, f32[264,256]{1,0:T(8,128)S(1)}, u32[]{:S(2)}, u32[]{:S(2)}) collective-permute-start(f32[264,256]{1,0:T(8,128)S(1)} %get-tuple-element.27.re), channel_id=1, source_target_pairs={{0,8},{4,12},{8,16},{10,2},{12,20},{14,6},{16,24},{18,10},{20,28},... | collective-permute-start | bytes 811016 | tf_op jit(solution)/shard_map/ppermute | solution.py:192
  11.4 7.2 %collective-permute-start = (f32[1,1,2,256,256]{4,3,2,1,0:T(8,128)S(1)}, f32[1,1,2,256,256]{4,3,2,1,0:T(8,128)S(1)}, u32[]{:S(2)}, u32[]{:S(2)}) collective-permute-start(f32[1,1,2,256,256]{4,3,2,1,0:T(8,128)S(1)} %copy-done.8), channel_id=1, source_target_pairs={{0,2},{2,0},{4,6},{6,4},{8,10},{10,8},{12,14},{14,12},{16,18},{18,... | collective-permute-start | bytes 1572872 | tf_op jit(solution)/shard_map/ppermute | solution.py:192
  12.7 5.8 %collective-permute-start.7 = (f32[264,256]{1,0:T(8,128)S(1)}, f32[264,256]{1,0:T(8,128)S(1)}, u32[]{:S(2)}, u32[]{:S(2)}) collective-permute-start(f32[264,256]{1,0:T(8,128)S(1)} %collective-permute-done.5.x), channel_id=1, source_target_pairs={{0,2},{2,0},{4,6},{6,4},{8,10},{10,8},{12,14},{14,12},{16,18},{18,... | collective-permute-start | bytes 811016 | tf_op jit(solution)/shard_map/ppermute | solution.py:192
  13.9 5.0 %collective-permute-start.4 = (f32[264,256]{1,0:T(8,128)S(1)}, f32[264,256]{1,0:T(8,128)S(1)}, u32[]{:S(2)}, u32[]{:S(2)}) collective-permute-start(f32[264,256]{1,0:T(8,128)S(1)} %collective-permute-done.2.two), channel_id=1, source_target_pairs={{0,2},{2,0},{4,6},{6,4},{8,10},{10,8},{12,14},{14,12},{16,18},{18,... | collective-permute-start | bytes 811016 | tf_op jit(solution)/shard_map/ppermute | solution.py:192
  17.5 2.2 %collective-permute-start.3 = (f32[264,256]{1,0:T(8,128)S(1)}, f32[264,256]{1,0:T(8,128)S(1)}, u32[]{:S(2)}, u32[]{:S(2)}) collective-permute-start(f32[264,256]{1,0:T(8,128)S(1)} %collective-permute-done.1.one), channel_id=1, source_target_pairs={{0,2},{2,0},{4,6},{6,4},{8,10},{10,8},{12,14},{14,12},{16,18},{18,... | collective-permute-start | bytes 811016 | tf_op jit(solution)/shard_map/ppermute | solution.py:192
  18.8 8.1 %copy-start = (f32[256,256]{1,0:T(8,128)S(1)}, f32[256,256]{1,0:T(8,128)}, u32[]{:S(2)}) copy-start(f32[256,256]{1,0:T(8,128)} %profile.3) | copy-start | bytes 786436
  18.8 8.1 %copy-start.1 = (f32[1,256,256]{2,1,0:T(8,128)S(1)}, f32[1,256,256]{2,1,0:T(8,128)}, u32[]{:S(2)}) copy-start(f32[1,256,256]{2,1,0:T(8,128)} %ham.1) | copy-start | bytes 786436
  18.9 8.1 %copy-start.2 = (f32[1,64,64]{2,1,0:T(8,128)S(1)}, f32[1,64,64]{2,1,0:T(8,128)}, u32[]{:S(2)}) copy-start(f32[1,64,64]{2,1,0:T(8,128)} %coup.1) | copy-start | bytes 49156
  19.9 7.0 %copy-start.7 = (s32[1,64]{1,0:T(1,128)S(1)}, s32[1,64]{1,0:T(1,128)}, u32[]{:S(2)}) copy-start(s32[1,64]{1,0:T(1,128)} %left.1) | copy-start | bytes 772
  19.9 14.1 %collective-permute-start.9 = (f32[264,256]{1,0:T(8,128)S(1)}, f32[264,256]{1,0:T(8,128)S(1)}, u32[]{:S(2)}, u32[]{:S(2)}) collective-permute-start(f32[264,256]{1,0:T(8,128)S(1)} %collective-permute-done.2.two), channel_id=1, source_target_pairs={{8,6},{14,16},{16,14},{22,24},{9,7},{15,17},{17,15},{23,25}} | collective-permute-start | bytes 811016 | tf_op jit(solution)/shard_map/ppermute | solution.py:192
  20.6 9.9 %collective-permute-start.8 = (f32[256,256]{1,0:T(8,128)S(1)}, f32[256,256]{1,0:T(8,128)S(1)}, u32[]{:S(2)}, u32[]{:S(2)}) collective-permute-start(f32[256,256]{1,0:T(8,128)S(1)} %shard_map.103), channel_id=1, source_target_pairs={{0,4},{2,6},{4,0},{6,2},{8,12},{10,14},{12,8},{14,10},{16,20},{18,... | collective-permute-start | bytes 786440 | tf_op jit(solution)/shard_map/ppermute | solution.py:192
  21.0 9.6 %collective-permute-start.10 = (f32[256,256]{1,0:T(8,128)S(1)}, f32[256,256]{1,0:T(8,128)S(1)}, u32[]{:S(2)}, u32[]{:S(2)}) collective-permute-start(f32[256,256]{1,0:T(8,128)S(1)} %get-tuple-element.37), channel_id=1, source_target_pairs={{0,8},{4,12},{8,16},{10,2},{12,20},{14,6},{16,24},{18,10},{20,28},... | collective-permute-start | bytes 786440 | tf_op jit(solution)/shard_map/ppermute | solution.py:192
  25.6 8.4 %collective-permute-start.11 = (f32[256,256]{1,0:T(8,128)S(1)}, f32[256,256]{1,0:T(8,128)S(1)}, u32[]{:S(2)}, u32[]{:S(2)}) collective-permute-start(f32[256,256]{1,0:T(8,128)S(1)} %get-tuple-element.38), channel_id=1, source_target_pairs={{2,10},{6,14},{8,0},{10,18},{12,4},{14,22},{16,8},{18,26},{20,12},... | collective-permute-start | bytes 786440 | tf_op jit(solution)/shard_map/ppermute | solution.py:192
  27.6 6.4 %copy-start.3 = (s32[1,64]{1,0:T(1,128)S(1)}, s32[1,64]{1,0:T(1,128)}, u32[]{:S(2)}) copy-start(s32[1,64]{1,0:T(1,128)} %right.3) | copy-start | bytes 772
  37.0 4.3 %collective-permute-start.12 = (f32[64,128]{1,0:T(8,128)S(1)}, f32[64,128]{1,0:T(8,128)S(1)}, u32[]{:S(2)}, u32[]{:S(2)}) collective-permute-start(f32[64,128]{1,0:T(8,128)S(1)} %get-tuple-element.45), channel_id=1, source_target_pairs={{0,1},{1,0},{2,3},{3,2},{4,5},{5,4},{6,7},{7,6},{8,9},{9,8},{10,11... | collective-permute-start | bytes 98312 | tf_op jit(solution)/shard_map/ppermute | solution.py:508
  41.3 4.9 %collective-permute-start.13 = (f32[64,128]{1,0:T(8,128)S(1)}, f32[64,128]{1,0:T(8,128)S(1)}, u32[]{:S(2)}, u32[]{:S(2)}) collective-permute-start(f32[64,128]{1,0:T(8,128)S(1)} %get-tuple-element.46), channel_id=1, source_target_pairs={{0,1},{1,0},{2,3},{3,2},{4,5},{5,4},{6,7},{7,6},{8,9},{9,8},{10,11... | collective-permute-start | bytes 98312 | tf_op jit(solution)/shard_map/ppermute | solution.py:508
